TPU v7x, 128 devices: a whole 4x4x4 slice. The times are simulated.
128 devices in a mesh: mp: 8 (over z_lo, x), feat: 16 (over y, z_hi, core).
Axes of the slice: x: 4, y: 4, z: 4 (z_hi: 2, z_lo: 2; z = z_hi * 2 + z_lo), core: 2. Of those that a mesh axis runs over, the one named last changes fastest.
Arguments:
- residual_in: bfloat16 [256, 3584], P(None, 'feat'), may hold values from -24 to 24
- norm_gain: float32 [3584], P('feat'), may hold values from 0.5 to 1.5
- gate_weight: bfloat16 [3584, 14336], P('feat', 'mp'), may hold values from -0.09375 to 0.09375
- up_weight: bfloat16 [3584, 14336], P('feat', 'mp'), may hold values from -0.09375 to 0.09375
- down_weight: bfloat16 [14336, 3584], P('mp', 'feat'), may hold values from -0.046875 to 0.046875
- encoder_weight: bfloat16 [3584, 65536], P(None, ('mp', 'feat')), may hold values from -0.375 to 0.375
- encoder_bias: float32 [65536], P(('mp', 'feat')), may hold values from -1.5 to 0.5
- decoder_weight: bfloat16 [65536, 3584], P(('mp', 'feat')), may hold values from -0.09375 to 0.09375
- decoder_bias: float32 [3584], replicated, may hold values from -3 to 3
Outputs:
- feature_codes: bfloat16 [256, 65536], P(None, ('mp', 'feat'))
- reconstruction: bfloat16 [256, 3584], P(('mp', 'feat'))
- encoder_gradient: bfloat16 [3584, 65536], P(None, ('mp', 'feat'))
- decoder_gradient: bfloat16 [65536, 3584], P(('mp', 'feat'))
- input_gradient: float32 [256, 3584], P(('mp', 'feat'))
All inputs are finite; a program needn't handle non-finite values.
Results may differ from a plain program's by a relative error of at most 0.023.
Values may be sent and summed in bfloat16 or wider, within the bound.
No kernel may reach another device: no remote copies, remote signals or barrier semaphores. Data moves between devices by JAX's collectives and lax.ppermute only.
A program may use at most 128 MiB of HBM per device.

v0:
```python
import jax
import jax.numpy as jnp
from jax import lax
from jax.sharding import PartitionSpec as P

D = 3584


sparsity_weight = 0.2
norm_eps = 1e-06


def shards(
    residual_in,
    norm_gain,
    gate_weight,
    up_weight,
    down_weight,
    encoder_weight,
    encoder_bias,
    decoder_weight,
    decoder_bias,
):
    rows_all = residual_in.shape[0]
    hidden_local = gate_weight.shape[1]
    rows_own = rows_all // lax.axis_size(("mp", "feat"))
    first_row = lax.axis_index(("mp", "feat")) * rows_own
    source = residual_in.astype(jnp.float32)
    squares = lax.psum(jnp.sum(source * source, axis=1), "feat")
    inverse_scale = lax.rsqrt(squares / D + norm_eps)
    normed = (source * inverse_scale[:, None] * norm_gain[None, :]).astype(jnp.bfloat16)
    joint_weight = jnp.concatenate([gate_weight, up_weight], axis=1)
    row_block = normed
    projected = lax.psum_scatter(
        jnp.dot(row_block, joint_weight, preferred_element_type=jnp.float32).astype(jnp.bfloat16),
        "feat",
        scatter_dimension=0,
        tiled=True,
    ).astype(jnp.float32)
    hidden = (jax.nn.silu(projected[:, :hidden_local]) * projected[:, hidden_local:]).astype(
        jnp.bfloat16
    )
    partial_mixed = jnp.dot(
        lax.all_gather(hidden, "feat", axis=0, tiled=True),
        down_weight,
        preferred_element_type=jnp.float32,
    )
    mixed_terms = lax.psum(partial_mixed.astype(jnp.bfloat16), "mp").astype(jnp.float32)
    stream_cols = (source + mixed_terms).astype(jnp.bfloat16)
    stream = lax.all_gather(stream_cols, "feat", axis=1, tiled=True)
    encoded = (
        jnp.dot(stream, encoder_weight, preferred_element_type=jnp.float32) + encoder_bias[None, :]
    )
    feature_codes = jax.nn.softplus(encoded).astype(jnp.bfloat16)
    partial_recon = jnp.dot(feature_codes, decoder_weight, preferred_element_type=jnp.float32)
    summed = lax.psum(partial_recon, ("mp", "feat"))
    recon_all = summed + decoder_bias[None, :]
    error = (recon_all - stream.astype(jnp.float32)).astype(jnp.bfloat16)
    recon_own = lax.dynamic_slice_in_dim(recon_all, first_row, rows_own, 0)
    error_own = lax.dynamic_slice_in_dim(error, first_row, rows_own, 0)
    decoder_gradient = lax.dot_general(
        feature_codes, error, (((0,), (0,)), ((), ())), preferred_element_type=jnp.float32
    ).astype(jnp.bfloat16)
    code_gradient = lax.dot_general(
        error, decoder_weight, (((1,), (1,)), ((), ())), preferred_element_type=jnp.float32
    )
    encoded_gradient = (jax.nn.sigmoid(encoded) * (code_gradient + sparsity_weight)).astype(
        jnp.bfloat16
    )
    encoder_gradient = lax.dot_general(
        stream, encoded_gradient, (((0,), (0,)), ((), ())), preferred_element_type=jnp.float32
    ).astype(jnp.bfloat16)
    row_block = encoded_gradient
    input_gradient = lax.psum_scatter(
        lax.dot_general(
            row_block, encoder_weight, (((1,), (1,)), ((), ())), preferred_element_type=jnp.float32
        ),
        ("mp", "feat"),
        scatter_dimension=0,
        tiled=True,
    ) - error_own.astype(jnp.float32)
    return (
        feature_codes,
        recon_own.astype(jnp.bfloat16),
        encoder_gradient,
        decoder_gradient,
        input_gradient,
    )


def solution(mesh):
    in_specs = (
        P(None, "feat"),
        P("feat"),
        P("feat", "mp"),
        P("feat", "mp"),
        P("mp", "feat"),
        P(None, ("mp", "feat")),
        P(("mp", "feat")),
        P(("mp", "feat"), None),
        P(),
    )
    out_specs = (
        P(None, ("mp", "feat")),
        P(("mp", "feat"), None),
        P(None, ("mp", "feat")),
        P(("mp", "feat"), None),
        P(("mp", "feat"), None),
    )
    return jax.shard_map(shards, mesh=mesh, in_specs=in_specs, out_specs=out_specs, check_vma=False)
```

profile of v0, /device:TPU:0, one launch (start us, length us, event | category | flops | bytes accessed | tf_op | source)
XLA Modules:
  0.0 596.3 jit_solution(6068600141430006881)
XLA Ops:
  7.2 0.0 copy-start
  7.2 0.0 reduce-scatter.3.cloned.1.call-start
  7.2 1.0 fusion.6
  8.2 39.0 %psum.21 = f32[256]{0:T(256)S(1)} all-reduce(f32[256]{0:T(256)S(1)} %fusion.6), channel_id=1, replica_groups=mesh['mp'=8,'feat'=16] {'feat'}, use_global_device_ids=true, to_apply=%region_1.0 | all-reduce | flops 256 | bytes 2048 | tf_op jit(solution)/shard_map/psum | solution.py:29
  47.2 0.0 copy-start.9
  47.2 3.5 convolution_convert_fusion.2
  50.7 0.0 copy-start.11
  50.7 0.0 reduce-scatter.3.cloned.1.call-update
  50.7 0.0 all-reduce.5.cloned.1.call-start
  50.8 66.8 %reduce-scatter.3.cloned.1.call-done = bf16[16,3584]{1,0:T(8,128)(2,1)} async-done(((bf16[256,3584]{1,0:T(8,128)(2,1)}), bf16[16,3584]{1,0:T(8,128)(2,1)}) %reduce-scatter.3.cloned.1.call-update) | async-done | bytes 114704 | tf_op jit(solution)/shard_map/reduce_scatter | solution.py:34
  117.5 0.9 convert_element_type.51
  118.5 24.2 %all_gather.6 = bf16[256,1792]{1,0:T(8,128)(2,1)S(1)} all-gather(bf16[16,1792]{1,0:T(8,128)(2,1)S(1)} %fusion.11), channel_id=1, replica_groups=mesh['mp'=8,'feat'=16] {'feat'}, dimensions={0}, use_global_device_ids=true | all-gather | bytes 974848 | tf_op jit(solution)/shard_map/all_gather | solution.py:44
  142.7 0.0 copy-done
  142.7 1.1 convolution_convert_fusion.3
  143.8 0.0 all-reduce.5.cloned.1.call-update
  143.9 0.0 all-gather.2.cloned.1.call-start
  143.9 68.6 %all-reduce.5.cloned.1.call-done = bf16[256,224]{0,1:T(8,128)(2,1)} async-done(((bf16[256,224]{0,1:T(8,128)(2,1)}), bf16[256,224]{0,1:T(8,128)(2,1)}) %all-reduce.5.cloned.1.call-update) | async-done | bytes 114704 | tf_op jit(solution)/shard_map/psum | solution.py:48
  212.5 0.0 copy-done.9
  212.5 1.6 fusion.9
  214.1 0.0 all-gather.2.cloned.1.call-update
  214.1 0.0 all-reduce.7.cloned.1.call-start
  214.1 49.9 %all-gather.2.cloned.1.call-done = bf16[256,3584]{0,1:T(8,128)(2,1)} async-done(((bf16[256,224]{0,1:T(8,128)(2,1)}), bf16[256,3584]{0,1:T(8,128)(2,1)}) %all-gather.2.cloned.1.call-update) | async-done | bytes 1835024 | tf_op jit(solution)/shard_map/all_gather | solution.py:50
  264.0 0.0 copy-done.11
  264.0 0.0 copy-start.3
  264.0 4.1 fusion.5
  268.1 0.0 copy-start.6
  268.2 0.7 copy-done.6
  268.9 0.0 copy-done.3
  268.9 3.5 fusion.15
  272.3 0.0 copy-start.1
  272.3 0.0 copy-start.10
  272.3 0.0 all-reduce.7.cloned.1.call-update
  272.3 0.0 all-reduce.9.cloned.1.call-start
  272.4 152.1 %all-reduce.7.cloned.1.call-done = f32[256,3584]{0,1:T(8,128)} async-done(((f32[256,3584]{0,1:T(8,128)}), f32[256,3584]{0,1:T(8,128)}) %all-reduce.7.cloned.1.call-update) | async-done | bytes 3670032 | tf_op jit(solution)/shard_map/psum | solution.py:56
  424.5 0.0 copy-done.1
  424.5 0.0 copy-done.10
  424.5 0.0 copy-start.4
  424.5 4.2 subtract_convert_fusion
  428.7 0.0 copy-start.2
  428.7 0.0 copy-done.4
  428.7 0.0 copy-start.5
  428.7 1.2 fusion.4
  429.9 0.1 copy-done.2
  430.0 0.0 copy-start.7
  430.0 0.7 copy-done.7
  430.7 0.8 copy-done.5
  431.5 3.0 fusion.16
  434.5 0.0 all-reduce.9.cloned.1.call-update
  434.5 1.5 dynamic-slice_convert_fusion
  436.0 0.9 copy.20
  437.0 0.0 copy-start.8
  437.0 4.6 convolution_convert_fusion
  441.6 0.0 copy-done.8
  441.6 3.0 convolution_convert_fusion.1
  444.6 141.6 %all-reduce.9.cloned.1.call-done = f32[256,3584]{0,1:T(8,128)} async-done(((f32[256,3584]{0,1:T(8,128)}), f32[256,3584]{0,1:T(8,128)}) %all-reduce.9.cloned.1.call-update) | async-done | bytes 3670032
  586.1 2.5 dynamic-slice_subtract_fusion
  588.6 1.2 copy.21
  (2 shorter events, 0.1 us)
Async XLA Ops:
  7.2 135.5 %copy-start = (bf16[1792,224]{0,1:T(8,128)(2,1)S(1)}, bf16[1792,224]{0,1:T(8,128)(2,1)}, u32[]{:S(2)}) copy-start(bf16[1792,224]{0,1:T(8,128)(2,1)} %param.13) | copy-start | bytes 2408452
  7.2 110.4 %reduce-scatter.3.cloned.1.call-start = ((), (), s32[]{:S(2)}) async-start(), calls=%async_computation.1 | async-start | bytes 1949696 | tf_op jit(solution)/shard_map/reduce_scatter | solution.py:34
  47.2 165.3 %copy-start.9 = (bf16[256,224]{0,1:T(8,128)(2,1)S(1)}, bf16[256,224]{0,1:T(8,128)(2,1)}, u32[]{:S(2)}) copy-start(bf16[256,224]{0,1:T(8,128)(2,1)} %param.9) | copy-start | bytes 344068
  50.7 213.3 %copy-start.11 = (f32[512]{0:T(512)S(1)}, f32[512]{0:T(512)}, u32[]{:S(2)}) copy-start(f32[512]{0:T(512)} %param.15) | copy-start | bytes 6148
  50.7 161.8 %all-reduce.5.cloned.1.call-start = ((), (), s32[]{:S(2)}) async-start(), calls=%async_computation.2 | async-start | bytes 229376 | tf_op jit(solution)/shard_map/psum | solution.py:48
  143.9 120.2 %all-gather.2.cloned.1.call-start = ((), (), s32[]{:S(2)}) async-start(), calls=%async_computation.3 | async-start | bytes 1949696 | tf_op jit(solution)/shard_map/all_gather | solution.py:50
  214.1 210.4 %all-reduce.7.cloned.1.call-start = ((), (), s32[]{:S(2)}) async-start(), calls=%async_computation.4 | async-start | bytes 7340032 | tf_op jit(solution)/shard_map/psum | solution.py:56
  264.0 4.8 copy-start.3
  268.1 0.7 copy-start.6
  272.3 152.2 %copy-start.1 = (bf16[256,3584]{0,1:T(8,128)(2,1)S(1)}, bf16[256,3584]{0,1:T(8,128)(2,1)}, u32[]{:S(2)}) copy-start(bf16[256,3584]{0,1:T(8,128)(2,1)} %all-gather.2.cloned.1.call-done) | copy-start | bytes 5505028
  272.3 152.2 %copy-start.10 = (f32[3584]{0:T(1024)S(1)}, f32[3584]{0:T(1024)}, u32[]{:S(2)}) copy-start(f32[3584]{0:T(1024)} %param.17) | copy-start | bytes 43012
  272.3 313.8 %all-reduce.9.cloned.1.call-start = ((), (), s32[]{:S(2)}) async-start(), calls=%async_computation.5 | async-start | bytes 7340032
  424.5 4.2 copy-start.4
  428.7 1.3 copy-start.2
  428.7 2.8 copy-start.5
  430.0 0.7 copy-start.7
  437.0 4.6 copy-start.8
Sparse Core Ops, SparseCore 0:
  50.8 66.6 reduce-scatter.2
  144.0 68.4 all-reduce.4
  215.5 48.5 all-gather.1
  272.5 152.0 all-reduce.6
  434.6 151.4 all-reduce.8
where the time goes:
time: 597 us; the launch traced here: 596 us
  waiting for transfers between devices  479 us (80%)
  blocking collectives  63.2 us (11%)
  matrix products  23.9 us (4%)
  between operations  13.9 us (2%)
  other arithmetic  10.2 us (2%)
    psum x1, waiting for transfers between devices, shards(): summed = lax.psum(partial_recon, ('mp', 'feat'))  152 us
    unnamed x6, waiting for transfers between devices  142 us
    psum x1, waiting for transfers between devices, shards(): lax.psum(partial_mixed.astype(jnp.bfloat16), 'mp').astype(jnp.float32)  68.6 us
    reduce_scatter x1, waiting for transfers between devices, shards(): lax.psum_scatter(jnp.dot(row_block, joint_weight, preferred_element_type=...  66.8 us
    all_gather x1, waiting for transfers between devices, shards(): stream = lax.all_gather(stream_cols, 'feat', axis=1, tiled=True)  49.9 us
    psum x1, blocking collectives, shards(): squares = lax.psum(jnp.sum(source * source, axis=1), 'feat')  39 us
    all_gather x1, blocking collectives, shards(): lax.all_gather(hidden, 'feat', axis=0, tiled=True)  24.2 us
  transfers between devices with their start and end apart: 5, of which 5 were waited for; matrix products, arithmetic and copies ran while one was open for 2% of the time, Pallas kernels for 0%

commit v1 on v0

v1 whole, which is shorter than its diff:
```python
import jax
import jax.numpy as jnp
from jax import lax
from jax.sharding import Mesh
from jax.sharding import PartitionSpec as P

D = 3584
ROWS = 256
HALF = ROWS // 2
CHIPS = 64

MP = ("zl", "x")
RING = ("y", "zh")
FEAT = RING + ("c",)
CHIP = MP + RING
ALL = MP + FEAT

sparsity_weight = 0.2
norm_eps = 1e-06
bf16 = jnp.bfloat16
f32 = jnp.float32


def dot(a, b, ca, cb):
    return lax.dot_general(a, b, (((ca,), (cb,)), ((), ())), preferred_element_type=f32)


def swap(v):
    return lax.ppermute(v, "c", [(0, 1), (1, 0)])


def scatter_sum(v, axes, parts):
    arrived = swap(v[HALF:].astype(bf16))
    both = (v[:HALF].astype(f32) + arrived.astype(f32)).astype(bf16)
    both = both.reshape(parts, HALF // parts, v.shape[1])
    both = lax.all_to_all(both, axes, 0, 0, tiled=True)
    return jnp.sum(both.astype(f32), axis=0)


def gather_rows(v, axes, parts):
    copies = jnp.broadcast_to(v[None], (parts,) + v.shape)
    own = lax.all_to_all(copies, axes, 0, 0, tiled=True).reshape(HALF, v.shape[1])
    return jnp.concatenate([own, swap(own)], axis=0)


def shards(
    residual_in,
    norm_gain,
    gate_weight,
    up_weight,
    down_weight,
    encoder_weight,
    encoder_bias,
    decoder_weight,
    decoder_bias,
):
    hidden_local = gate_weight.shape[1]
    core = lax.axis_index("c")
    at = lax.broadcasted_iota(jnp.int32, (ROWS, ROWS), 0)
    row = lax.broadcasted_iota(jnp.int32, (ROWS, ROWS), 1)
    inside = at % HALF
    wanted = (inside // 2) * 4 + ((at // HALF) ^ core) * 2 + inside % 2
    order = (row == wanted).astype(bf16)

    source = dot(order, residual_in, 1, 0)
    squares = jnp.sum(source * source, axis=1)
    scaled = (source * norm_gain[None, :]).astype(bf16)

    def three(v):
        hi = v.astype(bf16)
        mid = (v - hi.astype(f32)).astype(bf16)
        lo = (v - hi.astype(f32) - mid.astype(f32)).astype(bf16)
        return jnp.stack([hi, mid, lo], axis=-1)

    joint_weight = jnp.concatenate([gate_weight, up_weight], axis=1)
    partial = dot(scaled, joint_weight, 1, 0).astype(bf16)
    squares_both = squares[:HALF] + swap(squares[HALF:])
    arrived = swap(partial[HALF:])
    both = (partial[:HALF].astype(f32) + arrived.astype(f32)).astype(bf16)
    both = jnp.concatenate([both, jnp.pad(three(squares_both), ((0, 0), (0, 125)))], axis=1)
    both = lax.all_to_all(both.reshape(8, 16, both.shape[1]), RING, 0, 0, tiled=True)
    projected = jnp.sum(both.astype(f32), axis=0)
    mean = jnp.sum(projected[:, 2 * hidden_local :], axis=1, keepdims=True) / D
    projected = projected[:, : 2 * hidden_local] * lax.rsqrt(mean + norm_eps)
    hidden = (jax.nn.silu(projected[:, :hidden_local]) * projected[:, hidden_local:]).astype(bf16)

    hidden_all = gather_rows(hidden, RING, 8)
    partial_mixed = (dot(hidden_all, down_weight, 1, 0) + source * 0.125).astype(bf16)
    other = swap(partial_mixed[HALF:])
    own = partial_mixed[:HALF]
    first = jnp.where(core == 0, own, other)
    second = jnp.where(core == 0, other, own)
    columns = jnp.stack([first.reshape(CHIPS, 2, -1), second.reshape(CHIPS, 2, -1)], axis=1)
    columns = lax.all_to_all(columns, CHIP, 0, 0, tiled=True)
    columns = jnp.sum(columns.reshape(8, 8, 2, 2, -1).astype(f32), axis=0)
    stream_own = columns.transpose(2, 0, 1, 3).reshape(2, D).astype(bf16)
    stream = gather_rows(stream_own, CHIP, CHIPS)

    encoded = dot(stream, encoder_weight, 1, 0) + encoder_bias[None, :]
    feature_codes = jax.nn.softplus(encoded).astype(bf16)
    recon_own = scatter_sum(dot(feature_codes, decoder_weight, 1, 0), CHIP, CHIPS) + decoder_bias[None, :]
    error_own = (recon_own - stream_own.astype(f32)).astype(bf16)
    error = gather_rows(error_own, CHIP, CHIPS)
    code_gradient = dot(error, decoder_weight, 1, 1)
    encoded_gradient = (jax.nn.sigmoid(encoded) * (code_gradient + sparsity_weight)).astype(bf16)
    input_gradient = scatter_sum(
        dot(encoded_gradient, encoder_weight, 1, 1), CHIP, CHIPS
    ) - error_own.astype(f32)
    decoder_gradient = dot(feature_codes, error, 0, 0).astype(bf16)
    encoder_gradient = dot(stream, encoded_gradient, 0, 0).astype(bf16)
    codes_out = dot(order, feature_codes, 0, 0).astype(bf16)
    return codes_out, recon_own.astype(bf16), encoder_gradient, decoder_gradient, input_gradient


def solution(mesh):
    fine = Mesh(mesh.devices.reshape(2, 4, 4, 2, 2), ("zl", "x", "y", "zh", "c"))
    in_specs = (
        P(None, FEAT),
        P(FEAT),
        P(FEAT, MP),
        P(FEAT, MP),
        P(MP, FEAT),
        P(None, ALL),
        P(ALL),
        P(ALL, None),
        P(),
    )
    out_specs = (P(None, ALL), P(ALL, None), P(None, ALL), P(ALL, None), P(ALL, None))
    return jax.shard_map(shards, mesh=fine, in_specs=in_specs, out_specs=out_specs, check_vma=False)
```

time: 597 us -> 187 us (0.31)
  waiting for transfers between devices: 479 us -> 22.8 us
  blocking collectives: 63.2 us -> 118 us
  between operations: 13.9 us -> 1.23 us
  starting transfers between devices: 0.21 us -> 6.46 us
    psum x2 -> x0, waiting for transfers between devices: 221 us -> none  [the longest x1 152 us: shards(): summed = lax.psum(partial_recon, ('mp', 'feat'))]
    unnamed x6 -> x0, waiting for transfers between devices: 142 us -> none
    all_to_all x0 -> x6, blocking collectives: none -> 118 us  [the longest x3 55.1 us: gather_rows(): lax.all_to_all(copies, axes, 0, 0, tiled=True).reshape(HALF, v.shape[1])]
    reduce_scatter x1 -> x0, waiting for transfers between devices: 66.8 us -> none  [shards(): lax.psum_scatter(jnp.dot(row_block, joint_weight, preferred_element_type=...]
    all_gather x1 -> x0, waiting for transfers between devices: 49.9 us -> none  [shards(): stream = lax.all_gather(stream_cols, 'feat', axis=1, tiled=True)]
    psum x1 -> x0, blocking collectives: 39 us -> none  [shards(): squares = lax.psum(jnp.sum(source * source, axis=1), 'feat')]
    all_gather x1 -> x0, blocking collectives: 24.2 us -> none  [shards(): lax.all_gather(hidden, 'feat', axis=0, tiled=True)]
    ppermute x0 -> x8, waiting for transfers between devices: none -> 14 us  [swap(): return lax.ppermute(v, 'c', [(0, 1), (1, 0)])]
  transfers between devices with their start and end apart: 5 -> 9, of which waited for: 5 -> 8; matrix products, arithmetic and copies ran while one was open for 2% -> 6% of each run, Pallas kernels for 0% -> 0%
where the time goes in v1:
time: 187 us; the launch traced here: 186 us
  blocking collectives  118 us (63%)
  waiting for transfers between devices  22.8 us (12%)
  matrix products  20.5 us (11%)
  local copies, waits for them, and re-layouts  10.8 us (6%)
  starting transfers between devices  6.46 us (3%)
  other arithmetic  5.92 us (3%)
    all_to_all x3, blocking collectives, gather_rows(): lax.all_to_all(copies, axes, 0, 0, tiled=True).reshape(HALF, v.shape[1])  55.1 us
    all_to_all x1, blocking collectives, shards(): lax.all_to_all(both.reshape(8, 16, both.shape[1]), RING, 0, 0, tiled=True)  24 us
    all_to_all x1, blocking collectives, scatter_sum(): both = lax.all_to_all(both, axes, 0, 0, tiled=True)  22.7 us
    dot_general x10, matrix products, dot(): lax.dot_general(a, b, (((ca,), (cb,)), ((), ())), preferred_element_type=...  20.5 us
    all_to_all x1, blocking collectives, shards(): columns = lax.all_to_all(columns, CHIP, 0, 0, tiled=True)  16.4 us
    ppermute x8, waiting for transfers between devices, swap(): return lax.ppermute(v, 'c', [(0, 1), (1, 0)])  14 us
    all_to_all x1, waiting for transfers between devices, scatter_sum(): both = lax.all_to_all(both, axes, 0, 0, tiled=True)  8.76 us
    all_to_all x1, starting transfers between devices, scatter_sum(): both = lax.all_to_all(both, axes, 0, 0, tiled=True)  5.07 us
  transfers between devices with their start and end apart: 9, of which 8 were waited for; matrix products, arithmetic and copies ran while one was open for 6% of the time, Pallas kernels for 0%

profile of v1, /device:TPU:0, one launch (start us, length us, event | category | flops | bytes accessed | tf_op | source)
XLA Modules:
  0.0 186.0 jit_solution(3551095928024920360)
XLA Ops:
  0.8 1.5 multiply_reduce_fusion
  2.4 0.8 convolution_convert_fusion.2
  3.2 0.1 slice.59
  3.2 0.1 collective-permute-start
  3.3 0.5 collective-permute-start.1
  3.8 1.7 collective-permute-done.1
  5.5 0.6 pad_maximum_fusion.1
  6.1 1.4 copy.33
  7.5 1.4 add_convert_fusion
  8.9 0.1 fusion.9
  9.0 24.0 %all_to_all.35 = bf16[8,16,3712]{2,1,0:T(8,128)(2,1)S(1)} all-to-all(bf16[8,16,3712]{2,1,0:T(8,128)(2,1)S(1)} %bitcast.23), channel_id=1, replica_groups=mesh['zl'=2,'x'=4,'y'=4,'zh'=2,'c'=2] {'y','zh'}, dimensions={0} | all-to-all | bytes 1900544 | tf_op jit(solution)/shard_map/all_to_all | solution.py:81
  33.0 0.1 convert_reduce_fusion
  33.1 0.1 slice_reduce_fusion
  33.3 0.1 slice_multiply_fusion
  33.5 12.7 %all_to_all.36 = bf16[8,16,1792]{2,1,0:T(8,128)(2,1)S(1)} all-to-all(bf16[8,16,1792]{2,1,0:T(8,128)(2,1)S(1)} %broadcast_in_dim.6), channel_id=1, replica_groups=mesh['zl'=2,'x'=4,'y'=4,'zh'=2,'c'=2] {'y','zh'}, dimensions={0} | all-to-all | bytes 917504 | tf_op jit(solution)/shard_map/all_to_all | solution.py:42
  46.1 1.8 collective-permute-done.2
  47.9 0.4 fusion.8
  48.4 0.2 collective-permute-start.3
  48.6 1.1 collective-permute-done.3
  49.7 0.1 copy.34
  49.9 0.1 copy.35
  50.1 0.2 pad_maximum_fusion
  50.3 0.1 copy.36
  50.4 16.4 %all_to_all.37 = bf16[64,2,2,224]{3,2,1,0:T(2,128)(2,1)S(1)} all-to-all(bf16[64,2,2,224]{3,2,1,0:T(2,128)(2,1)S(1)} %copy.36), channel_id=1, replica_groups=mesh['zl'=2,'x'=4,'y'=4,'zh'=2,'c'=2] {'zl','x','y','zh'}, dimensions={0} | all-to-all | bytes 229376 | tf_op jit(solution)/shard_map/all_to_all | solution.py:94
  66.8 0.1 reduce
  66.9 0.1 convert_element_type.137
  67.1 0.6 copy-done.15
  67.6 0.5 broadcast_in_dim.7
  68.1 21.1 %all_to_all.38 = bf16[64,2,3584]{2,1,0:T(2,128)(2,1)S(1)} all-to-all(bf16[64,2,3584]{2,1,0:T(2,128)(2,1)S(1)} %broadcast_in_dim.7), channel_id=1, replica_groups=mesh['zl'=2,'x'=4,'y'=4,'zh'=2,'c'=2] {'zl','x','y','zh'}, dimensions={0} | all-to-all | bytes 1835008 | tf_op jit(solution)/shard_map/all_to_all | solution.py:42
  89.2 0.3 reshape.74
  89.6 0.1 collective-permute-start.4
  89.8 2.4 %collective-permute-done.4 = bf16[128,3584]{1,0:T(8,128)(2,1)S(1)} collective-permute-done((bf16[128,3584]{1,0:T(8,128)(2,1)S(1)}, bf16[128,3584]{1,0:T(8,128)(2,1)S(1)}, u32[]{:S(2)}, u32[]{:S(2)}) %collective-permute-start.4) | collective-permute-done | bytes 917536 | tf_op jit(solution)/shard_map/ppermute | solution.py:29
  92.2 3.3 %convolution_add_fusion.1 = f32[256,512]{1,0:T(8,128)S(1)} fusion(bf16[256,3584]{1,0:T(8,128)(2,1)S(1)} %constant_dynamic-update-slice_fusion, bf16[3584,512]{1,0:T(8,128)(2,1)} %param.14, f32[512]{0:T(512)S(1)} %copy-done.25), kind=kOutput, calls=%fused_computation.21 | convolution fusion | flops 939655168 | bytes 6031360 | tf_op jit(solution)/shard_map/dot_general | solution.py:25
  95.6 1.3 fusion.32
  96.8 0.1 slice.95
  97.0 0.2 collective-permute-start.5
  97.2 2.3 %collective-permute-done.5 = bf16[128,3584]{1,0:T(8,128)(2,1)S(1)} collective-permute-done((bf16[128,3584]{1,0:T(8,128)(2,1)S(1)}, bf16[128,3584]{1,0:T(8,128)(2,1)S(1)}, u32[]{:S(2)}, u32[]{:S(2)}) %collective-permute-start.5) | collective-permute-done | bytes 917536 | tf_op jit(solution)/shard_map/ppermute | solution.py:29
  99.5 0.2 fusion.2
  99.7 1.3 reshape.75
  100.9 22.7 %all_to_all.39 = bf16[64,2,3584]{2,1,0:T(2,128)(2,1)S(1)} all-to-all(bf16[64,2,3584]{2,1,0:T(2,128)(2,1)} %reshape.75), channel_id=1, replica_groups=mesh['zl'=2,'x'=4,'y'=4,'zh'=2,'c'=2] {'zl','x','y','zh'}, dimensions={0} | all-to-all | bytes 1835008 | tf_op jit(solution)/shard_map/all_to_all | solution.py:36
  123.7 0.7 convert_reduce_fusion.2
  124.4 0.6 subtract_convert_fusion
  125.1 0.5 broadcast_in_dim.8
  125.5 0.1 copy-done.17
  125.7 21.3 %all_to_all.40 = bf16[64,2,3584]{2,1,0:T(2,128)(2,1)} all-to-all(bf16[64,2,3584]{2,1,0:T(2,128)(2,1)S(1)} %broadcast_in_dim.8), channel_id=1, replica_groups=mesh['zl'=2,'x'=4,'y'=4,'zh'=2,'c'=2] {'zl','x','y','zh'}, dimensions={0} | all-to-all | bytes 1835008 | tf_op jit(solution)/shard_map/all_to_all | solution.py:42
  147.0 2.5 %reshape.76 = bf16[128,3584]{1,0:T(8,128)(2,1)S(1)} reshape(bf16[64,2,3584]{2,1,0:T(2,128)(2,1)} %all_to_all.40) | data formatting | bytes 1835008 | tf_op jit(solution)/shard_map/reshape | solution.py:42
  149.4 0.1 collective-permute-start.6
  149.5 0.1 constant_dynamic-update-slice_fusion.3
  149.6 2.4 %collective-permute-done.6 = bf16[128,3584]{1,0:T(8,128)(2,1)S(1)} collective-permute-done((bf16[128,3584]{1,0:T(8,128)(2,1)S(1)}, bf16[128,3584]{1,0:T(8,128)(2,1)S(1)}, u32[]{:S(2)}, u32[]{:S(2)}) %collective-permute-start.6) | collective-permute-done | bytes 917536 | tf_op jit(solution)/shard_map/ppermute | solution.py:29
  152.1 1.2 copy-done.2
  153.3 3.3 %fusion.7 = bf16[256,512]{1,0:T(8,128)(2,1)S(1)} fusion(bf16[256,3584]{1,0:T(8,128)(2,1)S(1)} %constant_dynamic-update-slice_fusion.2, bf16[512,3584]{1,0:T(8,128)(2,1)} %param.16, f32[256,512]{1,0:T(8,128)S(1)} %copy-done.6), kind=kOutput, calls=%fused_computation.22 | convolution fusion | flops 940310528 | bytes 6291456 | tf_op jit(solution)/shard_map/dot_general | solution.py:25
  156.7 1.1 fusion.35
  157.8 0.1 slice.94
  157.9 0.2 collective-permute-start.7
  158.2 2.3 %collective-permute-done.7 = bf16[128,3584]{1,0:T(8,128)(2,1)S(1)} collective-permute-done((bf16[128,3584]{1,0:T(8,128)(2,1)S(1)}, bf16[128,3584]{1,0:T(8,128)(2,1)S(1)}, u32[]{:S(2)}, u32[]{:S(2)}) %collective-permute-start.7) | collective-permute-done | bytes 917536 | tf_op jit(solution)/shard_map/ppermute | solution.py:29
  160.5 0.2 fusion.1
  160.7 1.3 reshape.77
  162.0 5.1 %all-to-all-start.6 = ((bf16[64,2,3584]{2,1,0:T(2,128)(2,1)}), bf16[64,2,3584]{2,1,0:T(2,128)(2,1)S(1)}, u32[]{:S(2)}, u32[]{:S(2)}) async-start(bf16[64,2,3584]{2,1,0:T(2,128)(2,1)} %reshape.77), calls=%async_computation.6 | async-start | bytes 1835008 | tf_op jit(solution)/shard_map/all_to_all | solution.py:36
  167.1 2.6 %convolution_convert_fusion.3 = bf16[256,512]{1,0:T(8,128)(2,1)} fusion(s32[]{:T(128)S(6)} %axis_index.12, s32[256]{0:T(256)} %copy-done.21, s32[256]{0:T(256)} %copy-done.24, s32[256]{0:T(256)} %copy-done.22, s32[256]{0:T(256)} %copy-done.23, pred[256]{0:T(512)(128)(4,1)} %copy-done.26, pred[256]{0:T(512)(128)(4,1)} %copy-done.27, f32[256,512]{1,0:T(8,128)} %copy-done.5), kind=kOutput, calls=%fused_computation.23 | convolution fusion | flops 69926912 | bytes 791044 | tf_op jit(solution)/shard_map/dot_general | solution.py:25
  169.6 3.0 %convolution_convert_fusion.1 = bf16[3584,512]{1,0:T(8,128)(2,1)} fusion(bf16[256,3584]{1,0:T(8,128)(2,1)S(1)} %constant_dynamic-update-slice_fusion, bf16[256,512]{1,0:T(8,128)(2,1)S(1)} %copy-done.9), kind=kOutput, calls=%fused_computation.1 | convolution fusion | flops 941359104 | bytes 5767168 | tf_op jit(solution)/shard_map/dot_general | solution.py:25
  172.6 3.2 %convolution_convert_fusion = bf16[512,3584]{1,0:T(8,128)(2,1)} fusion(bf16[256,3584]{1,0:T(8,128)(2,1)S(1)} %copy-done.3, f32[256,512]{1,0:T(8,128)S(1)} %copy-done.7), kind=kOutput, calls=%fused_computation | convolution fusion | flops 942276608 | bytes 6029312 | tf_op jit(solution)/shard_map/dot_general | solution.py:25
  175.8 8.8 %all-to-all-done.6 = bf16[64,2,3584]{2,1,0:T(2,128)(2,1)S(1)} async-done(((bf16[64,2,3584]{2,1,0:T(2,128)(2,1)}), bf16[64,2,3584]{2,1,0:T(2,128)(2,1)S(1)}, u32[]{:S(2)}, u32[]{:S(2)}) %all-to-all-start.6) | async-done | bytes 917536 | tf_op jit(solution)/shard_map/all_to_all | solution.py:36
  184.6 0.7 convert_reduce_fusion.1
  185.3 0.6 convert_subtract_fusion
  (71 shorter events, 0.5 us)
Async XLA Ops:
  0.6 47.3 %copy-start = (bf16[1792,224]{0,1:T(8,128)(2,1)S(1)}, bf16[1792,224]{0,1:T(8,128)(2,1)}, u32[]{:S(2)}) copy-start(bf16[1792,224]{0,1:T(8,128)(2,1)} %param.13) | copy-start | bytes 2408452
  0.6 1.7 copy-start.20
  0.7 1.7 copy-start.10
  0.7 1.6 copy-start.21
  0.7 1.6 copy-start.22
  0.7 1.6 copy-start.23
  0.7 1.6 copy-start.24
  0.7 1.6 copy-start.26
  0.8 1.6 copy-start.27
  0.8 1.6 copy-start.11
  2.4 0.8 copy-start.12
  3.2 4.3 %collective-permute-start = (bf16[128,3584]{1,0:T(8,128)(2,1)S(1)}, bf16[128,3584]{1,0:T(8,128)(2,1)}, u32[]{:S(2)}, u32[]{:S(2)}) collective-permute-start(bf16[128,3584]{1,0:T(8,128)(2,1)S(1)} %slice.59), channel_id=1, source_target_pairs={{0,1},{1,0},{2,3},{3,2},{4,5},{5,4},{6,7},{7,6},{8,9},{9,8},{10,11... | collective-permute-start | bytes 2752520 | tf_op jit(solution)/shard_map/ppermute | solution.py:29
  3.3 2.2 %collective-permute-start.1 = (f32[128]{0:T(128)S(1)}, f32[128]{0:T(128)S(1)}, u32[]{:S(2)}, u32[]{:S(2)}) collective-permute-start(f32[128]{0:T(128)S(1)} %slice.47), channel_id=1, source_target_pairs={{0,1},{1,0},{2,3},{3,2},{4,5},{5,4},{6,7},{7,6},{8,9},{9,8},{10,11... | collective-permute-start | bytes 1544 | tf_op jit(solution)/shard_map/ppermute | solution.py:29
  7.5 1.4 copy-start.14
  33.0 14.9 %copy-start.13 = (f32[256,224]{0,1:T(8,128)S(1)}, f32[256,224]{0,1:T(8,128)}, u32[]{:S(2)}) copy-start(f32[256,224]{0,1:T(8,128)} %copy-done.12) | copy-start | bytes 688132
  46.1 1.8 collective-permute-start.2
  48.4 1.3 collective-permute-start.3
  67.0 0.6 copy-start.15
  89.6 2.6 %copy-start.25 = (f32[512]{0:T(512)S(1)}, f32[512]{0:T(512)}, u32[]{:S(2)}) copy-start(f32[512]{0:T(512)} %param.15) | copy-start | bytes 6148
  89.6 2.6 %collective-permute-start.4 = (bf16[128,3584]{1,0:T(8,128)(2,1)S(1)}, bf16[128,3584]{1,0:T(8,128)(2,1)S(1)}, u32[]{:S(2)}, u32[]{:S(2)}) collective-permute-start(bf16[128,3584]{1,0:T(8,128)(2,1)S(1)} %reshape.74), channel_id=1, source_target_pairs={{0,1},{1,0},{2,3},{3,2},{4,5},{5,4},{6,7},{7,6},{8,9},{9,8},{10,11... | collective-permute-start | bytes 2752520 | tf_op jit(solution)/shard_map/ppermute | solution.py:29
  92.2 3.3 %copy-start.1 = (bf16[512,3584]{1,0:T(8,128)(2,1)S(1)}, bf16[512,3584]{1,0:T(8,128)(2,1)}, u32[]{:S(2)}) copy-start(bf16[512,3584]{1,0:T(8,128)(2,1)} %param.16) | copy-start | bytes 11010052
  95.5 1.3 copy-start.5
  97.0 2.6 %collective-permute-start.5 = (bf16[128,3584]{1,0:T(8,128)(2,1)S(1)}, bf16[128,3584]{1,0:T(8,128)(2,1)S(1)}, u32[]{:S(2)}, u32[]{:S(2)}) collective-permute-start(bf16[128,3584]{1,0:T(8,128)(2,1)S(1)} %slice.95), channel_id=1, source_target_pairs={{0,1},{1,0},{2,3},{3,2},{4,5},{5,4},{6,7},{7,6},{8,9},{9,8},{10,11... | collective-permute-start | bytes 2752520 | tf_op jit(solution)/shard_map/ppermute | solution.py:29
  100.9 23.5 %copy-start.16 = (bf16[2,3584]{1,0:T(2,128)(2,1)S(1)}, bf16[2,3584]{1,0:T(2,128)(2,1)}, u32[]{:S(2)}) copy-start(bf16[2,3584]{1,0:T(2,128)(2,1)} %copy-done.15) | copy-start | bytes 43012
  100.9 23.5 %copy-start.19 = (f32[3584]{0:T(1024)S(1)}, f32[3584]{0:T(1024)}, u32[]{:S(2)}) copy-start(f32[3584]{0:T(1024)} %param.17) | copy-start | bytes 43012
  125.1 0.6 copy-start.17
  149.4 3.9 %copy-start.6 = (f32[256,512]{1,0:T(8,128)S(1)}, f32[256,512]{1,0:T(8,128)}, u32[]{:S(2)}) copy-start(f32[256,512]{1,0:T(8,128)} %copy-done.5) | copy-start | bytes 1572868
  149.4 2.6 %collective-permute-start.6 = (bf16[128,3584]{1,0:T(8,128)(2,1)S(1)}, bf16[128,3584]{1,0:T(8,128)(2,1)S(1)}, u32[]{:S(2)}, u32[]{:S(2)}) collective-permute-start(bf16[128,3584]{1,0:T(8,128)(2,1)S(1)} %reshape.76), channel_id=1, source_target_pairs={{0,1},{1,0},{2,3},{3,2},{4,5},{5,4},{6,7},{7,6},{8,9},{9,8},{10,11... | collective-permute-start | bytes 2752520 | tf_op jit(solution)/shard_map/ppermute | solution.py:29
  152.1 1.2 copy-start.2
  153.3 3.4 %copy-start.4 = (bf16[3584,512]{1,0:T(8,128)(2,1)S(1)}, bf16[3584,512]{1,0:T(8,128)(2,1)}, u32[]{:S(2)}) copy-start(bf16[3584,512]{1,0:T(8,128)(2,1)} %param.14) | copy-start | bytes 11010052
  156.7 1.2 copy-start.8
  157.9 2.6 %collective-permute-start.7 = (bf16[128,3584]{1,0:T(8,128)(2,1)S(1)}, bf16[128,3584]{1,0:T(8,128)(2,1)S(1)}, u32[]{:S(2)}, u32[]{:S(2)}) collective-permute-start(bf16[128,3584]{1,0:T(8,128)(2,1)S(1)} %slice.94), channel_id=1, source_target_pairs={{0,1},{1,0},{2,3},{3,2},{4,5},{5,4},{6,7},{7,6},{8,9},{9,8},{10,11... | collective-permute-start | bytes 2752520 | tf_op jit(solution)/shard_map/ppermute | solution.py:29
  162.0 22.6 %all-to-all-start.6 = ((bf16[64,2,3584]{2,1,0:T(2,128)(2,1)}), bf16[64,2,3584]{2,1,0:T(2,128)(2,1)S(1)}, u32[]{:S(2)}, u32[]{:S(2)}) async-start(bf16[64,2,3584]{2,1,0:T(2,128)(2,1)} %reshape.77), calls=%async_computation.6 | async-start | bytes 1835008 | tf_op jit(solution)/shard_map/all_to_all | solution.py:36
  167.0 2.6 %copy-start.9 = (bf16[256,512]{1,0:T(8,128)(2,1)S(1)}, bf16[256,512]{1,0:T(8,128)(2,1)}, u32[]{:S(2)}) copy-start(bf16[256,512]{1,0:T(8,128)(2,1)} %copy-done.8) | copy-start | bytes 786436
  169.6 3.0 %copy-start.3 = (bf16[256,3584]{1,0:T(8,128)(2,1)S(1)}, bf16[256,3584]{1,0:T(8,128)(2,1)}, u32[]{:S(2)}) copy-start(bf16[256,3584]{1,0:T(8,128)(2,1)} %copy-done.2) | copy-start | bytes 5505028
  169.6 3.0 %copy-start.7 = (f32[256,512]{1,0:T(8,128)S(1)}, f32[256,512]{1,0:T(8,128)}, u32[]{:S(2)}) copy-start(f32[256,512]{1,0:T(8,128)} %copy-done.5) | copy-start | bytes 1572868
  172.6 12.7 %copy-start.18 = (bf16[2,3584]{1,0:T(2,128)(2,1)S(1)}, bf16[2,3584]{1,0:T(2,128)(2,1)}, u32[]{:S(2)}) copy-start(bf16[2,3584]{1,0:T(2,128)(2,1)} %copy-done.17) | copy-start | bytes 43012

commit v2 on v1

v2 whole, which is shorter than its diff:
```python
import jax
import jax.numpy as jnp
from jax import lax
from jax.sharding import Mesh
from jax.sharding import PartitionSpec as P

D = 3584
ROWS = 256
HALF = ROWS // 2
CHIPS = 64

MP = ("zl", "x")
RING = ("y", "zh")
FEAT = RING + ("c",)
CHIP = MP + RING
ALL = MP + FEAT

sparsity_weight = 0.2
norm_eps = 1e-06
bf16 = jnp.bfloat16
f32 = jnp.float32


def dot(a, b, ca, cb):
    return lax.dot_general(a, b, (((ca,), (cb,)), ((), ())), preferred_element_type=f32)


def swap(v):
    return lax.ppermute(v, "c", [(0, 1), (1, 0)])


def exchange(v, axes):
    return lax.all_to_all(v, axes, 0, 0, tiled=True)


def copies_to(v, axes, parts):
    return exchange(jnp.broadcast_to(v[None], (parts,) + v.shape), axes)


def three(v):
    hi = v.astype(bf16)
    mid = (v - hi.astype(f32)).astype(bf16)
    lo = (v - hi.astype(f32) - mid.astype(f32)).astype(bf16)
    return jnp.stack([hi, mid, lo], axis=-1)


def shards(
    residual_in,
    norm_gain,
    gate_weight,
    up_weight,
    down_weight,
    encoder_weight,
    encoder_bias,
    decoder_weight,
    decoder_bias,
):
    hidden_local = gate_weight.shape[1]
    core = lax.axis_index("c")

    def by_core(zero, one):
        return jnp.where(core == 0, zero, one)

    at = lax.broadcasted_iota(jnp.int32, (ROWS, ROWS), 0)
    row = lax.broadcasted_iota(jnp.int32, (ROWS, ROWS), 1)
    inside = at % HALF
    order = (row == (inside // 2) * 4 + (at // HALF) * 2 + inside % 2).astype(bf16)
    keep_order = by_core(order[:HALF], order[HALF:])
    send_order = by_core(order[HALF:], order[:HALF])

    joint_weight = jnp.concatenate([gate_weight, up_weight], axis=1)

    def project(rows):
        source = dot(rows, residual_in, 1, 0)
        squares = jnp.sum(source * source, axis=1)
        return dot((source * norm_gain[None, :]).astype(bf16), joint_weight, 1, 0), squares

    sent, squares_sent = project(send_order)
    arrived, squares_arrived = swap(sent.astype(bf16)), swap(squares_sent)
    kept, squares_kept = project(keep_order)
    both = (kept + arrived.astype(f32)).astype(bf16)
    both = jnp.concatenate([both, jnp.pad(three(squares_kept + squares_arrived), ((0, 0), (0, 125)))], axis=1)
    both = exchange(both.reshape(8, 16, both.shape[1]), RING)
    projected = jnp.sum(both.astype(f32), axis=0)
    mean = jnp.sum(projected[:, 2 * hidden_local :], axis=1, keepdims=True) / D
    projected = projected[:, : 2 * hidden_local] * lax.rsqrt(mean + norm_eps)
    hidden = (jax.nn.silu(projected[:, :hidden_local]) * projected[:, hidden_local:]).astype(bf16)

    hidden_kept = copies_to(hidden, RING, 8).reshape(HALF, hidden_local)
    hidden_other = swap(hidden_kept)
    mixed_kept = dot(down_weight, hidden_kept, 0, 1).astype(bf16)
    mixed_other = dot(down_weight, hidden_other, 0, 1).astype(bf16)
    mixed = by_core(
        jnp.concatenate([mixed_kept, mixed_other], axis=1),
        jnp.concatenate([mixed_other, mixed_kept], axis=1),
    )
    mixed = jnp.sum(copies_to(mixed, MP, 8).astype(f32), axis=0)
    stream_cols = (dot(residual_in, order, 0, 1) + mixed).astype(bf16)

    blocks_kept = copies_to(stream_cols, RING, 8)
    blocks_other = swap(blocks_kept)
    encoder_blocks = encoder_weight.reshape(8, 2, D // 16, -1)
    encoder_kept = by_core(encoder_blocks[:, 0], encoder_blocks[:, 1]).reshape(D // 2, -1)
    encoder_other = by_core(encoder_blocks[:, 1], encoder_blocks[:, 0]).reshape(D // 2, -1)
    encoded = (
        dot(blocks_kept.reshape(D // 2, ROWS), encoder_kept, 0, 0)
        + dot(blocks_other.reshape(D // 2, ROWS), encoder_other, 0, 0)
        + encoder_bias[None, :]
    )
    codes = jax.nn.softplus(encoded).astype(bf16)
    codes_kept = by_core(codes[:HALF], codes[HALF:])
    codes_other = by_core(codes[HALF:], codes[:HALF])

    arrived = swap(dot(codes_other, decoder_weight, 1, 0).astype(bf16))
    both = (dot(codes_kept, decoder_weight, 1, 0) + arrived.astype(f32)).astype(bf16)
    recon_own = jnp.sum(exchange(both.reshape(CHIPS, 2, D), CHIP).astype(f32), axis=0) + decoder_bias[None, :]

    stream = by_core(
        jnp.stack([blocks_kept, blocks_other], axis=1),
        jnp.stack([blocks_other, blocks_kept], axis=1),
    ).reshape(D, ROWS)
    chip = lax.axis_index(CHIP)
    own = core * HALF + chip * 2 + lax.broadcasted_iota(jnp.int32, (2, ROWS), 0)
    own = (lax.broadcasted_iota(jnp.int32, (2, ROWS), 1) == own).astype(bf16)
    stream_own = dot(own, stream, 1, 1)
    codes_out = dot(order, codes, 0, 0).astype(bf16)

    error_own = (recon_own - stream_own).astype(bf16)
    error_kept = copies_to(error_own, CHIP, CHIPS).reshape(HALF, D)
    error_other = swap(error_kept)
    slope = jax.nn.sigmoid(encoded)
    slope_kept = by_core(slope[:HALF], slope[HALF:])
    slope_other = by_core(slope[HALF:], slope[:HALF])
    grad_kept = (slope_kept * (dot(error_kept, decoder_weight, 1, 1) + sparsity_weight)).astype(bf16)
    grad_other = (slope_other * (dot(error_other, decoder_weight, 1, 1) + sparsity_weight)).astype(bf16)
    arrived = swap(dot(grad_other, encoder_weight, 1, 1).astype(bf16))
    both = (dot(grad_kept, encoder_weight, 1, 1) + arrived.astype(f32)).astype(bf16)
    input_gradient = jnp.sum(
        exchange(both.reshape(CHIPS, 2, D), CHIP).astype(f32), axis=0
    ) - error_own.astype(f32)

    decoder_gradient = dot(
        jnp.concatenate([codes_kept, codes_other], axis=0),
        jnp.concatenate([error_kept, error_other], axis=0),
        0,
        0,
    ).astype(bf16)
    grad = by_core(
        jnp.concatenate([grad_kept, grad_other], axis=0),
        jnp.concatenate([grad_other, grad_kept], axis=0),
    )
    encoder_gradient = dot(stream, grad, 1, 0).astype(bf16)
    return codes_out, recon_own.astype(bf16), encoder_gradient, decoder_gradient, input_gradient


def solution(mesh):
    fine = Mesh(mesh.devices.reshape(2, 4, 4, 2, 2), ("zl", "x", "y", "zh", "c"))
    in_specs = (
        P(None, FEAT),
        P(FEAT),
        P(FEAT, MP),
        P(FEAT, MP),
        P(MP, FEAT),
        P(None, ALL),
        P(ALL),
        P(ALL, None),
        P(),
    )
    out_specs = (P(None, ALL), P(ALL, None), P(None, ALL), P(ALL, None), P(ALL, None))
    return jax.shard_map(shards, mesh=fine, in_specs=in_specs, out_specs=out_specs, check_vma=False)
```

time: 187 us -> 188 us (level)
  blocking collectives: 118 us -> 95.8 us
  waiting for transfers between devices: 22.8 us -> 35.7 us
  matrix products: 20.5 us -> 26.1 us
  starting transfers between devices: 6.46 us -> 11.4 us
    all_to_all x6 -> x5, blocking collectives: 118 us -> 95.8 us  [exchange(): return lax.all_to_all(v, axes, 0, 0, tiled=True)]
    all_to_all x1 -> x2, waiting for transfers between devices: 8.76 us -> 26 us  [exchange(): return lax.all_to_all(v, axes, 0, 0, tiled=True)]
    dot_general x10 -> x19, matrix products: 20.5 us -> 26.1 us  [dot(): lax.dot_general(a, b, (((ca,), (cb,)), ((), ())), preferred_element_type=...]
    all_to_all x1 -> x2, starting transfers between devices: 5.07 us -> 10.3 us  [exchange(): return lax.all_to_all(v, axes, 0, 0, tiled=True)]
    ppermute x8 -> x7, waiting for transfers between devices: 14 us -> 9.7 us  [swap(): return lax.ppermute(v, 'c', [(0, 1), (1, 0)])]
    reshape x4 -> x3, local copies, waits for them, and re-layouts: 5.37 us -> 6.83 us  [the longest x2 4.36 us: shards(): both.reshape(CHIPS, 2, D)]
  transfers between devices with their start and end apart: 9 -> 9, of which waited for: 8 -> 8; matrix products, arithmetic and copies ran while one was open for 6% -> 7% of each run, Pallas kernels for 0% -> 0%
where the time goes in v2:
time: 188 us; the launch traced here: 187 us
  blocking collectives  95.8 us (51%)
  waiting for transfers between devices  35.7 us (19%)
  matrix products  26.1 us (14%)
  starting transfers between devices  11.4 us (6%)
  local copies, waits for them, and re-layouts  10.6 us (6%)
  other arithmetic  6.53 us (3%)
    all_to_all x5, blocking collectives, exchange(): return lax.all_to_all(v, axes, 0, 0, tiled=True)  95.8 us
    dot_general x19, matrix products, dot(): lax.dot_general(a, b, (((ca,), (cb,)), ((), ())), preferred_element_type=...  26.1 us
    all_to_all x2, waiting for transfers between devices, exchange(): return lax.all_to_all(v, axes, 0, 0, tiled=True)  26 us
    all_to_all x2, starting transfers between devices, exchange(): return lax.all_to_all(v, axes, 0, 0, tiled=True)  10.3 us
    ppermute x7, waiting for transfers between devices, swap(): return lax.ppermute(v, 'c', [(0, 1), (1, 0)])  9.7 us
    reshape x2, local copies, waits for them, and re-layouts, shards(): both.reshape(CHIPS, 2, D)  4.36 us
  transfers between devices with their start and end apart: 9, of which 8 were waited for; matrix products, arithmetic and copies ran while one was open for 7% of the time, Pallas kernels for 0%

profile of v2, /device:TPU:0, one launch (start us, length us, event | category | flops | bytes accessed | tf_op | source)
XLA Modules:
  0.0 187.4 jit_solution(7690427413537657440)
XLA Ops:
  0.8 1.3 constant_dynamic-update-slice_fusion.1
  2.1 0.1 constant_dynamic-update-slice_fusion
  2.2 0.3 fusion.74
  2.5 0.2 multiply_reduce_fusion
  2.7 0.5 convolution_convert_fusion.4
  3.2 0.1 collective-permute-start
  3.3 0.5 collective-permute-start.1
  3.8 0.2 multiply_reduce_fusion.1
  4.0 1.4 collective-permute-done.1
  5.4 0.1 copy.29
  5.5 0.3 collective-permute-done
  5.9 1.7 add_convert_fusion.2
  7.6 0.1 fusion.33
  7.6 23.9 %all_to_all.35 = bf16[8,16,3712]{2,1,0:T(8,128)(2,1)S(1)} all-to-all(bf16[8,16,3712]{2,1,0:T(8,128)(2,1)S(1)} %bitcast.112), channel_id=1, replica_groups=mesh['zl'=2,'x'=4,'y'=4,'zh'=2,'c'=2] {'y','zh'}, dimensions={0} | all-to-all | bytes 1900544 | tf_op jit(solution)/shard_map/all_to_all | solution.py:33
  31.6 0.1 convert_reduce_fusion
  31.7 0.1 slice_reduce_fusion
  31.8 0.1 slice_multiply_fusion
  32.0 12.6 %all_to_all.36 = bf16[8,16,1792]{2,1,0:T(8,128)(2,1)S(1)} all-to-all(bf16[8,16,1792]{2,1,0:T(8,128)(2,1)S(1)} %broadcast_in_dim.8), channel_id=1, replica_groups=mesh['zl'=2,'x'=4,'y'=4,'zh'=2,'c'=2] {'y','zh'}, dimensions={0} | all-to-all | bytes 917504 | tf_op jit(solution)/shard_map/all_to_all | solution.py:33
  44.6 0.4 fusion.31
  45.0 1.4 collective-permute-done.2
  46.4 0.4 fusion.32
  46.9 0.1 broadcast_in_dim.9
  46.9 19.2 %all_to_all.37 = bf16[8,224,256]{2,1,0:T(8,128)(2,1)S(1)} all-to-all(bf16[8,224,256]{2,1,0:T(8,128)(2,1)S(1)} %broadcast_in_dim.9), channel_id=1, replica_groups=mesh['zl'=2,'x'=4,'y'=4,'zh'=2,'c'=2] {'zl','x'}, dimensions={0} | all-to-all | bytes 1835008 | tf_op jit(solution)/shard_map/all_to_all | solution.py:33
  66.1 0.1 convert_reduce_fusion.3
  66.3 0.4 fusion.30
  66.7 0.1 broadcast_in_dim.10
  66.8 18.6 %all_to_all.38 = bf16[8,224,256]{2,1,0:T(8,128)(2,1)S(1)} all-to-all(bf16[8,224,256]{2,1,0:T(8,128)(2,1)S(1)} %broadcast_in_dim.10), channel_id=1, replica_groups=mesh['zl'=2,'x'=4,'y'=4,'zh'=2,'c'=2] {'y','zh'}, dimensions={0} | all-to-all | bytes 1835008 | tf_op jit(solution)/shard_map/all_to_all | solution.py:33
  85.4 0.7 fusion.13
  86.1 1.8 collective-permute-done.3
  87.9 1.8 add_divide_fusion
  89.7 0.7 convolution_convert_fusion.3
  90.4 0.2 collective-permute-start.4
  90.6 2.3 %collective-permute-done.4 = bf16[128,3584]{1,0:T(8,128)(2,1)S(1)} collective-permute-done((bf16[128,3584]{1,0:T(8,128)(2,1)S(1)}, bf16[128,3584]{1,0:T(8,128)(2,1)S(1)}, u32[]{:S(2)}, u32[]{:S(2)}) %collective-permute-start.4) | collective-permute-done | bytes 917536 | tf_op jit(solution)/shard_map/ppermute | solution.py:29
  93.0 0.7 add_convert_fusion.1
  93.6 1.3 reshape.87
  94.9 4.8 %all-to-all-start.4 = ((bf16[64,2,3584]{2,1,0:T(2,128)(2,1)}), bf16[64,2,3584]{2,1,0:T(2,128)(2,1)S(1)}, u32[]{:S(2)}, u32[]{:S(2)}) async-start(bf16[64,2,3584]{2,1,0:T(2,128)(2,1)} %reshape.87), calls=%async_computation.4 | async-start | bytes 1835008 | tf_op jit(solution)/shard_map/all_to_all | solution.py:33
  99.7 0.6 iota_add_fusion
  100.3 0.3 maximum_select_fusion
  100.6 0.1 copy.32
  100.7 16.8 %all-to-all-done.4 = bf16[64,2,3584]{2,1,0:T(2,128)(2,1)S(1)} async-done(((bf16[64,2,3584]{2,1,0:T(2,128)(2,1)}), bf16[64,2,3584]{2,1,0:T(2,128)(2,1)S(1)}, u32[]{:S(2)}, u32[]{:S(2)}) %all-to-all-start.4) | async-done | bytes 917536 | tf_op jit(solution)/shard_map/all_to_all | solution.py:33
  117.5 0.7 convert_reduce_fusion.2
  118.3 0.6 copy-done.18
  118.9 1.3 fusion
  120.2 0.5 broadcast_in_dim.11
  120.7 0.1 copy-done.19
  120.8 21.5 %all_to_all.39 = bf16[64,2,3584]{2,1,0:T(2,128)(2,1)} all-to-all(bf16[64,2,3584]{2,1,0:T(2,128)(2,1)S(1)} %broadcast_in_dim.11), channel_id=1, replica_groups=mesh['zl'=2,'x'=4,'y'=4,'zh'=2,'c'=2] {'zl','x','y','zh'}, dimensions={0} | all-to-all | bytes 1835008 | tf_op jit(solution)/shard_map/all_to_all | solution.py:33
  142.3 2.5 %reshape.88 = bf16[128,3584]{1,0:T(8,128)(2,1)S(1)} reshape(bf16[64,2,3584]{2,1,0:T(2,128)(2,1)} %all_to_all.39) | data formatting | bytes 1835008 | tf_op jit(solution)/shard_map/reshape | solution.py:129
  144.8 0.1 collective-permute-start.5
  144.9 2.5 %collective-permute-done.5 = bf16[128,3584]{1,0:T(8,128)(2,1)S(1)} collective-permute-done((bf16[128,3584]{1,0:T(8,128)(2,1)S(1)}, bf16[128,3584]{1,0:T(8,128)(2,1)S(1)}, u32[]{:S(2)}, u32[]{:S(2)}) %collective-permute-start.5) | collective-permute-done | bytes 917536 | tf_op jit(solution)/shard_map/ppermute | solution.py:29
  147.4 3.8 %fusion.29 = bf16[128,512]{1,0:T(8,128)(2,1)S(1)} fusion(bf16[128,3584]{1,0:T(8,128)(2,1)S(1)} %collective-permute-done.5, bf16[512,3584]{1,0:T(8,128)(2,1)} %param.16, f32[256,512]{1,0:T(8,128)} %get-tuple-element.5, pred[]{:T(512)S(6)} %eq.33), kind=kOutput, calls=%fused_computation.43 | convolution fusion | flops 470024192 | bytes 5242881 | tf_op jit(solution)/shard_map/dot_general | solution.py:25
  151.3 1.3 convolution_convert_fusion.2
  152.6 0.2 collective-permute-start.6
  152.9 1.2 convolution_convert_fusion.5
  154.1 1.3 fusion.28
  155.5 0.6 copy-done.7
  156.1 2.2 %add_convert_fusion = bf16[128,3584]{1,0:T(8,128)(2,1)} fusion(bf16[128,3584]{1,0:T(8,128)(2,1)S(1)} %collective-permute-done.6, bf16[128,512]{1,0:T(8,128)(2,1)S(1)} %fusion.28, bf16[3584,512]{1,0:T(8,128)(2,1)S(1)} %copy-done.4), kind=kOutput, calls=%fused_computation.21 | convolution fusion | flops 471138304 | bytes 5636096 | tf_op jit(solution)/shard_map/dot_general | solution.py:25
  158.3 3.1 %reshape.89 = bf16[64,2,3584]{2,1,0:T(2,128)(2,1)} reshape(bf16[128,3584]{1,0:T(8,128)(2,1)} %add_convert_fusion) | data formatting | bytes 1835008 | tf_op jit(solution)/shard_map/reshape | solution.py:139
  161.4 5.5 %all-to-all-start.6 = ((bf16[64,2,3584]{2,1,0:T(2,128)(2,1)}), bf16[64,2,3584]{2,1,0:T(2,128)(2,1)}, u32[]{:S(2)}, u32[]{:S(2)}) async-start(bf16[64,2,3584]{2,1,0:T(2,128)(2,1)} %reshape.89), calls=%async_computation.6 | async-start | bytes 1835008 | tf_op jit(solution)/shard_map/all_to_all | solution.py:33
  166.9 1.4 add_convert_fusion.3
  168.3 4.3 %convolution_convert_fusion = bf16[512,3584]{1,0:T(8,128)(2,1)} fusion(bf16[128,3584]{1,0:T(8,128)(2,1)} %copy-done.9, bf16[128,3584]{1,0:T(8,128)(2,1)S(1)} %reshape.88, bf16[128,512]{1,0:T(8,128)(2,1)} %copy-done.14, bf16[128,512]{1,0:T(8,128)(2,1)} %copy-done.15), kind=kOutput, calls=%fused_computation | convolution fusion | flops 945553408 | bytes 5767168 | tf_op jit(solution)/shard_map/dot_general | solution.py:25
  172.6 3.0 %convolution_convert_fusion.1 = bf16[3584,512]{1,0:T(8,128)(2,1)} fusion(bf16[3584,256]{1,0:T(8,128)(2,1)S(1)} %bitcast.109, bf16[128,512]{1,0:T(8,128)(2,1)S(1)} %copy-done.6, bf16[128,512]{1,0:T(8,128)(2,1)S(1)} %copy-done.8, pred[]{:T(512)S(6)} %eq.33), kind=kOutput, calls=%fused_computation.1 | convolution fusion | flops 942538752 | bytes 5767169 | tf_op jit(solution)/shard_map/dot_general | solution.py:25
  175.6 9.2 %all-to-all-done.6 = bf16[64,2,3584]{2,1,0:T(2,128)(2,1)} async-done(((bf16[64,2,3584]{2,1,0:T(2,128)(2,1)}), bf16[64,2,3584]{2,1,0:T(2,128)(2,1)}, u32[]{:S(2)}, u32[]{:S(2)}) %all-to-all-start.6) | async-done | bytes 917536 | tf_op jit(solution)/shard_map/all_to_all | solution.py:33
  184.8 1.9 %convert_reduce_fusion.1 = f32[2,3584]{1,0:T(2,128)S(1)} fusion(bf16[64,2,3584]{2,1,0:T(2,128)(2,1)} %all-to-all-done.6), kind=kLoop, calls=%fused_computation.20 | loop fusion | flops 910336 | bytes 946176 | tf_op jit(solution)/shard_map/reduce_sum | solution.py:138
  186.8 0.6 convert_subtract_fusion
  (86 shorter events, 0.4 us)
Async XLA Ops:
  0.6 44.0 %copy-start = (bf16[1792,224]{0,1:T(8,128)(2,1)S(1)}, bf16[1792,224]{0,1:T(8,128)(2,1)}, u32[]{:S(2)}) copy-start(bf16[1792,224]{0,1:T(8,128)(2,1)} %param.13) | copy-start | bytes 2408452
  0.6 1.5 copy-start.12
  0.7 1.8 copy-start.34
  0.7 65.5 %copy-start.30 = (pred[256]{0:T(512)(128)(4,1)}, pred[256]{0:T(512)(128)(4,1)S(1)}, u32[]{:S(2)}) copy-start(pred[256]{0:T(512)(128)(4,1)S(1)} %get-tuple-element.18) | copy-start | bytes 772
  0.7 65.5 %copy-start.32 = (pred[256]{0:T(512)(128)(4,1)}, pred[256]{0:T(512)(128)(4,1)S(1)}, u32[]{:S(2)}) copy-start(pred[256]{0:T(512)(128)(4,1)S(1)} %get-tuple-element.19) | copy-start | bytes 772
  0.7 65.5 %copy-start.21 = (s32[256]{0:T(256)}, s32[256]{0:T(256)S(1)}, u32[]{:S(2)}) copy-start(s32[256]{0:T(256)S(1)} %get-tuple-element.20) | copy-start | bytes 3076
  0.7 65.5 %copy-start.23 = (s32[256]{0:T(256)}, s32[256]{0:T(256)S(1)}, u32[]{:S(2)}) copy-start(s32[256]{0:T(256)S(1)} %get-tuple-element.21) | copy-start | bytes 3076
  0.7 65.5 %copy-start.25 = (s32[256]{0:T(256)}, s32[256]{0:T(256)S(1)}, u32[]{:S(2)}) copy-start(s32[256]{0:T(256)S(1)} %get-tuple-element.16) | copy-start | bytes 3076
  0.8 65.5 %copy-start.27 = (s32[256]{0:T(256)}, s32[256]{0:T(256)S(1)}, u32[]{:S(2)}) copy-start(s32[256]{0:T(256)S(1)} %get-tuple-element.17) | copy-start | bytes 3076
  0.8 1.9 %copy-start.29 = (f32[224]{0:T(256)S(1)}, f32[224]{0:T(256)}, u32[]{:S(2)}) copy-start(f32[224]{0:T(256)} %param.10) | copy-start | bytes 2692
  2.2 1.6 copy-start.35
  3.2 2.7 %collective-permute-start = (bf16[128,3584]{1,0:T(8,128)(2,1)S(1)}, bf16[128,3584]{1,0:T(8,128)(2,1)}, u32[]{:S(2)}, u32[]{:S(2)}) collective-permute-start(bf16[128,3584]{1,0:T(8,128)(2,1)S(1)} %convolution_convert_fusion.4), channel_id=1, source_target_pairs={{0,1},{1,0},{2,3},{3,2},{4,5},{5,4},{6,7},{7,6},{8,9},{9,8},{10,11... | collective-permute-start | bytes 2752520 | tf_op jit(solution)/shard_map/ppermute | solution.py:29
  3.3 2.1 %collective-permute-start.1 = (f32[128]{0:T(128)S(1)}, f32[128]{0:T(128)S(1)}, u32[]{:S(2)}, u32[]{:S(2)}) collective-permute-start(f32[128]{0:T(128)S(1)} %get-tuple-element.14), channel_id=1, source_target_pairs={{0,1},{1,0},{2,3},{3,2},{4,5},{5,4},{6,7},{7,6},{8,9},{9,8},{10,11... | collective-permute-start | bytes 1544 | tf_op jit(solution)/shard_map/ppermute | solution.py:29
  44.6 1.8 collective-permute-start.2
  46.9 19.4 %copy-start.36 = (bf16[256,224]{0,1:T(8,128)(2,1)S(1)}, bf16[256,224]{0,1:T(8,128)(2,1)}, u32[]{:S(2)}) copy-start(bf16[256,224]{0,1:T(8,128)(2,1)} %param.9) | copy-start | bytes 344068
  66.3 19.1 %copy-start.3 = (bf16[3584,512]{1,0:T(8,128)(2,1)S(1)}, bf16[3584,512]{1,0:T(8,128)(2,1)}, u32[]{:S(2)}) copy-start(bf16[3584,512]{1,0:T(8,128)(2,1)} %param.14) | copy-start | bytes 11010052
  85.4 2.5 %collective-permute-start.3 = (bf16[8,224,256]{2,1,0:T(8,128)(2,1)S(1)}, bf16[8,224,256]{2,1,0:T(8,128)(2,1)S(1)}, u32[]{:S(2)}, u32[]{:S(2)}) collective-permute-start(bf16[8,224,256]{2,1,0:T(8,128)(2,1)S(1)} %all_to_all.38), channel_id=1, source_target_pairs={{0,1},{1,0},{2,3},{3,2},{4,5},{5,4},{6,7},{7,6},{8,9},{9,8},{10,11... | collective-permute-start | bytes 2752520 | tf_op jit(solution)/shard_map/ppermute | solution.py:29
  85.4 2.5 %copy-start.37 = (f32[512]{0:T(512)S(1)}, f32[512]{0:T(512)}, u32[]{:S(2)}) copy-start(f32[512]{0:T(512)} %param.15) | copy-start | bytes 6148
  86.1 3.6 %copy-start.1 = (bf16[512,3584]{1,0:T(8,128)(2,1)S(1)}, bf16[512,3584]{1,0:T(8,128)(2,1)}, u32[]{:S(2)}) copy-start(bf16[512,3584]{1,0:T(8,128)(2,1)} %param.16) | copy-start | bytes 11010052
  87.9 1.8 copy-start.10
  89.7 0.7 copy-start.16
  89.7 0.7 copy-start.14
  89.7 3.3 %copy-start.15 = (bf16[128,512]{1,0:T(8,128)(2,1)}, bf16[128,512]{1,0:T(8,128)(2,1)S(1)}, u32[]{:S(2)}) copy-start(bf16[128,512]{1,0:T(8,128)(2,1)S(1)} %get-tuple-element.8) | copy-start | bytes 393220
  90.4 2.6 %collective-permute-start.4 = (bf16[128,3584]{1,0:T(8,128)(2,1)S(1)}, bf16[128,3584]{1,0:T(8,128)(2,1)S(1)}, u32[]{:S(2)}, u32[]{:S(2)}) collective-permute-start(bf16[128,3584]{1,0:T(8,128)(2,1)S(1)} %convolution_convert_fusion.3), channel_id=1, source_target_pairs={{0,1},{1,0},{2,3},{3,2},{4,5},{5,4},{6,7},{7,6},{8,9},{9,8},{10,11... | collective-permute-start | bytes 2752520 | tf_op jit(solution)/shard_map/ppermute | solution.py:29
  94.9 5.4 %copy-start.11 = (bf16[8,224,256]{2,1,0:T(8,128)(2,1)S(1)}, bf16[8,224,256]{2,1,0:T(8,128)(2,1)}, u32[]{:S(2)}) copy-start(bf16[8,224,256]{2,1,0:T(8,128)(2,1)} %copy-done.10) | copy-start | bytes 2752516
  94.9 22.6 %all-to-all-start.4 = ((bf16[64,2,3584]{2,1,0:T(2,128)(2,1)}), bf16[64,2,3584]{2,1,0:T(2,128)(2,1)S(1)}, u32[]{:S(2)}, u32[]{:S(2)}) async-start(bf16[64,2,3584]{2,1,0:T(2,128)(2,1)} %reshape.87), calls=%async_computation.4 | async-start | bytes 1835008 | tf_op jit(solution)/shard_map/all_to_all | solution.py:33
  118.3 0.6 copy-start.18
  120.2 0.6 copy-start.19
  144.8 2.6 %collective-permute-start.5 = (bf16[128,3584]{1,0:T(8,128)(2,1)S(1)}, bf16[128,3584]{1,0:T(8,128)(2,1)S(1)}, u32[]{:S(2)}, u32[]{:S(2)}) collective-permute-start(bf16[128,3584]{1,0:T(8,128)(2,1)S(1)} %reshape.88), channel_id=1, source_target_pairs={{0,1},{1,0},{2,3},{3,2},{4,5},{5,4},{6,7},{7,6},{8,9},{9,8},{10,11... | collective-permute-start | bytes 2752520 | tf_op jit(solution)/shard_map/ppermute | solution.py:29
  147.3 3.8 %copy-start.9 = (bf16[128,3584]{1,0:T(8,128)(2,1)}, bf16[128,3584]{1,0:T(8,128)(2,1)S(1)}, u32[]{:S(2)}) copy-start(bf16[128,3584]{1,0:T(8,128)(2,1)S(1)} %collective-permute-done.5) | copy-start | bytes 2752516
  147.4 3.8 %copy-start.4 = (bf16[3584,512]{1,0:T(8,128)(2,1)S(1)}, bf16[3584,512]{1,0:T(8,128)(2,1)}, u32[]{:S(2)}) copy-start(bf16[3584,512]{1,0:T(8,128)(2,1)} %param.14) | copy-start | bytes 11010052
  151.2 1.4 copy-start.5
  151.2 1.7 copy-start.17
  151.2 1.7 copy-start.22
  151.2 1.6 copy-start.24
  151.2 1.6 copy-start.26
  151.2 1.6 copy-start.28
  151.3 1.6 copy-start.31
  151.3 1.6 copy-start.33
  151.3 2.9 %copy-start.2 = (bf16[512,3584]{1,0:T(8,128)(2,1)S(1)}, bf16[512,3584]{1,0:T(8,128)(2,1)}, u32[]{:S(2)}) copy-start(bf16[512,3584]{1,0:T(8,128)(2,1)} %param.16) | copy-start | bytes 11010052
  152.6 1.5 copy-start.13
  152.6 2.8 %collective-permute-start.6 = (bf16[128,3584]{1,0:T(8,128)(2,1)S(1)}, bf16[128,3584]{1,0:T(8,128)(2,1)S(1)}, u32[]{:S(2)}, u32[]{:S(2)}) collective-permute-start(bf16[128,3584]{1,0:T(8,128)(2,1)S(1)} %convolution_convert_fusion.2), channel_id=1, source_target_pairs={{0,1},{1,0},{2,3},{3,2},{4,5},{5,4},{6,7},{7,6},{8,9},{9,8},{10,11... | collective-permute-start | bytes 2752520 | tf_op jit(solution)/shard_map/ppermute | solution.py:29
  155.4 0.6 copy-start.7
  161.4 23.4 %all-to-all-start.6 = ((bf16[64,2,3584]{2,1,0:T(2,128)(2,1)}), bf16[64,2,3584]{2,1,0:T(2,128)(2,1)}, u32[]{:S(2)}, u32[]{:S(2)}) async-start(bf16[64,2,3584]{2,1,0:T(2,128)(2,1)} %reshape.89), calls=%async_computation.6 | async-start | bytes 1835008 | tf_op jit(solution)/shard_map/all_to_all | solution.py:33
  168.3 4.3 %copy-start.6 = (bf16[128,512]{1,0:T(8,128)(2,1)S(1)}, bf16[128,512]{1,0:T(8,128)(2,1)}, u32[]{:S(2)}) copy-start(bf16[128,512]{1,0:T(8,128)(2,1)} %copy-done.5) | copy-start | bytes 393220
  168.3 4.3 %copy-start.8 = (bf16[128,512]{1,0:T(8,128)(2,1)S(1)}, bf16[128,512]{1,0:T(8,128)(2,1)}, u32[]{:S(2)}) copy-start(bf16[128,512]{1,0:T(8,128)(2,1)} %copy-done.7) | copy-start | bytes 393220
  172.6 14.2 %copy-start.20 = (bf16[2,3584]{1,0:T(2,128)(2,1)S(1)}, bf16[2,3584]{1,0:T(2,128)(2,1)}, u32[]{:S(2)}) copy-start(bf16[2,3584]{1,0:T(2,128)(2,1)} %copy-done.19) | copy-start | bytes 43012

commit v3 on v1

v3 whole, which is shorter than its diff:
```python
import jax
import jax.numpy as jnp
from jax import lax
from jax.sharding import Mesh
from jax.sharding import PartitionSpec as P

D = 3584
ROWS = 256
HALF = D // 2
CHIPS = 64

MP = ("zl", "x")
RING = ("y", "zh")
FEAT = RING + ("c",)
CHIP = MP + RING
ALL = MP + FEAT

sparsity_weight = 0.2
norm_eps = 1e-06
bf16 = jnp.bfloat16
f32 = jnp.float32


def dot(a, b, ca, cb):
    return lax.dot_general(a, b, (((ca,), (cb,)), ((), ())), preferred_element_type=f32)


def swap(v):
    return lax.ppermute(v, "c", [(0, 1), (1, 0)])


def exchange(v, axes):
    return lax.all_to_all(v, axes, 0, 0, tiled=True)


def copies_to(v, axes, parts):
    return exchange(jnp.broadcast_to(v[None], (parts,) + v.shape), axes)


def halves(v, core, axis):
    size = v.shape[axis] // 2
    return (
        lax.dynamic_slice_in_dim(v, core * size, size, axis),
        lax.dynamic_slice_in_dim(v, (1 - core) * size, size, axis),
    )


def shards(
    residual_in,
    norm_gain,
    gate_weight,
    up_weight,
    down_weight,
    encoder_weight,
    encoder_bias,
    decoder_weight,
    decoder_bias,
):
    core = lax.axis_index("c")
    chip = lax.axis_index(CHIP)

    def joined(kept, other, axis):
        return jnp.where(
            core == 0,
            jnp.concatenate([kept, other], axis=axis),
            jnp.concatenate([other, kept], axis=axis),
        )

    source = residual_in.astype(f32)
    scaled = (source * norm_gain[None, :]).astype(bf16)
    gate_kept, gate_other = halves(gate_weight, core, 1)
    up_kept, up_other = halves(up_weight, core, 1)
    hidden_half = gate_kept.shape[1]
    squared = source * source
    high = squared.astype(bf16)
    low = (squared - high.astype(f32)).astype(bf16)
    ones = jnp.ones((source.shape[1], 128), bf16)
    squares = dot(high, ones, 1, 0) + dot(low, ones, 1, 0)

    sent = jnp.concatenate([dot(scaled, gate_other, 1, 0), dot(scaled, up_other, 1, 0)], axis=1)
    arrived, squares_arrived = swap(sent.astype(bf16)), swap(squares)
    both = jnp.concatenate([dot(scaled, gate_kept, 1, 0), dot(scaled, up_kept, 1, 0)], axis=1)
    both = (both + arrived.astype(f32)).astype(bf16)
    squares = squares + squares_arrived
    first = squares.astype(bf16)
    second = (squares - first.astype(f32)).astype(bf16)
    third = (squares - first.astype(f32) - second.astype(f32)).astype(bf16)
    lane = lax.broadcasted_iota(jnp.int32, squares.shape, 1)
    parts = jnp.where(lane == 0, first, jnp.where(lane == 1, second, jnp.where(lane == 2, third, 0)))
    both = jnp.concatenate([both, parts.astype(bf16)], axis=1)
    both = exchange(both.reshape(8, 32, both.shape[1]), RING)
    projected = jnp.sum(both.astype(f32), axis=0)
    mean = jnp.sum(projected[:, 2 * hidden_half :], axis=1, keepdims=True) / D
    projected = projected[:, : 2 * hidden_half] * lax.rsqrt(mean + norm_eps)
    hidden = (jax.nn.silu(projected[:, :hidden_half]) * projected[:, hidden_half:]).astype(bf16)

    hidden_kept = copies_to(hidden, RING, 8).reshape(ROWS, hidden_half)
    hidden_other = swap(hidden_kept)
    down_kept, down_other = halves(down_weight, core, 0)
    mixed = (dot(down_kept, hidden_kept, 0, 1) + dot(down_other, hidden_other, 0, 1)).astype(bf16)
    mixed = jnp.sum(copies_to(mixed, MP, 8).astype(f32), axis=0)
    stream_cols = (source.T + mixed).astype(bf16)

    blocks_kept = copies_to(stream_cols, RING, 8)
    blocks_other = swap(blocks_kept)
    encoder_blocks = encoder_weight.reshape(8, 2, D // 16, -1)
    encoder_kept = jnp.where(core == 0, encoder_blocks[:, 0], encoder_blocks[:, 1]).reshape(HALF, -1)
    encoder_other = jnp.where(core == 0, encoder_blocks[:, 1], encoder_blocks[:, 0]).reshape(HALF, -1)
    encoded = (
        dot(blocks_kept.reshape(HALF, ROWS), encoder_kept, 0, 0)
        + dot(blocks_other.reshape(HALF, ROWS), encoder_other, 0, 0)
        + encoder_bias[None, :]
    )
    codes = jax.nn.softplus(encoded).astype(bf16)

    decoder_kept, decoder_other = halves(decoder_weight, core, 1)
    arrived = swap(dot(codes, decoder_other, 1, 0).astype(bf16))
    both = (dot(codes, decoder_kept, 1, 0) + arrived.astype(f32)).astype(bf16)
    recon = jnp.sum(exchange(both.reshape(CHIPS, 4, HALF), CHIP).astype(f32), axis=0)
    recon = recon + halves(decoder_bias, core, 0)[0][None, :]

    stream = jnp.where(
        core == 0,
        jnp.stack([blocks_kept, blocks_other], axis=1),
        jnp.stack([blocks_other, blocks_kept], axis=1),
    ).reshape(D, ROWS)
    own = chip * 4 + lax.broadcasted_iota(jnp.int32, (4, ROWS), 0)
    own = (lax.broadcasted_iota(jnp.int32, (4, ROWS), 1) == own).astype(bf16)
    stream_own = dot(own, halves(stream, core, 0)[0], 1, 1)

    error = (recon - stream_own).astype(bf16)
    error_kept = copies_to(error, CHIP, CHIPS).reshape(ROWS, HALF)
    error_other = swap(error_kept)
    code_gradient = dot(error_kept, decoder_kept, 1, 1) + dot(error_other, decoder_other, 1, 1)
    encoded_gradient = (jax.nn.sigmoid(encoded) * (code_gradient + sparsity_weight)).astype(bf16)

    top_kept, top_other = halves(encoder_weight, core, 0)
    arrived = swap(dot(encoded_gradient, top_other, 1, 1).astype(bf16))
    both = (dot(encoded_gradient, top_kept, 1, 1) + arrived.astype(f32)).astype(bf16)
    terms = exchange(both.reshape(CHIPS, 4, HALF), CHIP)
    decoder_gradient = dot(codes, joined(error_kept, error_other, 1), 0, 0).astype(bf16)
    encoder_gradient = dot(stream, encoded_gradient, 1, 0).astype(bf16)
    terms, decoder_gradient, encoder_gradient = lax.optimization_barrier(
        (terms, decoder_gradient, encoder_gradient)
    )
    input_gradient = jnp.sum(terms.astype(f32), axis=0) - error.astype(f32)

    def own_rows(v):
        mine, others = halves(v, core, 0)
        return joined(mine, swap(others), 1)

    return codes, own_rows(recon.astype(bf16)), encoder_gradient, decoder_gradient, own_rows(input_gradient)


def solution(mesh):
    fine = Mesh(mesh.devices.reshape(2, 4, 4, 2, 2), ("zl", "x", "y", "zh", "c"))
    in_specs = (
        P(None, FEAT),
        P(FEAT),
        P(FEAT, MP),
        P(FEAT, MP),
        P(MP, FEAT),
        P(None, ALL),
        P(ALL),
        P(ALL, None),
        P(),
    )
    out_specs = (P(None, ALL), P(ALL, None), P(None, ALL), P(ALL, None), P(ALL, None))
    return jax.shard_map(shards, mesh=fine, in_specs=in_specs, out_specs=out_specs, check_vma=False)
```

time: 187 us -> 189 us (1.011)
  blocking collectives: 118 us -> 95.7 us
  matrix products: 20.5 us -> 31.8 us
  waiting for transfers between devices: 22.8 us -> 28.8 us
  starting transfers between devices: 6.46 us -> 11.5 us
    all_to_all x6 -> x5, blocking collectives: 118 us -> 95.7 us  [exchange(): return lax.all_to_all(v, axes, 0, 0, tiled=True)]
    all_to_all x1 -> x2, waiting for transfers between devices: 8.76 us -> 23.9 us  [exchange(): return lax.all_to_all(v, axes, 0, 0, tiled=True)]
    dot_general x10 -> x19, matrix products: 20.5 us -> 31.8 us  [dot(): lax.dot_general(a, b, (((ca,), (cb,)), ((), ())), preferred_element_type=...]
    ppermute x8 -> x9, waiting for transfers between devices: 14 us -> 4.86 us  [swap(): return lax.ppermute(v, 'c', [(0, 1), (1, 0)])]
    all_to_all x1 -> x2, starting transfers between devices: 5.07 us -> 9.81 us  [exchange(): return lax.all_to_all(v, axes, 0, 0, tiled=True)]
    select_n x1 -> x4, other arithmetic: 0.02 us -> 3.33 us  [the longest x2 2.03 us: joined(): jnp.where(core == 0, jnp.concatenate([kept, other], axis=axis), jnp.conca...]
    dynamic_slice x0 -> x3, local copies, waits for them, and re-layouts: none -> 2.81 us  [halves(): lax.dynamic_slice_in_dim(v, core * size, size, axis)]
    reshape x4 -> x3, local copies, waits for them, and re-layouts: 5.37 us -> 3.44 us  [the longest x1 1.17 us: shards(): terms = exchange(both.reshape(CHIPS, 4, HALF), CHIP)]
  transfers between devices with their start and end apart: 9 -> 11, of which waited for: 8 -> 6; matrix products, arithmetic and copies ran while one was open for 6% -> 14% of each run, Pallas kernels for 0% -> 0%
where the time goes in v3:
time: 189 us; the launch traced here: 187 us
  blocking collectives  95.7 us (51%)
  matrix products  31.8 us (17%)
  waiting for transfers between devices  28.8 us (15%)
  starting transfers between devices  11.5 us (6%)
  local copies, waits for them, and re-layouts  10.3 us (5%)
  other arithmetic  7.59 us (4%)
    all_to_all x5, blocking collectives, exchange(): return lax.all_to_all(v, axes, 0, 0, tiled=True)  95.7 us
    dot_general x19, matrix products, dot(): lax.dot_general(a, b, (((ca,), (cb,)), ((), ())), preferred_element_type=...  31.8 us
    all_to_all x2, waiting for transfers between devices, exchange(): return lax.all_to_all(v, axes, 0, 0, tiled=True)  23.9 us
    all_to_all x2, starting transfers between devices, exchange(): return lax.all_to_all(v, axes, 0, 0, tiled=True)  9.81 us
    ppermute x9, waiting for transfers between devices, swap(): return lax.ppermute(v, 'c', [(0, 1), (1, 0)])  4.86 us
  transfers between devices with their start and end apart: 11, of which 6 were waited for; matrix products, arithmetic and copies ran while one was open for 14% of the time, Pallas kernels for 0%

profile of v3, /device:TPU:0, one launch (start us, length us, event | category | flops | bytes accessed | tf_op | source)
XLA Modules:
  0.0 186.7 jit_solution(3420802983170183424)
XLA Ops:
  0.7 1.1 copy-done
  1.8 1.4 convolution_convert_fusion.4
  3.2 1.5 convolution_convert_fusion.5
  4.7 0.1 collective-permute-start
  4.8 0.2 fusion.75
  5.1 0.9 convolution_add_fusion.1
  6.0 0.5 collective-permute-start.1
  6.4 1.1 fusion.60
  7.5 1.1 fusion.62
  8.7 1.0 convert_select_fusion
  9.7 0.2 fusion.1
  9.9 24.1 %all_to_all.35 = bf16[8,32,1920]{2,1,0:T(8,128)(2,1)S(1)} all-to-all(bf16[8,32,1920]{2,1,0:T(8,128)(2,1)S(1)} %bitcast.87), channel_id=1, replica_groups=mesh['zl'=2,'x'=4,'y'=4,'zh'=2,'c'=2] {'y','zh'}, dimensions={0} | all-to-all | bytes 1966080 | tf_op jit(solution)/shard_map/all_to_all | solution.py:33
  34.0 0.1 convert_reduce_fusion
  34.2 0.1 slice_reduce_fusion
  34.3 0.1 slice_multiply_fusion
  34.5 12.7 %all_to_all.36 = bf16[8,32,896]{2,1,0:T(8,128)(2,1)S(1)} all-to-all(bf16[8,32,896]{2,1,0:T(8,128)(2,1)S(1)} %broadcast_in_dim.16), channel_id=1, replica_groups=mesh['zl'=2,'x'=4,'y'=4,'zh'=2,'c'=2] {'y','zh'}, dimensions={0} | all-to-all | bytes 917504 | tf_op jit(solution)/shard_map/all_to_all | solution.py:33
  47.2 0.3 fusion.64
  47.5 1.5 collective-permute-done.2
  49.0 0.3 fusion.54
  49.4 19.1 %all_to_all.37 = bf16[8,224,256]{2,1,0:T(8,128)(2,1)S(1)} all-to-all(bf16[8,224,256]{2,1,0:T(8,128)(2,1)S(1)} %broadcast_in_dim.17), channel_id=1, replica_groups=mesh['zl'=2,'x'=4,'y'=4,'zh'=2,'c'=2] {'zl','x'}, dimensions={0} | all-to-all | bytes 1835008 | tf_op jit(solution)/shard_map/all_to_all | solution.py:33
  68.6 0.1 convert_reduce_fusion.3
  68.8 18.3 %all_to_all.38 = bf16[8,224,256]{2,1,0:T(8,128)(2,1)S(1)} all-to-all(bf16[8,224,256]{2,1,0:T(8,128)(2,1)S(1)} %broadcast_in_dim.18), channel_id=1, replica_groups=mesh['zl'=2,'x'=4,'y'=4,'zh'=2,'c'=2] {'y','zh'}, dimensions={0} | all-to-all | bytes 1835008 | tf_op jit(solution)/shard_map/all_to_all | solution.py:33
  87.1 2.9 %fusion.39 = f32[256,512]{1,0:T(8,128)S(1)} fusion(bf16[8,224,256]{2,1,0:T(8,128)(2,1)S(1)} %all_to_all.38, pred[]{:T(512)S(6)} %eq.38, bf16[8,2,224,512]{3,2,1,0:T(8,128)(2,1)} %bitcast.88), kind=kOutput, calls=%fused_computation.48 | convolution fusion | flops 470679552 | bytes 5111809 | tf_op jit(solution)/shard_map/dot_general | solution.py:25
  90.0 0.2 copy-done.3
  90.3 1.8 fusion.56
  92.0 0.6 copy-done.1
  92.6 0.6 convolution_convert_fusion.3
  93.3 0.6 collective-permute-start.4
  93.9 2.2 %collective-permute-done.4 = bf16[256,1792]{1,0:T(8,128)(2,1)} collective-permute-done((bf16[256,1792]{1,0:T(8,128)(2,1)S(1)}, bf16[256,1792]{1,0:T(8,128)(2,1)}, u32[]{:S(2)}, u32[]{:S(2)}) %collective-permute-start.4) | collective-permute-done | bytes 917536 | tf_op jit(solution)/shard_map/ppermute | solution.py:29
  96.1 2.4 %add_convert_fusion.1 = bf16[256,1792]{1,0:T(8,128)(2,1)S(1)} fusion(bf16[256,1792]{1,0:T(8,128)(2,1)} %collective-permute-done.4, bf16[256,512]{1,0:T(8,128)(2,1)S(1)} %get-tuple-element.15, bf16[512,3584]{1,0:T(8,128)(2,1)} %param.16, s32[]{:T(128)S(6)} %select_n.107), kind=kOutput, calls=%fused_computation.28 | convolution fusion | flops 471138304 | bytes 3932164 | tf_op jit(solution)/shard_map/dot_general | solution.py:25
  98.5 1.1 reshape.59
  99.6 4.8 %all-to-all-start.4 = ((bf16[64,4,1792]{2,1,0:T(4,128)(2,1)}), bf16[64,4,1792]{2,1,0:T(4,128)(2,1)S(1)}, u32[]{:S(2)}, u32[]{:S(2)}) async-start(bf16[64,4,1792]{2,1,0:T(4,128)(2,1)} %reshape.59), calls=%async_computation.4 | async-start | bytes 1835008 | tf_op jit(solution)/shard_map/all_to_all | solution.py:33
  104.4 1.4 dynamic_slice.56
  105.8 0.5 iota_add_fusion
  106.3 0.3 maximum_select_fusion
  106.6 0.1 copy.27
  106.8 15.7 %all-to-all-done.4 = bf16[64,4,1792]{2,1,0:T(4,128)(2,1)S(1)} async-done(((bf16[64,4,1792]{2,1,0:T(4,128)(2,1)}), bf16[64,4,1792]{2,1,0:T(4,128)(2,1)S(1)}, u32[]{:S(2)}, u32[]{:S(2)}) %all-to-all-start.4) | async-done | bytes 917536 | tf_op jit(solution)/shard_map/all_to_all | solution.py:33
  122.5 0.4 convert_reduce_fusion.2
  122.9 0.6 copy-done.12
  123.5 1.1 fusion
  124.6 0.6 copy-done.13
  125.2 0.2 broadcast_in_dim.19
  125.4 21.4 %all_to_all.39 = bf16[64,4,1792]{2,1,0:T(4,128)(2,1)S(1)} all-to-all(bf16[64,4,1792]{2,1,0:T(4,128)(2,1)S(1)} %broadcast_in_dim.19), channel_id=1, replica_groups=mesh['zl'=2,'x'=4,'y'=4,'zh'=2,'c'=2] {'zl','x','y','zh'}, dimensions={0} | all-to-all | bytes 1835008 | tf_op jit(solution)/shard_map/all_to_all | solution.py:33
  146.9 1.1 reshape.60
  148.0 2.5 %fusion.24 = f32[256,512]{1,0:T(8,128)S(1)} fusion(bf16[256,1792]{1,0:T(8,128)(2,1)} %reshape.60, bf16[512,3584]{1,0:T(8,128)(2,1)} %param.16, s32[]{:T(128)S(6)} %select_n.107), kind=kOutput, calls=%fused_computation.38 | convolution fusion | flops 469762048 | bytes 3276804 | tf_op jit(solution)/shard_map/dot_general | solution.py:25
  150.5 0.2 collective-permute-done.6
  150.7 2.6 %fusion.51 = bf16[256,512]{1,0:T(8,128)(2,1)S(1)} fusion(f32[256,512]{1,0:T(8,128)S(1)} %fusion.24, bf16[256,1792]{1,0:T(8,128)(2,1)S(1)} %collective-permute-done.6, bf16[512,3584]{1,0:T(8,128)(2,1)} %param.16, s32[]{:T(128)S(6)} %select_n.108, f32[256,512]{1,0:T(8,128)S(1)} %copy-done.16), kind=kOutput, calls=%fused_computation.52 | convolution fusion | flops 470679552 | bytes 4063236 | tf_op jit(solution)/shard_map/dot_general | solution.py:25
  153.3 0.3 copy-done.4
  153.6 0.7 convolution_convert_fusion.2
  154.3 0.4 collective-permute-start.7
  154.7 1.4 add_convert_fusion.2
  156.1 1.0 collective-permute-done.7
  157.0 2.5 %add_convert_fusion = bf16[256,1792]{1,0:T(8,128)(2,1)S(1)} fusion(bf16[256,1792]{1,0:T(8,128)(2,1)} %collective-permute-done.7, bf16[256,512]{1,0:T(8,128)(2,1)} %copy-done.5, bf16[3584,512]{1,0:T(8,128)(2,1)} %param.14, s32[]{:T(128)S(6)} %select_n.107), kind=kOutput, calls=%fused_computation.23 | convolution fusion | flops 471138304 | bytes 3932164 | tf_op jit(solution)/shard_map/dot_general | solution.py:25
  159.5 1.2 reshape.61
  160.7 5.0 %all-to-all-start.6 = ((bf16[64,4,1792]{2,1,0:T(4,128)(2,1)}), bf16[64,4,1792]{2,1,0:T(4,128)(2,1)S(1)}, u32[]{:S(2)}, u32[]{:S(2)}) async-start(bf16[64,4,1792]{2,1,0:T(4,128)(2,1)} %reshape.61), calls=%async_computation.6 | async-start | bytes 1835008 | tf_op jit(solution)/shard_map/all_to_all | solution.py:33
  165.7 1.4 constant_dynamic-slice_fusion.3
  167.2 5.1 %convolution_convert_fusion.1 = bf16[512,3584]{1,0:T(8,128)(2,1)} fusion(bf16[256,512]{1,0:T(8,128)(2,1)} %copy-done.7, bf16[256,1792]{1,0:T(8,128)(2,1)} %copy-done.14, bf16[256,1792]{1,0:T(8,128)(2,1)} %reshape.60, pred[]{:T(512)S(6)} %eq.38), kind=kOutput, calls=%fused_computation.1 | convolution fusion | flops 949616640 | bytes 5767169 | tf_op jit(solution)/shard_map/dot_general | solution.py:25
  172.3 3.0 %convolution_convert_fusion = bf16[3584,512]{1,0:T(8,128)(2,1)} fusion(bf16[3584,256]{1,0:T(8,128)(2,1)S(1)} %bitcast.86, bf16[256,512]{1,0:T(8,128)(2,1)S(1)} %copy-done.6), kind=kOutput, calls=%fused_computation | convolution fusion | flops 941359104 | bytes 5767168 | tf_op jit(solution)/shard_map/dot_general | solution.py:25
  175.3 8.2 %all-to-all-done.6 = bf16[64,4,1792]{2,1,0:T(4,128)(2,1)S(1)} async-done(((bf16[64,4,1792]{2,1,0:T(4,128)(2,1)}), bf16[64,4,1792]{2,1,0:T(4,128)(2,1)S(1)}, u32[]{:S(2)}, u32[]{:S(2)}) %all-to-all-start.6) | async-done | bytes 917536 | tf_op jit(solution)/shard_map/all_to_all | solution.py:33
  183.4 0.4 convert_reduce_fusion.1
  183.8 0.7 convert_subtract_fusion.1
  184.6 0.1 collective-permute-start.8
  184.7 1.4 broadcast_select_fusion
  186.1 0.6 maximum_select_fusion.3
  (48 shorter events, 0.5 us)
Async XLA Ops:
  0.6 1.1 copy-start
  1.8 3.1 %copy-start.2 = (bf16[256,224]{0,1:T(8,128)(2,1)S(1)}, bf16[256,224]{0,1:T(8,128)(2,1)}, u32[]{:S(2)}) copy-start(bf16[256,224]{0,1:T(8,128)(2,1)} %param.9) | copy-start | bytes 344068
  4.6 2.9 %copy-start.10 = (bf16[224,1792]{1,0:T(8,128)(2,1)S(1)}, bf16[224,1792]{1,0:T(8,128)(2,1)}, u32[]{:S(2)}) copy-start(bf16[224,1792]{1,0:T(8,128)(2,1)} %param.11) | copy-start | bytes 2408452
  4.7 4.9 %collective-permute-start = (bf16[256,1792]{1,0:T(8,128)(2,1)S(1)}, bf16[256,1792]{1,0:T(8,128)(2,1)S(1)}, u32[]{:S(2)}, u32[]{:S(2)}) collective-permute-start(bf16[256,1792]{1,0:T(8,128)(2,1)S(1)} %pad_maximum_fusion.1), channel_id=1, source_target_pairs={{0,1},{1,0},{2,3},{3,2},{4,5},{5,4},{6,7},{7,6},{8,9},{9,8},{10,11... | collective-permute-start | bytes 2752520 | tf_op jit(solution)/shard_map/ppermute | solution.py:29
  6.0 2.7 %collective-permute-start.1 = (f32[256,128]{1,0:T(8,128)}, f32[256,128]{1,0:T(8,128)}, u32[]{:S(2)}, u32[]{:S(2)}) collective-permute-start(f32[256,128]{1,0:T(8,128)} %convolution_add_fusion.1), channel_id=1, source_target_pairs={{0,1},{1,0},{2,3},{3,2},{4,5},{5,4},{6,7},{7,6},{8,9},{9,8},{10,11... | collective-permute-start | bytes 393224 | tf_op jit(solution)/shard_map/ppermute | solution.py:29
  34.0 13.2 %copy-start.11 = (bf16[1792,224]{0,1:T(8,128)(2,1)S(1)}, bf16[1792,224]{0,1:T(8,128)(2,1)}, u32[]{:S(2)}) copy-start(bf16[1792,224]{0,1:T(8,128)(2,1)} %param.13) | copy-start | bytes 2408452
  47.2 1.8 collective-permute-start.2
  87.1 2.9 %collective-permute-start.3 = (bf16[8,224,256]{2,1,0:T(8,128)(2,1)S(1)}, bf16[8,224,256]{2,1,0:T(8,128)(2,1)S(1)}, u32[]{:S(2)}, u32[]{:S(2)}) collective-permute-start(bf16[8,224,256]{2,1,0:T(8,128)(2,1)S(1)} %all_to_all.38), channel_id=1, source_target_pairs={{0,1},{1,0},{2,3},{3,2},{4,5},{5,4},{6,7},{7,6},{8,9},{9,8},{10,11... | collective-permute-start | bytes 2752520 | tf_op jit(solution)/shard_map/ppermute | solution.py:29
  87.1 3.1 %copy-start.3 = (bf16[3584,512]{1,0:T(8,128)(2,1)S(1)}, bf16[3584,512]{1,0:T(8,128)(2,1)}, u32[]{:S(2)}) copy-start(bf16[3584,512]{1,0:T(8,128)(2,1)} %param.14) | copy-start | bytes 11010052
  87.1 3.1 %copy-start.15 = (f32[512]{0:T(512)S(1)}, f32[512]{0:T(512)}, u32[]{:S(2)}) copy-start(f32[512]{0:T(512)} %param.15) | copy-start | bytes 6148
  90.0 2.6 %copy-start.1 = (bf16[512,3584]{1,0:T(8,128)(2,1)S(1)}, bf16[512,3584]{1,0:T(8,128)(2,1)}, u32[]{:S(2)}) copy-start(bf16[512,3584]{1,0:T(8,128)(2,1)} %param.16) | copy-start | bytes 11010052
  90.3 1.8 copy-start.8
  92.0 6.5 %copy-start.7 = (bf16[256,512]{1,0:T(8,128)(2,1)}, bf16[256,512]{1,0:T(8,128)(2,1)S(1)}, u32[]{:S(2)}) copy-start(bf16[256,512]{1,0:T(8,128)(2,1)S(1)} %get-tuple-element.15) | copy-start | bytes 786436
  93.3 2.8 %collective-permute-start.4 = (bf16[256,1792]{1,0:T(8,128)(2,1)S(1)}, bf16[256,1792]{1,0:T(8,128)(2,1)}, u32[]{:S(2)}, u32[]{:S(2)}) collective-permute-start(bf16[256,1792]{1,0:T(8,128)(2,1)S(1)} %convolution_convert_fusion.3), channel_id=1, source_target_pairs={{0,1},{1,0},{2,3},{3,2},{4,5},{5,4},{6,7},{7,6},{8,9},{9,8},{10,11... | collective-permute-start | bytes 2752520 | tf_op jit(solution)/shard_map/ppermute | solution.py:29
  99.6 6.7 %copy-start.9 = (bf16[8,224,256]{2,1,0:T(8,128)(2,1)S(1)}, bf16[8,224,256]{2,1,0:T(8,128)(2,1)}, u32[]{:S(2)}) copy-start(bf16[8,224,256]{2,1,0:T(8,128)(2,1)} %copy-done.8) | copy-start | bytes 2752516
  99.6 22.8 %all-to-all-start.4 = ((bf16[64,4,1792]{2,1,0:T(4,128)(2,1)}), bf16[64,4,1792]{2,1,0:T(4,128)(2,1)S(1)}, u32[]{:S(2)}, u32[]{:S(2)}) async-start(bf16[64,4,1792]{2,1,0:T(4,128)(2,1)} %reshape.59), calls=%async_computation.4 | async-start | bytes 1835008 | tf_op jit(solution)/shard_map/all_to_all | solution.py:33
  122.9 0.6 copy-start.12
  124.6 0.6 copy-start.13
  148.0 2.7 %copy-start.16 = (f32[256,512]{1,0:T(8,128)S(1)}, f32[256,512]{1,0:T(8,128)}, u32[]{:S(2)}) copy-start(f32[256,512]{1,0:T(8,128)} %get-tuple-element.16) | copy-start | bytes 1572868
  148.0 2.7 %collective-permute-start.6 = (bf16[256,1792]{1,0:T(8,128)(2,1)}, bf16[256,1792]{1,0:T(8,128)(2,1)S(1)}, u32[]{:S(2)}, u32[]{:S(2)}) collective-permute-start(bf16[256,1792]{1,0:T(8,128)(2,1)} %reshape.60), channel_id=1, source_target_pairs={{0,1},{1,0},{2,3},{3,2},{4,5},{5,4},{6,7},{7,6},{8,9},{9,8},{10,11... | collective-permute-start | bytes 2752520 | tf_op jit(solution)/shard_map/ppermute | solution.py:29
  150.7 2.6 %copy-start.14 = (bf16[256,1792]{1,0:T(8,128)(2,1)}, bf16[256,1792]{1,0:T(8,128)(2,1)S(1)}, u32[]{:S(2)}) copy-start(bf16[256,1792]{1,0:T(8,128)(2,1)S(1)} %collective-permute-done.6) | copy-start | bytes 2752516
  150.7 2.9 %copy-start.4 = (bf16[3584,512]{1,0:T(8,128)(2,1)S(1)}, bf16[3584,512]{1,0:T(8,128)(2,1)}, u32[]{:S(2)}) copy-start(bf16[3584,512]{1,0:T(8,128)(2,1)} %param.14) | copy-start | bytes 11010052
  153.6 0.7 copy-start.5
  154.3 2.7 %collective-permute-start.7 = (bf16[256,1792]{1,0:T(8,128)(2,1)S(1)}, bf16[256,1792]{1,0:T(8,128)(2,1)}, u32[]{:S(2)}, u32[]{:S(2)}) collective-permute-start(bf16[256,1792]{1,0:T(8,128)(2,1)S(1)} %convolution_convert_fusion.2), channel_id=1, source_target_pairs={{0,1},{1,0},{2,3},{3,2},{4,5},{5,4},{6,7},{7,6},{8,9},{9,8},{10,11... | collective-permute-start | bytes 2752520 | tf_op jit(solution)/shard_map/ppermute | solution.py:29
  160.7 22.8 %all-to-all-start.6 = ((bf16[64,4,1792]{2,1,0:T(4,128)(2,1)}), bf16[64,4,1792]{2,1,0:T(4,128)(2,1)S(1)}, u32[]{:S(2)}, u32[]{:S(2)}) async-start(bf16[64,4,1792]{2,1,0:T(4,128)(2,1)} %reshape.61), calls=%async_computation.6 | async-start | bytes 1835008 | tf_op jit(solution)/shard_map/all_to_all | solution.py:33
  167.1 5.2 %copy-start.6 = (bf16[256,512]{1,0:T(8,128)(2,1)S(1)}, bf16[256,512]{1,0:T(8,128)(2,1)}, u32[]{:S(2)}) copy-start(bf16[256,512]{1,0:T(8,128)(2,1)} %copy-done.5) | copy-start | bytes 786436
  167.1 17.5 %collective-permute-start.5 = (bf16[2,1792]{1,0:T(2,128)(2,1)}, bf16[2,1792]{1,0:T(2,128)(2,1)}, u32[]{:S(2)}, u32[]{:S(2)}) collective-permute-start(bf16[2,1792]{1,0:T(2,128)(2,1)} %get-tuple-element.14), channel_id=1, source_target_pairs={{0,1},{1,0},{2,3},{3,2},{4,5},{5,4},{6,7},{7,6},{8,9},{9,8},{10,11... | collective-permute-start | bytes 21512 | tf_op jit(solution)/shard_map/ppermute | solution.py:29
  184.6 1.5 collective-permute-start.8

commit v4 on v2

--- a/solution.py
+++ b/solution.py
@@ -113,8 +113,7 @@
 
     arrived = swap(dot(codes_other, decoder_weight, 1, 0).astype(bf16))
     both = (dot(codes_kept, decoder_weight, 1, 0) + arrived.astype(f32)).astype(bf16)
-    recon_own = jnp.sum(exchange(both.reshape(CHIPS, 2, D), CHIP).astype(f32), axis=0) + decoder_bias[None, :]
-
+    terms = exchange(both.reshape(CHIPS, 2, D), CHIP)
     stream = by_core(
         jnp.stack([blocks_kept, blocks_other], axis=1),
         jnp.stack([blocks_other, blocks_kept], axis=1),
@@ -122,34 +121,30 @@
     chip = lax.axis_index(CHIP)
     own = core * HALF + chip * 2 + lax.broadcasted_iota(jnp.int32, (2, ROWS), 0)
     own = (lax.broadcasted_iota(jnp.int32, (2, ROWS), 1) == own).astype(bf16)
-    stream_own = dot(own, stream, 1, 1)
-    codes_out = dot(order, codes, 0, 0).astype(bf16)
+    terms, stream, stream_own, codes_out = lax.optimization_barrier(
+        (terms, stream, dot(own, stream, 1, 1), dot(order, codes, 0, 0).astype(bf16))
+    )
+    recon_own = jnp.sum(terms.astype(f32), axis=0) + decoder_bias[None, :]
+    error_own = (recon_own - stream_own).astype(bf16)
 
-    error_own = (recon_own - stream_own).astype(bf16)
     error_kept = copies_to(error_own, CHIP, CHIPS).reshape(HALF, D)
-    error_other = swap(error_kept)
+    error = jnp.concatenate([error_kept, swap(error_kept)], axis=0)
     slope = jax.nn.sigmoid(encoded)
-    slope_kept = by_core(slope[:HALF], slope[HALF:])
-    slope_other = by_core(slope[HALF:], slope[:HALF])
-    grad_kept = (slope_kept * (dot(error_kept, decoder_weight, 1, 1) + sparsity_weight)).astype(bf16)
-    grad_other = (slope_other * (dot(error_other, decoder_weight, 1, 1) + sparsity_weight)).astype(bf16)
-    arrived = swap(dot(grad_other, encoder_weight, 1, 1).astype(bf16))
-    both = (dot(grad_kept, encoder_weight, 1, 1) + arrived.astype(f32)).astype(bf16)
-    input_gradient = jnp.sum(
-        exchange(both.reshape(CHIPS, 2, D), CHIP).astype(f32), axis=0
-    ) - error_own.astype(f32)
+    slope = by_core(slope, jnp.concatenate([slope[HALF:], slope[:HALF]], axis=0))
+    code_gradient = dot(error, decoder_weight, 1, 1)
+    grad = (slope * (code_gradient + sparsity_weight)).astype(bf16)
+    summed = dot(grad, encoder_weight, 1, 1)
+    arrived = swap(summed[HALF:].astype(bf16))
+    both = (summed[:HALF] + arrived.astype(f32)).astype(bf16)
+    terms = exchange(both.reshape(CHIPS, 2, D), CHIP)
 
-    decoder_gradient = dot(
-        jnp.concatenate([codes_kept, codes_other], axis=0),
-        jnp.concatenate([error_kept, error_other], axis=0),
-        0,
-        0,
-    ).astype(bf16)
-    grad = by_core(
-        jnp.concatenate([grad_kept, grad_other], axis=0),
-        jnp.concatenate([grad_other, grad_kept], axis=0),
+    decoder_gradient = dot(jnp.concatenate([codes_kept, codes_other], axis=0), error, 0, 0).astype(bf16)
+    grad = by_core(grad, jnp.concatenate([grad[HALF:], grad[:HALF]], axis=0))
+    encoder_gradient = dot(stream, grad, 1, 0).astype(bf16)
+    terms, decoder_gradient, encoder_gradient = lax.optimization_barrier(
+        (terms, decoder_gradient, encoder_gradient)
     )
-    encoder_gradient = dot(stream, grad, 1, 0).astype(bf16)
+    input_gradient = jnp.sum(terms.astype(f32), axis=0) - error_own.astype(f32)
     return codes_out, recon_own.astype(bf16), encoder_gradient, decoder_gradient, input_gradient
 
 

time: 188 us -> 181 us (0.963)
  matrix products: 26.1 us -> 20.1 us
  waiting for transfers between devices: 35.7 us -> 33.8 us
    dot_general x19 -> x17, matrix products: 26.1 us -> 20.1 us  [dot(): lax.dot_general(a, b, (((ca,), (cb,)), ((), ())), preferred_element_type=...]
    all_to_all x2, waiting for transfers between devices: 26 us -> 23.2 us  [exchange(): return lax.all_to_all(v, axes, 0, 0, tiled=True)]
    slice x0 -> x3, local copies, waits for them, and re-layouts: none -> 2.2 us  [the longest x1 1.12 us: shards(): slope[HALF:]]
    unnamed x77 -> x70, local copies, waits for them, and re-layouts: 2.84 us -> 3.89 us
  transfers between devices with their start and end apart: 9 -> 9, of which waited for: 8 -> 9; matrix products, arithmetic and copies ran while one was open for 7% -> 8% of each run, Pallas kernels for 0% -> 0%
where the time goes in v4:
time: 181 us; the launch traced here: 180 us
  blocking collectives  95.8 us (53%)
  waiting for transfers between devices  33.8 us (19%)
  matrix products  20.1 us (11%)
  local copies, waits for them, and re-layouts  12.1 us (7%)
  starting transfers between devices  11.4 us (6%)
  other arithmetic  5.66 us (3%)
    all_to_all x5, blocking collectives, exchange(): return lax.all_to_all(v, axes, 0, 0, tiled=True)  95.8 us
    all_to_all x2, waiting for transfers between devices, exchange(): return lax.all_to_all(v, axes, 0, 0, tiled=True)  23.2 us
    dot_general x17, matrix products, dot(): lax.dot_general(a, b, (((ca,), (cb,)), ((), ())), preferred_element_type=...  20.1 us
    ppermute x7, waiting for transfers between devices, swap(): return lax.ppermute(v, 'c', [(0, 1), (1, 0)])  10.6 us
    all_to_all x2, starting transfers between devices, exchange(): return lax.all_to_all(v, axes, 0, 0, tiled=True)  9.86 us
    unnamed x70, local copies, waits for them, and re-layouts  3.89 us
  transfers between devices with their start and end apart: 9, of which 9 were waited for; matrix products, arithmetic and copies ran while one was open for 8% of the time, Pallas kernels for 0%

profile of v4, /device:TPU:0, one launch (start us, length us, event | category | flops | bytes accessed | tf_op | source)
XLA Modules:
  0.0 180.2 jit_solution(16976079127764851834)
XLA Ops:
  0.8 1.3 constant_dynamic-update-slice_fusion.1
  2.2 0.3 fusion.67
  2.5 0.2 multiply_reduce_fusion
  2.7 0.5 convolution_convert_fusion.3
  3.2 0.1 collective-permute-start
  3.3 0.5 collective-permute-start.1
  3.8 0.2 multiply_reduce_fusion.1
  4.0 1.4 collective-permute-done.1
  5.4 0.1 copy.29
  5.5 0.3 collective-permute-done
  5.9 1.7 add_convert_fusion.1
  7.6 0.1 fusion.28
  7.6 23.9 %all_to_all.35 = bf16[8,16,3712]{2,1,0:T(8,128)(2,1)S(1)} all-to-all(bf16[8,16,3712]{2,1,0:T(8,128)(2,1)S(1)} %bitcast.107), channel_id=1, replica_groups=mesh['zl'=2,'x'=4,'y'=4,'zh'=2,'c'=2] {'y','zh'}, dimensions={0} | all-to-all | bytes 1900544 | tf_op jit(solution)/shard_map/all_to_all | solution.py:33
  31.6 0.1 convert_reduce_fusion
  31.7 0.1 slice_reduce_fusion
  31.8 0.1 slice_multiply_fusion
  32.0 12.6 %all_to_all.36 = bf16[8,16,1792]{2,1,0:T(8,128)(2,1)S(1)} all-to-all(bf16[8,16,1792]{2,1,0:T(8,128)(2,1)S(1)} %broadcast_in_dim.8), channel_id=1, replica_groups=mesh['zl'=2,'x'=4,'y'=4,'zh'=2,'c'=2] {'y','zh'}, dimensions={0} | all-to-all | bytes 917504 | tf_op jit(solution)/shard_map/all_to_all | solution.py:33
  44.6 0.4 fusion.26
  45.0 1.4 collective-permute-done.2
  46.4 0.4 fusion.27
  46.9 19.2 %all_to_all.37 = bf16[8,224,256]{2,1,0:T(8,128)(2,1)S(1)} all-to-all(bf16[8,224,256]{2,1,0:T(8,128)(2,1)S(1)} %broadcast_in_dim.9), channel_id=1, replica_groups=mesh['zl'=2,'x'=4,'y'=4,'zh'=2,'c'=2] {'zl','x'}, dimensions={0} | all-to-all | bytes 1835008 | tf_op jit(solution)/shard_map/all_to_all | solution.py:33
  66.1 0.1 convert_reduce_fusion.3
  66.3 0.4 fusion.25
  66.8 18.6 %all_to_all.38 = bf16[8,224,256]{2,1,0:T(8,128)(2,1)S(1)} all-to-all(bf16[8,224,256]{2,1,0:T(8,128)(2,1)S(1)} %broadcast_in_dim.10), channel_id=1, replica_groups=mesh['zl'=2,'x'=4,'y'=4,'zh'=2,'c'=2] {'y','zh'}, dimensions={0} | all-to-all | bytes 1835008 | tf_op jit(solution)/shard_map/all_to_all | solution.py:33
  85.4 0.7 fusion.10
  86.1 1.8 collective-permute-done.3
  87.9 2.0 %add_divide_fusion = (f32[256,512]{1,0:T(8,128)}, bf16[256,512]{1,0:T(8,128)(2,1)S(1)}, f32[256,512]{1,0:T(8,128)}) fusion(f32[512]{0:T(512)S(1)} %copy-done.32, f32[256,512]{1,0:T(8,128)S(1)} %fusion.10, bf16[8,224,256]{2,1,0:T(8,128)(2,1)S(1)} %collective-permute-done.3, pred[]{:T(512)S(6)} %eq.31, bf16[8,2,224,512]{3,2,1,0:T(8,128)(2,1)S(1)} %bitcast.109), kind=kOutput, calls=%fused_computation.49 | convolution fusion | flops 472252416 | bytes 6424577 | tf_op jit(solution)/shard_map/dot_general | solution.py:25
  89.9 0.7 convolution_convert_fusion.2
  90.6 0.2 collective-permute-start.4
  90.8 2.3 %collective-permute-done.4 = bf16[128,3584]{1,0:T(8,128)(2,1)S(1)} collective-permute-done((bf16[128,3584]{1,0:T(8,128)(2,1)S(1)}, bf16[128,3584]{1,0:T(8,128)(2,1)S(1)}, u32[]{:S(2)}, u32[]{:S(2)}) %collective-permute-start.4) | collective-permute-done | bytes 917536 | tf_op jit(solution)/shard_map/ppermute | solution.py:29
  93.2 0.7 add_convert_fusion
  93.8 1.3 reshape.87
  95.1 4.8 %all-to-all-start.4 = ((bf16[64,2,3584]{2,1,0:T(2,128)(2,1)}), bf16[64,2,3584]{2,1,0:T(2,128)(2,1)S(1)}, u32[]{:S(2)}, u32[]{:S(2)}) async-start(bf16[64,2,3584]{2,1,0:T(2,128)(2,1)} %reshape.87), calls=%async_computation.4 | async-start | bytes 1835008 | tf_op jit(solution)/shard_map/all_to_all | solution.py:33
  99.9 0.3 maximum_select_fusion
  100.3 0.1 copy.32
  100.4 0.7 copy-done.14
  101.2 1.2 convolution_convert_fusion.4
  102.4 1.2 fusion.58
  103.6 14.1 %all-to-all-done.4 = bf16[64,2,3584]{2,1,0:T(2,128)(2,1)S(1)} async-done(((bf16[64,2,3584]{2,1,0:T(2,128)(2,1)}), bf16[64,2,3584]{2,1,0:T(2,128)(2,1)S(1)}, u32[]{:S(2)}, u32[]{:S(2)}) %all-to-all-start.4) | async-done | bytes 917536 | tf_op jit(solution)/shard_map/all_to_all | solution.py:33
  117.7 0.7 convert_reduce_fusion.2
  118.5 1.4 subtract_convert_fusion
  119.8 0.5 broadcast_in_dim.11
  120.3 0.1 copy-done.15
  120.4 21.5 %all_to_all.39 = bf16[64,2,3584]{2,1,0:T(2,128)(2,1)} all-to-all(bf16[64,2,3584]{2,1,0:T(2,128)(2,1)S(1)} %broadcast_in_dim.11), channel_id=1, replica_groups=mesh['zl'=2,'x'=4,'y'=4,'zh'=2,'c'=2] {'zl','x','y','zh'}, dimensions={0} | all-to-all | bytes 1835008 | tf_op jit(solution)/shard_map/all_to_all | solution.py:33
  141.9 2.5 %reshape.88 = bf16[128,3584]{1,0:T(8,128)(2,1)S(1)} reshape(bf16[64,2,3584]{2,1,0:T(2,128)(2,1)} %all_to_all.39) | data formatting | bytes 1835008 | tf_op jit(solution)/shard_map/reshape | solution.py:130
  144.4 0.1 collective-permute-start.5
  144.5 1.1 fusion.69
  145.7 1.2 collective-permute-done.5
  147.1 0.6 copy-done.2
  147.7 1.2 fusion.23
  148.9 0.8 copy-done.5
  149.7 1.1 fusion.71
  150.9 0.1 slice.151
  151.0 0.7 collective-permute-start.6
  151.7 2.1 %collective-permute-done.6 = bf16[128,3584]{1,0:T(8,128)(2,1)S(1)} collective-permute-done((bf16[128,3584]{1,0:T(8,128)(2,1)S(1)}, bf16[128,3584]{1,0:T(8,128)(2,1)S(1)}, u32[]{:S(2)}, u32[]{:S(2)}) %collective-permute-start.6) | collective-permute-done | bytes 917536 | tf_op jit(solution)/shard_map/ppermute | solution.py:29
  153.8 0.2 fusion.1
  154.0 1.3 reshape.89
  155.3 5.1 %all-to-all-start.6 = ((bf16[64,2,3584]{2,1,0:T(2,128)(2,1)}), bf16[64,2,3584]{2,1,0:T(2,128)(2,1)S(1)}, u32[]{:S(2)}, u32[]{:S(2)}) async-start(bf16[64,2,3584]{2,1,0:T(2,128)(2,1)} %reshape.89), calls=%async_computation.6 | async-start | bytes 1835008 | tf_op jit(solution)/shard_map/all_to_all | solution.py:33
  160.4 1.0 fusion.70
  161.4 4.7 %convolution_convert_fusion.1 = bf16[512,3584]{1,0:T(8,128)(2,1)} fusion(bf16[256,3584]{1,0:T(8,128)(2,1)} %copy-done.3, bf16[128,512]{1,0:T(8,128)(2,1)} %copy-done.8, bf16[128,512]{1,0:T(8,128)(2,1)} %copy-done.9), kind=kOutput, calls=%fused_computation.1 | convolution fusion | flops 941883392 | bytes 5767168 | tf_op jit(solution)/shard_map/dot_general | solution.py:25
  166.0 3.0 %convolution_convert_fusion = bf16[3584,512]{1,0:T(8,128)(2,1)} fusion(bf16[3584,256]{1,0:T(8,128)(2,1)S(1)} %bitcast.106, bf16[256,512]{1,0:T(8,128)(2,1)S(1)} %copy-done.7, bf16[128,512]{1,0:T(8,128)(2,1)S(1)} %get-tuple-element.24, bf16[128,512]{1,0:T(8,128)(2,1)S(1)} %get-tuple-element.23, pred[]{:T(512)S(6)} %eq.31), kind=kOutput, calls=%fused_computation | convolution fusion | flops 942014464 | bytes 6029313 | tf_op jit(solution)/shard_map/dot_general | solution.py:25
  169.0 9.1 %all-to-all-done.6 = bf16[64,2,3584]{2,1,0:T(2,128)(2,1)S(1)} async-done(((bf16[64,2,3584]{2,1,0:T(2,128)(2,1)}), bf16[64,2,3584]{2,1,0:T(2,128)(2,1)S(1)}, u32[]{:S(2)}, u32[]{:S(2)}) %all-to-all-start.6) | async-done | bytes 917536 | tf_op jit(solution)/shard_map/all_to_all | solution.py:33
  178.1 0.7 convert_reduce_fusion.1
  178.9 1.3 convert_subtract_fusion
  (82 shorter events, 0.7 us)
Async XLA Ops:
  0.6 44.0 %copy-start = (bf16[1792,224]{0,1:T(8,128)(2,1)S(1)}, bf16[1792,224]{0,1:T(8,128)(2,1)}, u32[]{:S(2)}) copy-start(bf16[1792,224]{0,1:T(8,128)(2,1)} %param.13) | copy-start | bytes 2408452
  0.6 1.5 copy-start.12
  0.7 1.8 %copy-start.29 = (bf16[256,224]{0,1:T(8,128)(2,1)S(1)}, bf16[256,224]{0,1:T(8,128)(2,1)}, u32[]{:S(2)}) copy-start(bf16[256,224]{0,1:T(8,128)(2,1)} %param.9) | copy-start | bytes 344068
  0.7 65.5 %copy-start.16 = (s32[256]{0:T(256)}, s32[256]{0:T(256)S(1)}, u32[]{:S(2)}) copy-start(s32[256]{0:T(256)S(1)} %get-tuple-element.37) | copy-start | bytes 3076
  0.7 65.5 %copy-start.18 = (s32[256]{0:T(256)}, s32[256]{0:T(256)S(1)}, u32[]{:S(2)}) copy-start(s32[256]{0:T(256)S(1)} %get-tuple-element.38) | copy-start | bytes 3076
  0.7 65.5 %copy-start.20 = (s32[256]{0:T(256)}, s32[256]{0:T(256)S(1)}, u32[]{:S(2)}) copy-start(s32[256]{0:T(256)S(1)} %get-tuple-element.41) | copy-start | bytes 3076
  0.7 65.5 %copy-start.22 = (s32[256]{0:T(256)}, s32[256]{0:T(256)S(1)}, u32[]{:S(2)}) copy-start(s32[256]{0:T(256)S(1)} %get-tuple-element.42) | copy-start | bytes 3076
  0.8 65.5 %copy-start.25 = (pred[256]{0:T(512)(128)(4,1)}, pred[256]{0:T(512)(128)(4,1)S(1)}, u32[]{:S(2)}) copy-start(pred[256]{0:T(512)(128)(4,1)S(1)} %get-tuple-element.39) | copy-start | bytes 772
  0.8 65.5 %copy-start.27 = (pred[256]{0:T(512)(128)(4,1)}, pred[256]{0:T(512)(128)(4,1)S(1)}, u32[]{:S(2)}) copy-start(pred[256]{0:T(512)(128)(4,1)S(1)} %get-tuple-element.40) | copy-start | bytes 772
  0.8 1.9 %copy-start.24 = (f32[224]{0:T(256)S(1)}, f32[224]{0:T(256)}, u32[]{:S(2)}) copy-start(f32[224]{0:T(256)} %param.10) | copy-start | bytes 2692
  2.2 1.6 copy-start.30
  3.2 2.7 %collective-permute-start = (bf16[128,3584]{1,0:T(8,128)(2,1)S(1)}, bf16[128,3584]{1,0:T(8,128)(2,1)}, u32[]{:S(2)}, u32[]{:S(2)}) collective-permute-start(bf16[128,3584]{1,0:T(8,128)(2,1)S(1)} %convolution_convert_fusion.3), channel_id=1, source_target_pairs={{0,1},{1,0},{2,3},{3,2},{4,5},{5,4},{6,7},{7,6},{8,9},{9,8},{10,11... | collective-permute-start | bytes 2752520 | tf_op jit(solution)/shard_map/ppermute | solution.py:29
  3.3 2.1 %collective-permute-start.1 = (f32[128]{0:T(128)S(1)}, f32[128]{0:T(128)S(1)}, u32[]{:S(2)}, u32[]{:S(2)}) collective-permute-start(f32[128]{0:T(128)S(1)} %get-tuple-element.34), channel_id=1, source_target_pairs={{0,1},{1,0},{2,3},{3,2},{4,5},{5,4},{6,7},{7,6},{8,9},{9,8},{10,11... | collective-permute-start | bytes 1544 | tf_op jit(solution)/shard_map/ppermute | solution.py:29
  44.6 1.8 %collective-permute-start.2 = (bf16[128,1792]{1,0:T(8,128)(2,1)S(1)}, bf16[128,1792]{1,0:T(8,128)(2,1)S(1)}, u32[]{:S(2)}, u32[]{:S(2)}) collective-permute-start(bf16[128,1792]{1,0:T(8,128)(2,1)S(1)} %bitcast.111), channel_id=1, source_target_pairs={{0,1},{1,0},{2,3},{3,2},{4,5},{5,4},{6,7},{7,6},{8,9},{9,8},{10,11... | collective-permute-start | bytes 1376264 | tf_op jit(solution)/shard_map/ppermute | solution.py:29
  46.9 19.4 %copy-start.31 = (bf16[256,224]{0,1:T(8,128)(2,1)S(1)}, bf16[256,224]{0,1:T(8,128)(2,1)}, u32[]{:S(2)}) copy-start(bf16[256,224]{0,1:T(8,128)(2,1)} %param.9) | copy-start | bytes 344068
  66.3 19.1 %copy-start.4 = (bf16[3584,512]{1,0:T(8,128)(2,1)S(1)}, bf16[3584,512]{1,0:T(8,128)(2,1)}, u32[]{:S(2)}) copy-start(bf16[3584,512]{1,0:T(8,128)(2,1)} %param.14) | copy-start | bytes 11010052
  85.4 2.5 %collective-permute-start.3 = (bf16[8,224,256]{2,1,0:T(8,128)(2,1)S(1)}, bf16[8,224,256]{2,1,0:T(8,128)(2,1)S(1)}, u32[]{:S(2)}, u32[]{:S(2)}) collective-permute-start(bf16[8,224,256]{2,1,0:T(8,128)(2,1)S(1)} %all_to_all.38), channel_id=1, source_target_pairs={{0,1},{1,0},{2,3},{3,2},{4,5},{5,4},{6,7},{7,6},{8,9},{9,8},{10,11... | collective-permute-start | bytes 2752520 | tf_op jit(solution)/shard_map/ppermute | solution.py:29
  85.4 2.5 %copy-start.32 = (f32[512]{0:T(512)S(1)}, f32[512]{0:T(512)}, u32[]{:S(2)}) copy-start(f32[512]{0:T(512)} %param.15) | copy-start | bytes 6148
  86.1 3.8 %copy-start.1 = (bf16[512,3584]{1,0:T(8,128)(2,1)S(1)}, bf16[512,3584]{1,0:T(8,128)(2,1)}, u32[]{:S(2)}) copy-start(bf16[512,3584]{1,0:T(8,128)(2,1)} %param.16) | copy-start | bytes 11010052
  87.9 2.0 %copy-start.10 = (bf16[8,224,256]{2,1,0:T(8,128)(2,1)}, bf16[8,224,256]{2,1,0:T(8,128)(2,1)S(1)}, u32[]{:S(2)}) copy-start(bf16[8,224,256]{2,1,0:T(8,128)(2,1)S(1)} %collective-permute-done.3) | copy-start | bytes 2752516
  89.9 0.7 copy-start.13
  89.9 0.7 copy-start.8
  89.9 3.3 %copy-start.9 = (bf16[128,512]{1,0:T(8,128)(2,1)}, bf16[128,512]{1,0:T(8,128)(2,1)S(1)}, u32[]{:S(2)}) copy-start(bf16[128,512]{1,0:T(8,128)(2,1)S(1)} %get-tuple-element.26) | copy-start | bytes 393220
  90.6 2.6 %collective-permute-start.4 = (bf16[128,3584]{1,0:T(8,128)(2,1)S(1)}, bf16[128,3584]{1,0:T(8,128)(2,1)S(1)}, u32[]{:S(2)}, u32[]{:S(2)}) collective-permute-start(bf16[128,3584]{1,0:T(8,128)(2,1)S(1)} %convolution_convert_fusion.2), channel_id=1, source_target_pairs={{0,1},{1,0},{2,3},{3,2},{4,5},{5,4},{6,7},{7,6},{8,9},{9,8},{10,11... | collective-permute-start | bytes 2752520 | tf_op jit(solution)/shard_map/ppermute | solution.py:29
  95.1 4.8 %copy-start.11 = (bf16[8,224,256]{2,1,0:T(8,128)(2,1)S(1)}, bf16[8,224,256]{2,1,0:T(8,128)(2,1)}, u32[]{:S(2)}) copy-start(bf16[8,224,256]{2,1,0:T(8,128)(2,1)} %copy-done.10) | copy-start | bytes 2752516
  95.1 22.6 %all-to-all-start.4 = ((bf16[64,2,3584]{2,1,0:T(2,128)(2,1)}), bf16[64,2,3584]{2,1,0:T(2,128)(2,1)S(1)}, u32[]{:S(2)}, u32[]{:S(2)}) async-start(bf16[64,2,3584]{2,1,0:T(2,128)(2,1)} %reshape.87), calls=%async_computation.4 | async-start | bytes 1835008 | tf_op jit(solution)/shard_map/all_to_all | solution.py:33
  100.2 1.0 copy-start.14
  100.2 0.9 copy-start.17
  100.2 0.9 copy-start.19
  100.3 0.9 copy-start.21
  100.3 0.9 copy-start.23
  100.3 0.9 copy-start.26
  100.3 0.9 copy-start.28
  119.8 0.6 copy-start.15
  144.4 2.6 %collective-permute-start.5 = (bf16[128,3584]{1,0:T(8,128)(2,1)S(1)}, bf16[128,3584]{1,0:T(8,128)(2,1)S(1)}, u32[]{:S(2)}, u32[]{:S(2)}) collective-permute-start(bf16[128,3584]{1,0:T(8,128)(2,1)S(1)} %reshape.88), channel_id=1, source_target_pairs={{0,1},{1,0},{2,3},{3,2},{4,5},{5,4},{6,7},{7,6},{8,9},{9,8},{10,11... | collective-permute-start | bytes 2752520 | tf_op jit(solution)/shard_map/ppermute | solution.py:29
  144.5 2.5 %copy-start.33 = (f32[256,512]{1,0:T(8,128)S(1)}, f32[256,512]{1,0:T(8,128)}, u32[]{:S(2)}) copy-start(f32[256,512]{1,0:T(8,128)} %get-tuple-element.36) | copy-start | bytes 1572868
  145.7 2.1 %copy-start.2 = (bf16[512,3584]{1,0:T(8,128)(2,1)S(1)}, bf16[512,3584]{1,0:T(8,128)(2,1)}, u32[]{:S(2)}) copy-start(bf16[512,3584]{1,0:T(8,128)(2,1)} %param.16) | copy-start | bytes 11010052
  147.0 1.9 %copy-start.3 = (bf16[256,3584]{1,0:T(8,128)(2,1)}, bf16[256,3584]{1,0:T(8,128)(2,1)S(1)}, u32[]{:S(2)}) copy-start(bf16[256,3584]{1,0:T(8,128)(2,1)S(1)} %constant_dynamic-update-slice_fusion.2) | copy-start | bytes 5505028
  147.7 2.0 %copy-start.5 = (bf16[3584,512]{1,0:T(8,128)(2,1)S(1)}, bf16[3584,512]{1,0:T(8,128)(2,1)}, u32[]{:S(2)}) copy-start(bf16[3584,512]{1,0:T(8,128)(2,1)} %param.14) | copy-start | bytes 11010052
  149.7 1.2 copy-start.6
  151.0 2.8 %collective-permute-start.6 = (bf16[128,3584]{1,0:T(8,128)(2,1)S(1)}, bf16[128,3584]{1,0:T(8,128)(2,1)S(1)}, u32[]{:S(2)}, u32[]{:S(2)}) collective-permute-start(bf16[128,3584]{1,0:T(8,128)(2,1)S(1)} %slice.151), channel_id=1, source_target_pairs={{0,1},{1,0},{2,3},{3,2},{4,5},{5,4},{6,7},{7,6},{8,9},{9,8},{10,11... | collective-permute-start | bytes 2752520 | tf_op jit(solution)/shard_map/ppermute | solution.py:29
  155.3 22.9 %all-to-all-start.6 = ((bf16[64,2,3584]{2,1,0:T(2,128)(2,1)}), bf16[64,2,3584]{2,1,0:T(2,128)(2,1)S(1)}, u32[]{:S(2)}, u32[]{:S(2)}) async-start(bf16[64,2,3584]{2,1,0:T(2,128)(2,1)} %reshape.89), calls=%async_computation.6 | async-start | bytes 1835008 | tf_op jit(solution)/shard_map/all_to_all | solution.py:33
  161.4 4.7 %copy-start.7 = (bf16[256,512]{1,0:T(8,128)(2,1)S(1)}, bf16[256,512]{1,0:T(8,128)(2,1)}, u32[]{:S(2)}) copy-start(bf16[256,512]{1,0:T(8,128)(2,1)} %copy-done.6) | copy-start | bytes 786436

commit v5 on v2

v5 whole, which is shorter than its diff:
```python
import jax
import jax.numpy as jnp
import numpy as np
from jax import lax
from jax.experimental import pallas as pl
from jax.experimental.pallas import tpu as pltpu
from jax.sharding import Mesh
from jax.sharding import PartitionSpec as P

D = 3584
ROWS = 256
HALF = ROWS // 2
CHIPS = 64

MP = ("zl", "x")
RING = ("y", "zh")
FEAT = RING + ("c",)
CHIP = MP + RING
ALL = MP + FEAT

sparsity_weight = 0.2
norm_eps = 1e-06
bf16 = jnp.bfloat16
f32 = jnp.float32


def dot(a, b, ca, cb):
    return lax.dot_general(a, b, (((ca,), (cb,)), ((), ())), preferred_element_type=f32)


def swap(v):
    return lax.ppermute(v, "c", [(0, 1), (1, 0)])


def exchange(v, axes):
    return lax.all_to_all(v, axes, 0, 0, tiled=True)


def copies_to(v, axes, parts):
    return exchange(jnp.broadcast_to(v[None], (parts,) + v.shape), axes)


def local(kernel, outs, ins, flops):
    return pl.pallas_call(
        kernel,
        out_shape=[jax.ShapeDtypeStruct(shape, kind) for shape, kind in outs],
        in_specs=[pl.BlockSpec(memory_space=pltpu.VMEM) for _ in ins],
        out_specs=[pl.BlockSpec(memory_space=pltpu.VMEM) for _ in outs],
        compiler_params=pltpu.CompilerParams(vmem_limit_bytes=12 * 2**20),
        cost_estimate=pl.CostEstimate(flops=flops, bytes_accessed=2**21, transcendentals=0),
    )(*ins)


def three(v):
    first = v.astype(bf16).astype(f32)
    second = (v - first).astype(bf16).astype(f32)
    third = v - first - second
    lane = lax.broadcasted_iota(jnp.int32, v.shape, 1)
    parts = jnp.where(lane == 0, first, jnp.where(lane == 1, second, jnp.where(lane == 2, third, 0.0)))
    return parts.astype(bf16)


def rows_of(core):
    row = lax.broadcasted_iota(jnp.int32, (ROWS, HALF), 0)
    at = lax.broadcasted_iota(jnp.int32, (ROWS, HALF), 1)
    return (row == (at // 2) * 4 + core * 2 + at % 2).astype(bf16)


def scaled_rows(source, gain, picked):
    size = source.shape[0]
    same = lax.broadcasted_iota(jnp.int32, (size, size), 0) == lax.broadcasted_iota(jnp.int32, (size, size), 1)
    column = jnp.sum(jnp.where(same, gain[...], 0.0), axis=1, keepdims=True)
    rows = dot(source[...], picked, 1, 0)
    squared = rows * rows
    high = squared.astype(bf16)
    low = (squared - high.astype(f32)).astype(bf16)
    ones = jnp.ones((size, 128), bf16)
    return (rows * column).astype(bf16), dot(high, ones, 0, 0) + dot(low, ones, 0, 0)


def assemble(kept, other, out):
    core = lax.axis_index("c")
    for k in range(kept.shape[0]):
        out[k, core] = kept[k]
        out[k, 1 - core] = other[k]


def reorder(rows, v, out):
    out[...] = dot(rows[...], v[...], 1, 0).astype(bf16)


def retile(v, out):
    for at in range(0, v.shape[2], 512):
        out[:, at : at + 512] = v[:, :, at : at + 512].astype(f32).reshape(HALF, 512).astype(bf16)


def merge(kept, arrived, out):
    for at in range(0, out.shape[2], 512):
        term = kept[:, at : at + 512] + arrived[:, at : at + 512].astype(f32)
        out[:, :, at : at + 512] = term.reshape(CHIPS, 2, 512).astype(bf16)


def project_other(source, gain, weight, order, sent, ordered):
    ordered[...] = dot(source[...], order[...], 1, 1).astype(bf16)
    scaled, squares = scaled_rows(source, gain, rows_of(1 - lax.axis_index("c")))
    columns = weight.shape[1]
    for at in range(0, columns, 512):
        sent[:, at : at + 512] = dot(scaled, weight[:, at : at + 512], 0, 0).astype(bf16)
    sent[:, columns:] = three(squares)


def project_kept(source, gain, weight, arrived, out):
    scaled, squares = scaled_rows(source, gain, rows_of(lax.axis_index("c")))
    columns = weight.shape[1]
    for at in range(0, columns, 512):
        term = dot(scaled, weight[:, at : at + 512], 0, 0)
        out[:, at : at + 512] = (term + arrived[:, at : at + 512].astype(f32)).astype(bf16)
    out[:, columns:] = three(squares + jnp.sum(arrived[:, columns:].astype(f32), axis=1, keepdims=True))


def shards(
    residual_in,
    norm_gain,
    gate_weight,
    up_weight,
    down_weight,
    encoder_weight,
    encoder_bias,
    decoder_weight,
    decoder_bias,
):
    hidden_local = gate_weight.shape[1]
    core = lax.axis_index("c")
    piece = residual_in.shape[1] // 8
    first_core, piece_at, own_at, residual_in = lax.optimization_barrier(
        (
            core == 0,
            (lax.axis_index(MP) * piece).astype(jnp.uint32),
            core * HALF + lax.axis_index(CHIP) * 2,
            residual_in,
        )
    )

    def by_core(zero, one):
        return jnp.where(first_core, zero, one)

    at = np.arange(ROWS)
    place = (at % HALF) // 2 * 4 + at // HALF * 2 + at % 2
    order = jnp.asarray(np.eye(ROWS)[place], bf16)

    joint_weight = jnp.concatenate([gate_weight, up_weight], axis=1)
    operands = [residual_in.T, norm_gain[None, :], joint_weight]
    payload = [((HALF, joint_weight.shape[1] + 128), bf16)]
    sent, ordered = local(
        project_other,
        payload + [(operands[0].shape, bf16)],
        operands + [order],
        10**9,
    )
    (both,) = local(project_kept, payload, operands + [swap(sent)], 10**9)
    both = exchange(both.reshape(8, 16, both.shape[1]), RING)
    projected = jnp.sum(both.astype(f32), axis=0)
    mean = jnp.sum(projected[:, 2 * hidden_local :], axis=1, keepdims=True) / D
    projected = projected[:, : 2 * hidden_local] * lax.rsqrt(mean + norm_eps)
    hidden = (jax.nn.silu(projected[:, :hidden_local]) * projected[:, hidden_local:]).astype(bf16)

    hidden_kept = copies_to(hidden, RING, 8).reshape(HALF, hidden_local)
    hidden_other = swap(hidden_kept)
    mixed_kept = dot(down_weight, hidden_kept, 0, 1).astype(bf16)
    mixed_other = dot(down_weight, hidden_other, 0, 1).astype(bf16)
    mixed = by_core(
        jnp.concatenate([mixed_kept, mixed_other], axis=1),
        jnp.concatenate([mixed_other, mixed_kept], axis=1),
    )
    mixed = jnp.sum(exchange(mixed.reshape(8, piece, ROWS), MP).astype(f32), axis=0)
    source = lax.dynamic_slice(ordered, (piece_at, jnp.uint32(0)), (piece, ROWS)).astype(f32)
    stream_piece = (source + mixed).astype(bf16)

    blocks_kept = copies_to(stream_piece, RING + MP, CHIPS).reshape(8, 8 * piece, ROWS)
    blocks_kept = lax.optimization_barrier(blocks_kept)
    blocks_other = swap(blocks_kept)
    (stream,) = local(
        assemble, [((8, 2) + blocks_kept.shape[1:], bf16)], [blocks_kept, blocks_other], 10**7
    )
    stream = stream.reshape(D, ROWS)
    encoded = dot(stream, encoder_weight, 0, 0) + encoder_bias[None, :]
    codes = jax.nn.softplus(encoded).astype(bf16)
    codes_kept = by_core(codes[:HALF], codes[HALF:])
    codes_other = by_core(codes[HALF:], codes[:HALF])

    arrived = swap(dot(codes_other, decoder_weight, 1, 0).astype(bf16))
    pieces = [((CHIPS, 2, D), bf16)]
    own = own_at + lax.broadcasted_iota(jnp.int32, (2, ROWS), 0)
    own = (lax.broadcasted_iota(jnp.int32, (2, ROWS), 1) == own).astype(bf16)
    kept, offset = lax.optimization_barrier(
        (dot(codes_kept, decoder_weight, 1, 0), decoder_bias[None, :] - dot(own, stream, 1, 1))
    )
    (both,) = local(merge, pieces, [kept, arrived], 10**7)
    terms = exchange(both, CHIP)
    recon_own = jnp.sum(terms.astype(f32), axis=0)
    error_own = (recon_own + offset).astype(bf16)

    error_kept = copies_to(error_own, CHIP, CHIPS)
    error_other = swap(error_kept)
    (error_kept,) = local(retile, [((HALF, D), bf16)], [error_kept], 10**7)
    slope = jax.nn.sigmoid(encoded)
    slope_kept = by_core(slope[:HALF], slope[HALF:])
    slope_other = by_core(slope[HALF:], slope[:HALF])
    grad_kept = (slope_kept * (dot(error_kept, decoder_weight, 1, 1) + sparsity_weight)).astype(bf16)
    grad_kept, error_other = lax.optimization_barrier((grad_kept, error_other))
    (error_other,) = local(retile, [((HALF, D), bf16)], [error_other], 10**7)
    grad_other = (slope_other * (dot(error_other, decoder_weight, 1, 1) + sparsity_weight)).astype(bf16)
    arrived = swap(dot(grad_other, encoder_weight, 1, 1).astype(bf16))
    (both,) = local(merge, pieces, [dot(grad_kept, encoder_weight, 1, 1), arrived], 10**7)
    both, recon_own, codes, codes_kept, codes_other, error_kept, error_other, grad_kept, grad_other = (
        lax.optimization_barrier(
            (both, recon_own, codes, codes_kept, codes_other, error_kept, error_other, grad_kept, grad_other)
        )
    )
    terms = exchange(both, CHIP)
    recon_own = (recon_own + decoder_bias[None, :]).astype(bf16)
    (codes_out,) = local(
        reorder, [(codes.shape, bf16)], [jnp.asarray(np.eye(ROWS)[place].T, bf16), codes], 10**8
    )
    decoder_gradient = dot(
        jnp.concatenate([codes_kept, codes_other], axis=0),
        jnp.concatenate([error_kept, error_other], axis=0),
        0,
        0,
    ).astype(bf16)
    grad = by_core(
        jnp.concatenate([grad_kept, grad_other], axis=0),
        jnp.concatenate([grad_other, grad_kept], axis=0),
    )
    encoder_gradient = dot(stream, grad, 1, 0).astype(bf16)
    terms, decoder_gradient, encoder_gradient, recon_own, codes_out = lax.optimization_barrier(
        (terms, decoder_gradient, encoder_gradient, recon_own, codes_out)
    )
    input_gradient = jnp.sum(terms.astype(f32), axis=0) - error_own.astype(f32)
    return codes_out, recon_own, encoder_gradient, decoder_gradient, input_gradient


def solution(mesh):
    fine = Mesh(mesh.devices.reshape(2, 4, 4, 2, 2), ("zl", "x", "y", "zh", "c"))
    in_specs = (
        P(None, FEAT),
        P(FEAT),
        P(FEAT, MP),
        P(FEAT, MP),
        P(MP, FEAT),
        P(None, ALL),
        P(ALL),
        P(ALL, None),
        P(),
    )
    out_specs = (P(None, ALL), P(ALL, None), P(None, ALL), P(ALL, None), P(ALL, None))
    return jax.shard_map(shards, mesh=fine, in_specs=in_specs, out_specs=out_specs, check_vma=False)
```

time: 188 us -> 173 us (0.920)
  blocking collectives: 95.8 us -> 114 us
  waiting for transfers between devices: 35.7 us -> 18.2 us
  matrix products: 26.1 us -> 17.3 us
  starting transfers between devices: 11.4 us -> 6.07 us
  Pallas kernels: 0 us -> 4.79 us
  local copies, waits for them, and re-layouts: 10.6 us -> 6.85 us
  other arithmetic: 6.53 us -> 4.46 us
    all_to_all x5 -> x6, blocking collectives: 95.8 us -> 114 us  [exchange(): return lax.all_to_all(v, axes, 0, 0, tiled=True)]
    all_to_all x2 -> x1, waiting for transfers between devices: 26 us -> 8.88 us  [exchange(): return lax.all_to_all(v, axes, 0, 0, tiled=True)]
    dot_general x19 -> x12, matrix products: 26.1 us -> 17.3 us  [dot(): lax.dot_general(a, b, (((ca,), (cb,)), ((), ())), preferred_element_type=...]
    reshape x3 -> x1, local copies, waits for them, and re-layouts: 6.83 us -> 0.17 us  [shards(): copies_to(stream_piece, RING + MP, CHIPS).reshape(8, 8 * piece, ROWS)]
    pallas_call x0 -> x8, Pallas kernels: none -> 4.79 us  [local(): pl.pallas_call(kernel, out_shape=[jax.ShapeDtypeStruct(shape, kind) for s...]
    all_to_all x2 -> x1, starting transfers between devices: 10.3 us -> 5.48 us  [exchange(): return lax.all_to_all(v, axes, 0, 0, tiled=True)]
    unnamed x77 -> x53, local copies, waits for them, and re-layouts: 2.84 us -> 4.83 us
    ppermute x7 -> x6, waiting for transfers between devices: 9.7 us -> 9.33 us  [swap(): return lax.ppermute(v, 'c', [(0, 1), (1, 0)])]
  transfers between devices with their start and end apart: 9 -> 7, of which waited for: 8 -> 7; matrix products, arithmetic and copies ran while one was open for 7% -> 7% of each run, Pallas kernels for 0% -> 1%
where the time goes in v5:
time: 173 us; the launch traced here: 172 us
  blocking collectives  114 us (66%)
  waiting for transfers between devices  18.2 us (11%)
  matrix products  17.3 us (10%)
  local copies, waits for them, and re-layouts  6.85 us (4%)
  starting transfers between devices  6.07 us (4%)
  Pallas kernels  4.79 us (3%)
  other arithmetic  4.46 us (3%)
    all_to_all x6, blocking collectives, exchange(): return lax.all_to_all(v, axes, 0, 0, tiled=True)  114 us
    dot_general x12, matrix products, dot(): lax.dot_general(a, b, (((ca,), (cb,)), ((), ())), preferred_element_type=...  17.3 us
    ppermute x6, waiting for transfers between devices, swap(): return lax.ppermute(v, 'c', [(0, 1), (1, 0)])  9.33 us
    all_to_all x1, waiting for transfers between devices, exchange(): return lax.all_to_all(v, axes, 0, 0, tiled=True)  8.88 us
    all_to_all x1, starting transfers between devices, exchange(): return lax.all_to_all(v, axes, 0, 0, tiled=True)  5.48 us
    unnamed x53, local copies, waits for them, and re-layouts  4.83 us
    pallas_call x8, Pallas kernels, local(): pl.pallas_call(kernel, out_shape=[jax.ShapeDtypeStruct(shape, kind) for s...  4.79 us
  transfers between devices with their start and end apart: 7, of which 7 were waited for; matrix products, arithmetic and copies ran while one was open for 7% of the time, Pallas kernels for 1%

profile of v5, /device:TPU:0, one launch (start us, length us, event | category | flops | bytes accessed | tf_op | source)
XLA Modules:
  0.0 172.5 jit_solution(4265988434503860294)
XLA Ops:
  0.6 0.0 copy-start
  0.6 0.0 copy-start.8
  0.7 0.0 copy-start.10
  0.7 1.3 constant_dynamic-update-slice_fusion.1
  2.0 1.2 constant_dynamic-update-slice_fusion.weight
  3.2 0.0 copy-start.7
  3.2 0.9 copy-done.7
  4.1 0.7 copy-done.9
  4.7 0.9 copy-done.11
  5.6 0.7 shard_map.146
  6.3 0.1 collective-permute-start
  6.4 2.5 %collective-permute-done.arrived = bf16[128,3712]{1,0:T(8,128)(2,1)S(1)} collective-permute-done((bf16[128,3712]{1,0:T(8,128)(2,1)S(1)}, bf16[128,3712]{1,0:T(8,128)(2,1)S(1)}, u32[]{:S(2)}, u32[]{:S(2)}) %collective-permute-start) | collective-permute-done | bytes 950304 | tf_op jit(solution)/shard_map/ppermute | solution.py:32
  8.9 0.7 shard_map.147
  9.7 23.9 %all_to_all.35 = bf16[8,16,3712]{2,1,0:T(8,128)(2,1)S(1)} all-to-all(bf16[8,16,3712]{2,1,0:T(8,128)(2,1)S(1)} %bitcast.32), channel_id=1, replica_groups=mesh['zl'=2,'x'=4,'y'=4,'zh'=2,'c'=2] {'y','zh'}, dimensions={0} | all-to-all | bytes 1900544 | tf_op jit(solution)/shard_map/all_to_all | solution.py:36
  33.6 0.1 convert_reduce_fusion
  33.7 0.1 slice_reduce_fusion
  33.8 0.1 slice_multiply_fusion
  34.0 12.6 %all_to_all.36 = bf16[8,16,1792]{2,1,0:T(8,128)(2,1)S(1)} all-to-all(bf16[8,16,1792]{2,1,0:T(8,128)(2,1)S(1)} %broadcast_in_dim.9), channel_id=1, replica_groups=mesh['zl'=2,'x'=4,'y'=4,'zh'=2,'c'=2] {'y','zh'}, dimensions={0} | all-to-all | bytes 917504 | tf_op jit(solution)/shard_map/all_to_all | solution.py:36
  46.6 0.4 fusion.7
  47.0 1.4 collective-permute-done.1
  48.4 0.4 fusion.8
  48.9 11.1 %all_to_all.37 = bf16[8,28,256]{2,1,0:T(8,128)(2,1)S(1)} all-to-all(bf16[8,28,256]{2,1,0:T(8,128)(2,1)S(1)} %maximum_select_fusion.2), channel_id=1, replica_groups=mesh['zl'=2,'x'=4,'y'=4,'zh'=2,'c'=2] {'zl','x'}, dimensions={0} | all-to-all | bytes 229376 | tf_op jit(solution)/shard_map/all_to_all | solution.py:36
  60.1 0.1 broadcast_in_dim.10
  60.2 23.0 %all_to_all.38 = bf16[64,28,256]{2,1,0:T(8,128)(2,1)S(1)} all-to-all(bf16[64,28,256]{2,1,0:T(8,128)(2,1)S(1)} %broadcast_in_dim.10), channel_id=1, replica_groups=mesh['zl'=2,'x'=4,'y'=4,'zh'=2,'c'=2] {'y','zh','zl','x'}, dimensions={0} | all-to-all | bytes 1835008 | tf_op jit(solution)/shard_map/all_to_all | solution.py:36
  83.2 0.2 reshape.42.kept
  83.4 0.0 copy-start.13
  83.4 0.1 collective-permute-start.2
  83.5 2.5 %collective-permute-done.2.other = bf16[8,224,256]{2,1,0:T(8,128)(2,1)S(1)} collective-permute-done((bf16[8,224,256]{2,1,0:T(8,128)(2,1)S(1)}, bf16[8,224,256]{2,1,0:T(8,128)(2,1)S(1)}, u32[]{:S(2)}, u32[]{:S(2)}) %collective-permute-start.2) | collective-permute-done | bytes 917536 | tf_op jit(solution)/shard_map/ppermute | solution.py:32
  85.9 0.1 shard_map.148
  86.1 0.0 copy-start.12
  86.1 2.3 %add_divide_fusion = (f32[256,512]{1,0:T(8,128)S(1)}, bf16[256,512]{1,0:T(8,128)(2,1)S(1)}) fusion(f32[512]{0:T(512)} %param.17, bf16[3584,256]{1,0:T(8,128)(2,1)S(1)} %bitcast.29, bf16[3584,512]{1,0:T(8,128)(2,1)S(1)} %copy-done.13), kind=kOutput, calls=%fused_computation.24 | convolution fusion | flops 940965888 | bytes 6293504 | tf_op jit(solution)/shard_map/dot_general | solution.py:28
  88.4 0.0 copy-start.4
  88.4 0.0 copy-start.24
  88.4 0.7 convolution_convert_fusion.3
  89.1 0.2 collective-permute-start.3
  89.3 0.6 convolution_subtract_fusion
  89.9 0.7 fusion.25.kept
  90.6 1.1 collective-permute-done.3.arrived
  91.7 0.9 shard_map.149
  92.6 21.9 %all_to_all.39 = bf16[64,2,3584]{2,1,0:T(2,128)(2,1)S(1)} all-to-all(bf16[64,2,3584]{2,1,0:T(2,128)(2,1)S(1)} %shard_map.149), channel_id=1, replica_groups=mesh['zl'=2,'x'=4,'y'=4,'zh'=2,'c'=2] {'zl','x','y','zh'}, dimensions={0} | all-to-all | bytes 1835008 | tf_op jit(solution)/shard_map/all_to_all | solution.py:36
  114.4 0.7 convert_reduce_fusion.2
  115.2 0.5 broadcast_in_dim.11
  115.7 21.2 %all_to_all.40.v = bf16[64,2,3584]{2,1,0:T(2,128)(2,1)S(1)} all-to-all(bf16[64,2,3584]{2,1,0:T(2,128)(2,1)S(1)} %broadcast_in_dim.11), channel_id=1, replica_groups=mesh['zl'=2,'x'=4,'y'=4,'zh'=2,'c'=2] {'zl','x','y','zh'}, dimensions={0} | all-to-all | bytes 1835008 | tf_op jit(solution)/shard_map/all_to_all | solution.py:36
  136.9 0.3 shard_map.150
  137.2 1.3 fusion.5
  138.5 0.9 collective-permute-done.4.v
  139.4 0.3 shard_map.151
  139.7 0.0 copy-start.1
  139.7 1.3 fusion.6
  141.0 1.3 convolution_convert_fusion.2
  142.3 0.2 collective-permute-start.5
  142.5 1.3 fusion.26.kept
  143.8 1.0 collective-permute-done.5.arrived
  144.9 0.9 shard_map.152
  145.8 1.0 copy-done.3
  146.7 5.5 %all-to-all-start.6 = ((bf16[64,2,3584]{2,1,0:T(2,128)(2,1)}), bf16[64,2,3584]{2,1,0:T(2,128)(2,1)}, u32[]{:S(2)}, u32[]{:S(2)}) async-start(bf16[64,2,3584]{2,1,0:T(2,128)(2,1)} %copy-done.3), calls=%async_computation.6 | async-start | bytes 1835008 | tf_op jit(solution)/shard_map/all_to_all | solution.py:36
  152.3 4.2 %convolution_convert_fusion = bf16[3584,512]{1,0:T(8,128)(2,1)} fusion(bf16[3584,256]{1,0:T(8,128)(2,1)S(1)} %bitcast.31, bf16[128,512]{1,0:T(8,128)(2,1)} %copy-done.15, bf16[128,512]{1,0:T(8,128)(2,1)} %copy-done.14, pred[]{:T(512)S(6)} %eq.6), kind=kOutput, calls=%fused_computation | convolution fusion | flops 942538752 | bytes 5767169 | tf_op jit(solution)/shard_map/dot_general | solution.py:28
  156.4 0.0 copy-start.6
  156.5 3.0 %convolution_convert_fusion.1 = bf16[512,3584]{1,0:T(8,128)(2,1)} fusion(bf16[128,3584]{1,0:T(8,128)(2,1)S(1)} %copy-done.2, bf16[128,3584]{1,0:T(8,128)(2,1)S(1)} %shard_map.150, bf16[128,512]{1,0:T(8,128)(2,1)S(1)} %copy-done.17, bf16[128,512]{1,0:T(8,128)(2,1)S(1)} %copy-done.19), kind=kOutput, calls=%fused_computation.1 | convolution fusion | flops 945553408 | bytes 5767168 | tf_op jit(solution)/shard_map/dot_general | solution.py:28
  159.5 0.9 shard_map.153
  160.4 0.6 add_convert_fusion.1
  161.0 8.9 %all-to-all-done.6 = bf16[64,2,3584]{2,1,0:T(2,128)(2,1)} async-done(((bf16[64,2,3584]{2,1,0:T(2,128)(2,1)}), bf16[64,2,3584]{2,1,0:T(2,128)(2,1)}, u32[]{:S(2)}, u32[]{:S(2)}) %all-to-all-start.6) | async-done | bytes 917536 | tf_op jit(solution)/shard_map/all_to_all | solution.py:36
  169.9 1.9 %convert_reduce_fusion.1 = f32[2,3584]{1,0:T(2,128)S(1)} fusion(bf16[64,2,3584]{2,1,0:T(2,128)(2,1)} %all-to-all-done.6), kind=kLoop, calls=%fused_computation.9 | loop fusion | flops 910336 | bytes 946176 | tf_op jit(solution)/shard_map/reduce_sum | solution.py:239
  171.9 0.6 convert_subtract_fusion
  (51 shorter events, 0.3 us)
Async XLA Ops:
  0.6 46.0 %copy-start = (bf16[1792,224]{0,1:T(8,128)(2,1)S(1)}, bf16[1792,224]{0,1:T(8,128)(2,1)}, u32[]{:S(2)}) copy-start(bf16[1792,224]{0,1:T(8,128)(2,1)} %param.15) | copy-start | bytes 2408452
  0.6 8.3 %copy-start.8 = (bf16[256,224]{0,1:T(8,128)(2,1)S(1)}, bf16[256,224]{0,1:T(8,128)(2,1)}, u32[]{:S(2)}) copy-start(bf16[256,224]{0,1:T(8,128)(2,1)} %param.11) | copy-start | bytes 344068
  0.7 8.3 %copy-start.10 = (f32[224]{0:T(256)S(1)}, f32[224]{0:T(256)}, u32[]{:S(2)}) copy-start(f32[224]{0:T(256)} %param.12) | copy-start | bytes 2692
  3.2 0.9 copy-start.7
  4.1 0.7 copy-start.9
  4.7 0.9 copy-start.11
  6.3 2.6 %collective-permute-start = (bf16[128,3712]{1,0:T(8,128)(2,1)S(1)}, bf16[128,3712]{1,0:T(8,128)(2,1)S(1)}, u32[]{:S(2)}, u32[]{:S(2)}) collective-permute-start(bf16[128,3712]{1,0:T(8,128)(2,1)S(1)} %get-tuple-element.33), channel_id=1, source_target_pairs={{0,1},{1,0},{2,3},{3,2},{4,5},{5,4},{6,7},{7,6},{8,9},{9,8},{10,11... | collective-permute-start | bytes 2850824 | tf_op jit(solution)/shard_map/ppermute | solution.py:32
  46.6 1.8 %collective-permute-start.1 = (bf16[128,1792]{1,0:T(8,128)(2,1)S(1)}, bf16[128,1792]{1,0:T(8,128)(2,1)S(1)}, u32[]{:S(2)}, u32[]{:S(2)}) collective-permute-start(bf16[128,1792]{1,0:T(8,128)(2,1)S(1)} %bitcast.37), channel_id=1, source_target_pairs={{0,1},{1,0},{2,3},{3,2},{4,5},{5,4},{6,7},{7,6},{8,9},{9,8},{10,11... | collective-permute-start | bytes 1376264 | tf_op jit(solution)/shard_map/ppermute | solution.py:32
  83.4 2.7 %copy-start.13 = (bf16[3584,512]{1,0:T(8,128)(2,1)S(1)}, bf16[3584,512]{1,0:T(8,128)(2,1)}, u32[]{:S(2)}) copy-start(bf16[3584,512]{1,0:T(8,128)(2,1)} %param.16) | copy-start | bytes 11010052
  83.4 2.6 %collective-permute-start.2 = (bf16[8,224,256]{2,1,0:T(8,128)(2,1)S(1)}, bf16[8,224,256]{2,1,0:T(8,128)(2,1)S(1)}, u32[]{:S(2)}, u32[]{:S(2)}) collective-permute-start(bf16[8,224,256]{2,1,0:T(8,128)(2,1)S(1)} %reshape.42.kept), channel_id=1, source_target_pairs={{0,1},{1,0},{2,3},{3,2},{4,5},{5,4},{6,7},{7,6},{8,9},{9,8},{10,11... | collective-permute-start | bytes 2752520 | tf_op jit(solution)/shard_map/ppermute | solution.py:32
  86.1 2.4 %copy-start.12 = (bf16[512,3584]{1,0:T(8,128)(2,1)S(1)}, bf16[512,3584]{1,0:T(8,128)(2,1)}, u32[]{:S(2)}) copy-start(bf16[512,3584]{1,0:T(8,128)(2,1)} %param.18) | copy-start | bytes 11010052
  88.4 1.5 copy-start.4
  88.4 1.0 copy-start.24
  88.4 2.2 %copy-start.16 = (bf16[128,512]{1,0:T(8,128)(2,1)}, bf16[128,512]{1,0:T(8,128)(2,1)S(1)}, u32[]{:S(2)}) copy-start(bf16[128,512]{1,0:T(8,128)(2,1)S(1)} %get-tuple-element.41) | copy-start | bytes 393220
  88.4 2.2 %copy-start.18 = (bf16[128,512]{1,0:T(8,128)(2,1)}, bf16[128,512]{1,0:T(8,128)(2,1)S(1)}, u32[]{:S(2)}) copy-start(bf16[128,512]{1,0:T(8,128)(2,1)S(1)} %get-tuple-element.40) | copy-start | bytes 393220
  89.1 2.6 %collective-permute-start.3 = (bf16[128,3584]{1,0:T(8,128)(2,1)S(1)}, bf16[128,3584]{1,0:T(8,128)(2,1)S(1)}, u32[]{:S(2)}, u32[]{:S(2)}) collective-permute-start(bf16[128,3584]{1,0:T(8,128)(2,1)S(1)} %convolution_convert_fusion.3), channel_id=1, source_target_pairs={{0,1},{1,0},{2,3},{3,2},{4,5},{5,4},{6,7},{7,6},{8,9},{9,8},{10,11... | collective-permute-start | bytes 2752520 | tf_op jit(solution)/shard_map/ppermute | solution.py:32
  115.2 22.0 %copy-start.20 = (f32[2,3584]{1,0:T(2,128)}, f32[2,3584]{1,0:T(2,128)S(1)}, u32[]{:S(2)}) copy-start(f32[2,3584]{1,0:T(2,128)S(1)} %convert_reduce_fusion.2) | copy-start | bytes 86020
  115.2 22.0 %copy-start.22 = (bf16[2,3584]{1,0:T(2,128)(2,1)}, bf16[2,3584]{1,0:T(2,128)(2,1)S(1)}, u32[]{:S(2)}) copy-start(bf16[2,3584]{1,0:T(2,128)(2,1)S(1)} %add_convert_fusion.2) | copy-start | bytes 43012
  136.9 2.5 %collective-permute-start.4 = (bf16[64,2,3584]{2,1,0:T(2,128)(2,1)S(1)}, bf16[64,2,3584]{2,1,0:T(2,128)(2,1)S(1)}, u32[]{:S(2)}, u32[]{:S(2)}) collective-permute-start(bf16[64,2,3584]{2,1,0:T(2,128)(2,1)S(1)} %all_to_all.40.v), channel_id=1, source_target_pairs={{0,1},{1,0},{2,3},{3,2},{4,5},{5,4},{6,7},{7,6},{8,9},{9,8},{10,11... | collective-permute-start | bytes 2752520 | tf_op jit(solution)/shard_map/ppermute | solution.py:32
  138.5 4.0 %copy-start.14 = (bf16[128,512]{1,0:T(8,128)(2,1)}, bf16[128,512]{1,0:T(8,128)(2,1)S(1)}, u32[]{:S(2)}) copy-start(bf16[128,512]{1,0:T(8,128)(2,1)S(1)} %fusion.5) | copy-start | bytes 393220
  139.7 2.6 %copy-start.1 = (bf16[128,3584]{1,0:T(8,128)(2,1)}, bf16[128,3584]{1,0:T(8,128)(2,1)S(1)}, u32[]{:S(2)}) copy-start(bf16[128,3584]{1,0:T(8,128)(2,1)S(1)} %shard_map.151) | copy-start | bytes 2752516
  141.0 2.9 %copy-start.15 = (bf16[128,512]{1,0:T(8,128)(2,1)}, bf16[128,512]{1,0:T(8,128)(2,1)S(1)}, u32[]{:S(2)}) copy-start(bf16[128,512]{1,0:T(8,128)(2,1)S(1)} %fusion.6) | copy-start | bytes 393220
  142.3 2.6 %collective-permute-start.5 = (bf16[128,3584]{1,0:T(8,128)(2,1)S(1)}, bf16[128,3584]{1,0:T(8,128)(2,1)S(1)}, u32[]{:S(2)}, u32[]{:S(2)}) collective-permute-start(bf16[128,3584]{1,0:T(8,128)(2,1)S(1)} %convolution_convert_fusion.2), channel_id=1, source_target_pairs={{0,1},{1,0},{2,3},{3,2},{4,5},{5,4},{6,7},{7,6},{8,9},{9,8},{10,11... | collective-permute-start | bytes 2752520 | tf_op jit(solution)/shard_map/ppermute | solution.py:32
  145.8 1.0 copy-start.3
  146.7 23.2 %all-to-all-start.6 = ((bf16[64,2,3584]{2,1,0:T(2,128)(2,1)}), bf16[64,2,3584]{2,1,0:T(2,128)(2,1)}, u32[]{:S(2)}, u32[]{:S(2)}) async-start(bf16[64,2,3584]{2,1,0:T(2,128)(2,1)} %copy-done.3), calls=%async_computation.6 | async-start | bytes 1835008 | tf_op jit(solution)/shard_map/all_to_all | solution.py:36
  152.2 4.2 %copy-start.2 = (bf16[128,3584]{1,0:T(8,128)(2,1)S(1)}, bf16[128,3584]{1,0:T(8,128)(2,1)}, u32[]{:S(2)}) copy-start(bf16[128,3584]{1,0:T(8,128)(2,1)} %copy-done.1) | copy-start | bytes 2752516
  152.2 4.2 %copy-start.17 = (bf16[128,512]{1,0:T(8,128)(2,1)S(1)}, bf16[128,512]{1,0:T(8,128)(2,1)}, u32[]{:S(2)}) copy-start(bf16[128,512]{1,0:T(8,128)(2,1)} %copy-done.16) | copy-start | bytes 393220
  152.2 4.2 %copy-start.19 = (bf16[128,512]{1,0:T(8,128)(2,1)S(1)}, bf16[128,512]{1,0:T(8,128)(2,1)}, u32[]{:S(2)}) copy-start(bf16[128,512]{1,0:T(8,128)(2,1)} %copy-done.18) | copy-start | bytes 393220
  156.4 3.0 %copy-start.5 = (bf16[256,512]{1,0:T(8,128)(2,1)S(1)}, bf16[256,512]{1,0:T(8,128)(2,1)}, u32[]{:S(2)}) copy-start(bf16[256,512]{1,0:T(8,128)(2,1)} %copy-done.4) | copy-start | bytes 786436
  156.4 3.0 %copy-start.6 = (bf16[256,256]{1,0:T(8,128)(2,1)S(1)}, bf16[256,256]{1,0:T(8,128)(2,1)}, u32[]{:S(2)}) copy-start(bf16[256,256]{1,0:T(8,128)(2,1)} %constant.55.clone.rows) | copy-start | bytes 393220
  156.5 4.0 %copy-start.21 = (f32[2,3584]{1,0:T(2,128)S(1)}, f32[2,3584]{1,0:T(2,128)}, u32[]{:S(2)}) copy-start(f32[2,3584]{1,0:T(2,128)} %copy-done.20) | copy-start | bytes 86020
  156.5 4.0 %copy-start.25 = (f32[3584]{0:T(1024)S(1)}, f32[3584]{0:T(1024)}, u32[]{:S(2)}) copy-start(f32[3584]{0:T(1024)} %param.19) | copy-start | bytes 43012
  156.5 15.4 %copy-start.23 = (bf16[2,3584]{1,0:T(2,128)(2,1)S(1)}, bf16[2,3584]{1,0:T(2,128)(2,1)}, u32[]{:S(2)}) copy-start(bf16[2,3584]{1,0:T(2,128)(2,1)} %copy-done.22) | copy-start | bytes 43012

commit v6 on v5

--- a/solution.py
+++ b/solution.py
@@ -66,18 +66,6 @@
     return (row == (at // 2) * 4 + core * 2 + at % 2).astype(bf16)
 
 
-def scaled_rows(source, gain, picked):
-    size = source.shape[0]
-    same = lax.broadcasted_iota(jnp.int32, (size, size), 0) == lax.broadcasted_iota(jnp.int32, (size, size), 1)
-    column = jnp.sum(jnp.where(same, gain[...], 0.0), axis=1, keepdims=True)
-    rows = dot(source[...], picked, 1, 0)
-    squared = rows * rows
-    high = squared.astype(bf16)
-    low = (squared - high.astype(f32)).astype(bf16)
-    ones = jnp.ones((size, 128), bf16)
-    return (rows * column).astype(bf16), dot(high, ones, 0, 0) + dot(low, ones, 0, 0)
-
-
 def assemble(kept, other, out):
     core = lax.axis_index("c")
     for k in range(kept.shape[0]):
@@ -100,22 +88,39 @@
         out[:, :, at : at + 512] = term.reshape(CHIPS, 2, 512).astype(bf16)
 
 
-def project_other(source, gain, weight, order, sent, ordered):
-    ordered[...] = dot(source[...], order[...], 1, 1).astype(bf16)
-    scaled, squares = scaled_rows(source, gain, rows_of(1 - lax.axis_index("c")))
+def square_sums(rows):
+    squared = rows * rows
+    high = squared.astype(bf16)
+    low = (squared - high.astype(f32)).astype(bf16)
+    ones = jnp.ones((rows.shape[0], 128), bf16)
+    return dot(high, ones, 0, 0) + dot(low, ones, 0, 0)
+
+
+def project_other(source, gain, weight, sent, ordered, scaled, squares):
+    size = source.shape[0]
+    same = lax.broadcasted_iota(jnp.int32, (size, size), 0) == lax.broadcasted_iota(jnp.int32, (size, size), 1)
+    column = jnp.sum(jnp.where(same, gain[...], 0.0), axis=1, keepdims=True)
+    zero, one = dot(source[...], rows_of(0), 1, 0), dot(source[...], rows_of(1), 1, 0)
+    ordered[:, :HALF] = zero.astype(bf16)
+    ordered[:, HALF:] = one.astype(bf16)
+    first = lax.axis_index("c") == 0
+    kept, other = jnp.where(first, zero, one), jnp.where(first, one, zero)
+    scaled[...] = (kept * column).astype(bf16)
+    squares[...] = square_sums(kept)
+    other_scaled = (other * column).astype(bf16)
     columns = weight.shape[1]
     for at in range(0, columns, 512):
-        sent[:, at : at + 512] = dot(scaled, weight[:, at : at + 512], 0, 0).astype(bf16)
-    sent[:, columns:] = three(squares)
-
-
-def project_kept(source, gain, weight, arrived, out):
-    scaled, squares = scaled_rows(source, gain, rows_of(lax.axis_index("c")))
+        sent[:, at : at + 512] = dot(other_scaled, weight[:, at : at + 512], 0, 0).astype(bf16)
+    sent[:, columns:] = three(square_sums(other))
+
+
+def project_kept(scaled, squares, weight, arrived, out):
     columns = weight.shape[1]
     for at in range(0, columns, 512):
-        term = dot(scaled, weight[:, at : at + 512], 0, 0)
+        term = dot(scaled[...], weight[:, at : at + 512], 0, 0)
         out[:, at : at + 512] = (term + arrived[:, at : at + 512].astype(f32)).astype(bf16)
-    out[:, columns:] = three(squares + jnp.sum(arrived[:, columns:].astype(f32), axis=1, keepdims=True))
+    more = jnp.sum(arrived[:, columns:].astype(f32), axis=1, keepdims=True)
+    out[:, columns:] = three(squares[...] + more)
 
 
 def shards(
@@ -146,18 +151,16 @@
 
     at = np.arange(ROWS)
     place = (at % HALF) // 2 * 4 + at // HALF * 2 + at % 2
-    order = jnp.asarray(np.eye(ROWS)[place], bf16)
-
     joint_weight = jnp.concatenate([gate_weight, up_weight], axis=1)
-    operands = [residual_in.T, norm_gain[None, :], joint_weight]
     payload = [((HALF, joint_weight.shape[1] + 128), bf16)]
-    sent, ordered = local(
+    columns = residual_in.shape[1]
+    sent, ordered, scaled, squares = local(
         project_other,
-        payload + [(operands[0].shape, bf16)],
-        operands + [order],
+        payload + [((columns, ROWS), bf16), ((columns, HALF), bf16), ((HALF, 128), f32)],
+        [residual_in.T, norm_gain[None, :], joint_weight],
         10**9,
     )
-    (both,) = local(project_kept, payload, operands + [swap(sent)], 10**9)
+    (both,) = local(project_kept, payload, [scaled, squares, joint_weight, swap(sent)], 10**9)
     both = exchange(both.reshape(8, 16, both.shape[1]), RING)
     projected = jnp.sum(both.astype(f32), axis=0)
     mean = jnp.sum(projected[:, 2 * hidden_local :], axis=1, keepdims=True) / D

time: 173 us -> 172 us (level)
    unnamed x53 -> x47, local copies, waits for them, and re-layouts: 4.83 us -> 3.9 us
where the time goes in v6:
time: 172 us; the launch traced here: 171 us
  blocking collectives  114 us (66%)
  waiting for transfers between devices  18.2 us (11%)
  matrix products  17.3 us (10%)
  starting transfers between devices  6.07 us (4%)
  local copies, waits for them, and re-layouts  5.92 us (3%)
  Pallas kernels  4.53 us (3%)
  other arithmetic  4.46 us (3%)
    all_to_all x6, blocking collectives, exchange(): return lax.all_to_all(v, axes, 0, 0, tiled=True)  114 us
    dot_general x12, matrix products, dot(): lax.dot_general(a, b, (((ca,), (cb,)), ((), ())), preferred_element_type=...  17.3 us
    ppermute x6, waiting for transfers between devices, swap(): return lax.ppermute(v, 'c', [(0, 1), (1, 0)])  9.32 us
    all_to_all x1, waiting for transfers between devices, exchange(): return lax.all_to_all(v, axes, 0, 0, tiled=True)  8.88 us
    all_to_all x1, starting transfers between devices, exchange(): return lax.all_to_all(v, axes, 0, 0, tiled=True)  5.48 us
    pallas_call x8, Pallas kernels, local(): pl.pallas_call(kernel, out_shape=[jax.ShapeDtypeStruct(shape, kind) for s...  4.53 us
    unnamed x47, local copies, waits for them, and re-layouts  3.9 us
  transfers between devices with their start and end apart: 7, of which 7 were waited for; matrix products, arithmetic and copies ran while one was open for 7% of the time, Pallas kernels for 1%

profile of v6, /device:TPU:0, one launch (start us, length us, event | category | flops | bytes accessed | tf_op | source)
XLA Modules:
  0.0 171.3 jit_solution(13390837693691563712)
XLA Ops:
  0.6 0.0 copy-start
  0.7 1.3 constant_dynamic-update-slice_fusion.1
  1.9 1.2 constant_dynamic-update-slice_fusion.weight
  3.1 0.0 copy-start.7
  3.1 0.9 copy-done.7
  4.0 0.7 copy-done.8
  4.7 0.7 shard_map.137
  5.4 0.1 collective-permute-start
  5.5 2.5 %collective-permute-done.arrived = bf16[128,3712]{1,0:T(8,128)(2,1)S(1)} collective-permute-done((bf16[128,3712]{1,0:T(8,128)(2,1)S(1)}, bf16[128,3712]{1,0:T(8,128)(2,1)S(1)}, u32[]{:S(2)}, u32[]{:S(2)}) %collective-permute-start) | collective-permute-done | bytes 950304 | tf_op jit(solution)/shard_map/ppermute | solution.py:32
  8.0 0.4 shard_map.138
  8.5 23.9 %all_to_all.35 = bf16[8,16,3712]{2,1,0:T(8,128)(2,1)S(1)} all-to-all(bf16[8,16,3712]{2,1,0:T(8,128)(2,1)S(1)} %bitcast.32), channel_id=1, replica_groups=mesh['zl'=2,'x'=4,'y'=4,'zh'=2,'c'=2] {'y','zh'}, dimensions={0} | all-to-all | bytes 1900544 | tf_op jit(solution)/shard_map/all_to_all | solution.py:36
  32.4 0.1 convert_reduce_fusion
  32.5 0.1 slice_reduce_fusion
  32.6 0.1 slice_multiply_fusion
  32.8 12.6 %all_to_all.36 = bf16[8,16,1792]{2,1,0:T(8,128)(2,1)S(1)} all-to-all(bf16[8,16,1792]{2,1,0:T(8,128)(2,1)S(1)} %broadcast_in_dim.9), channel_id=1, replica_groups=mesh['zl'=2,'x'=4,'y'=4,'zh'=2,'c'=2] {'y','zh'}, dimensions={0} | all-to-all | bytes 917504 | tf_op jit(solution)/shard_map/all_to_all | solution.py:36
  45.4 0.4 fusion.7
  45.8 1.4 collective-permute-done.1
  47.2 0.4 fusion.8
  47.7 11.1 %all_to_all.37 = bf16[8,28,256]{2,1,0:T(8,128)(2,1)S(1)} all-to-all(bf16[8,28,256]{2,1,0:T(8,128)(2,1)S(1)} %maximum_select_fusion.2), channel_id=1, replica_groups=mesh['zl'=2,'x'=4,'y'=4,'zh'=2,'c'=2] {'zl','x'}, dimensions={0} | all-to-all | bytes 229376 | tf_op jit(solution)/shard_map/all_to_all | solution.py:36
  58.9 0.1 broadcast_in_dim.10
  59.0 23.0 %all_to_all.38 = bf16[64,28,256]{2,1,0:T(8,128)(2,1)S(1)} all-to-all(bf16[64,28,256]{2,1,0:T(8,128)(2,1)S(1)} %broadcast_in_dim.10), channel_id=1, replica_groups=mesh['zl'=2,'x'=4,'y'=4,'zh'=2,'c'=2] {'y','zh','zl','x'}, dimensions={0} | all-to-all | bytes 1835008 | tf_op jit(solution)/shard_map/all_to_all | solution.py:36
  82.0 0.2 reshape.42.kept
  82.2 0.0 copy-start.10
  82.2 0.1 collective-permute-start.2
  82.3 2.5 %collective-permute-done.2.other = bf16[8,224,256]{2,1,0:T(8,128)(2,1)S(1)} collective-permute-done((bf16[8,224,256]{2,1,0:T(8,128)(2,1)S(1)}, bf16[8,224,256]{2,1,0:T(8,128)(2,1)S(1)}, u32[]{:S(2)}, u32[]{:S(2)}) %collective-permute-start.2) | collective-permute-done | bytes 917536 | tf_op jit(solution)/shard_map/ppermute | solution.py:32
  84.7 0.1 shard_map.139
  84.9 0.0 copy-start.9
  84.9 2.3 %add_divide_fusion = (f32[256,512]{1,0:T(8,128)S(1)}, bf16[256,512]{1,0:T(8,128)(2,1)S(1)}) fusion(f32[512]{0:T(512)} %param.16, bf16[3584,256]{1,0:T(8,128)(2,1)S(1)} %bitcast.29, bf16[3584,512]{1,0:T(8,128)(2,1)S(1)} %copy-done.10), kind=kOutput, calls=%fused_computation.24 | convolution fusion | flops 940965888 | bytes 6293504 | tf_op jit(solution)/shard_map/dot_general | solution.py:28
  87.1 0.0 copy-start.4
  87.2 0.0 copy-start.21
  87.2 0.7 convolution_convert_fusion.3
  87.9 0.2 collective-permute-start.3
  88.1 0.6 convolution_subtract_fusion
  88.7 0.7 fusion.25.kept
  89.4 1.1 collective-permute-done.3.arrived
  90.4 0.9 shard_map.140
  91.3 21.9 %all_to_all.39 = bf16[64,2,3584]{2,1,0:T(2,128)(2,1)S(1)} all-to-all(bf16[64,2,3584]{2,1,0:T(2,128)(2,1)S(1)} %shard_map.140), channel_id=1, replica_groups=mesh['zl'=2,'x'=4,'y'=4,'zh'=2,'c'=2] {'zl','x','y','zh'}, dimensions={0} | all-to-all | bytes 1835008 | tf_op jit(solution)/shard_map/all_to_all | solution.py:36
  113.2 0.7 convert_reduce_fusion.2
  114.0 0.5 broadcast_in_dim.11
  114.5 21.2 %all_to_all.40.v = bf16[64,2,3584]{2,1,0:T(2,128)(2,1)S(1)} all-to-all(bf16[64,2,3584]{2,1,0:T(2,128)(2,1)S(1)} %broadcast_in_dim.11), channel_id=1, replica_groups=mesh['zl'=2,'x'=4,'y'=4,'zh'=2,'c'=2] {'zl','x','y','zh'}, dimensions={0} | all-to-all | bytes 1835008 | tf_op jit(solution)/shard_map/all_to_all | solution.py:36
  135.7 0.3 shard_map.141
  136.0 1.3 fusion.5
  137.3 0.9 collective-permute-done.4.v
  138.2 0.3 shard_map.142
  138.4 0.0 copy-start.1
  138.5 1.3 fusion.6
  139.8 1.3 convolution_convert_fusion.2
  141.1 0.2 collective-permute-start.5
  141.3 1.3 fusion.26.kept
  142.6 1.0 collective-permute-done.5.arrived
  143.7 0.9 shard_map.143
  144.6 1.0 copy-done.3
  145.5 5.5 %all-to-all-start.6 = ((bf16[64,2,3584]{2,1,0:T(2,128)(2,1)}), bf16[64,2,3584]{2,1,0:T(2,128)(2,1)}, u32[]{:S(2)}, u32[]{:S(2)}) async-start(bf16[64,2,3584]{2,1,0:T(2,128)(2,1)} %copy-done.3), calls=%async_computation.6 | async-start | bytes 1835008 | tf_op jit(solution)/shard_map/all_to_all | solution.py:36
  151.0 0.0 copy-start.2
  151.0 4.2 %convolution_convert_fusion = bf16[3584,512]{1,0:T(8,128)(2,1)} fusion(bf16[3584,256]{1,0:T(8,128)(2,1)S(1)} %bitcast.31, bf16[128,512]{1,0:T(8,128)(2,1)} %copy-done.12, bf16[128,512]{1,0:T(8,128)(2,1)} %copy-done.11, pred[]{:T(512)S(6)} %eq.6), kind=kOutput, calls=%fused_computation | convolution fusion | flops 942538752 | bytes 5767169 | tf_op jit(solution)/shard_map/dot_general | solution.py:28
  155.2 0.0 copy-start.5
  155.2 0.0 copy-start.6
  155.2 0.0 copy-start.18
  155.3 3.0 %convolution_convert_fusion.1 = bf16[512,3584]{1,0:T(8,128)(2,1)} fusion(bf16[128,3584]{1,0:T(8,128)(2,1)S(1)} %copy-done.2, bf16[128,3584]{1,0:T(8,128)(2,1)S(1)} %shard_map.141, bf16[128,512]{1,0:T(8,128)(2,1)S(1)} %copy-done.14, bf16[128,512]{1,0:T(8,128)(2,1)S(1)} %copy-done.16), kind=kOutput, calls=%fused_computation.1 | convolution fusion | flops 945553408 | bytes 5767168 | tf_op jit(solution)/shard_map/dot_general | solution.py:28
  158.3 0.9 shard_map.144
  159.2 0.6 add_convert_fusion.1
  159.8 8.9 %all-to-all-done.6 = bf16[64,2,3584]{2,1,0:T(2,128)(2,1)} async-done(((bf16[64,2,3584]{2,1,0:T(2,128)(2,1)}), bf16[64,2,3584]{2,1,0:T(2,128)(2,1)}, u32[]{:S(2)}, u32[]{:S(2)}) %all-to-all-start.6) | async-done | bytes 917536 | tf_op jit(solution)/shard_map/all_to_all | solution.py:36
  168.7 1.9 %convert_reduce_fusion.1 = f32[2,3584]{1,0:T(2,128)S(1)} fusion(bf16[64,2,3584]{2,1,0:T(2,128)(2,1)} %all-to-all-done.6), kind=kLoop, calls=%fused_computation.9 | loop fusion | flops 910336 | bytes 946176 | tf_op jit(solution)/shard_map/reduce_sum | solution.py:242
  170.6 0.6 convert_subtract_fusion
  (45 shorter events, 0.3 us)
Async XLA Ops:
  0.6 44.8 %copy-start = (bf16[1792,224]{0,1:T(8,128)(2,1)S(1)}, bf16[1792,224]{0,1:T(8,128)(2,1)}, u32[]{:S(2)}) copy-start(bf16[1792,224]{0,1:T(8,128)(2,1)} %param.14) | copy-start | bytes 2408452
  3.1 0.9 copy-start.7
  4.0 0.7 copy-start.8
  5.4 2.6 %collective-permute-start = (bf16[128,3712]{1,0:T(8,128)(2,1)S(1)}, bf16[128,3712]{1,0:T(8,128)(2,1)S(1)}, u32[]{:S(2)}, u32[]{:S(2)}) collective-permute-start(bf16[128,3712]{1,0:T(8,128)(2,1)S(1)} %get-tuple-element.37), channel_id=1, source_target_pairs={{0,1},{1,0},{2,3},{3,2},{4,5},{5,4},{6,7},{7,6},{8,9},{9,8},{10,11... | collective-permute-start | bytes 2850824 | tf_op jit(solution)/shard_map/ppermute | solution.py:32
  45.4 1.8 %collective-permute-start.1 = (bf16[128,1792]{1,0:T(8,128)(2,1)S(1)}, bf16[128,1792]{1,0:T(8,128)(2,1)S(1)}, u32[]{:S(2)}, u32[]{:S(2)}) collective-permute-start(bf16[128,1792]{1,0:T(8,128)(2,1)S(1)} %bitcast.35), channel_id=1, source_target_pairs={{0,1},{1,0},{2,3},{3,2},{4,5},{5,4},{6,7},{7,6},{8,9},{9,8},{10,11... | collective-permute-start | bytes 1376264 | tf_op jit(solution)/shard_map/ppermute | solution.py:32
  82.2 2.7 %copy-start.10 = (bf16[3584,512]{1,0:T(8,128)(2,1)S(1)}, bf16[3584,512]{1,0:T(8,128)(2,1)}, u32[]{:S(2)}) copy-start(bf16[3584,512]{1,0:T(8,128)(2,1)} %param.15) | copy-start | bytes 11010052
  82.2 2.6 %collective-permute-start.2 = (bf16[8,224,256]{2,1,0:T(8,128)(2,1)S(1)}, bf16[8,224,256]{2,1,0:T(8,128)(2,1)S(1)}, u32[]{:S(2)}, u32[]{:S(2)}) collective-permute-start(bf16[8,224,256]{2,1,0:T(8,128)(2,1)S(1)} %reshape.42.kept), channel_id=1, source_target_pairs={{0,1},{1,0},{2,3},{3,2},{4,5},{5,4},{6,7},{7,6},{8,9},{9,8},{10,11... | collective-permute-start | bytes 2752520 | tf_op jit(solution)/shard_map/ppermute | solution.py:32
  84.9 2.4 %copy-start.9 = (bf16[512,3584]{1,0:T(8,128)(2,1)S(1)}, bf16[512,3584]{1,0:T(8,128)(2,1)}, u32[]{:S(2)}) copy-start(bf16[512,3584]{1,0:T(8,128)(2,1)} %param.17) | copy-start | bytes 11010052
  87.1 1.6 copy-start.4
  87.2 1.0 copy-start.21
  87.2 2.2 %copy-start.13 = (bf16[128,512]{1,0:T(8,128)(2,1)}, bf16[128,512]{1,0:T(8,128)(2,1)S(1)}, u32[]{:S(2)}) copy-start(bf16[128,512]{1,0:T(8,128)(2,1)S(1)} %get-tuple-element.45) | copy-start | bytes 393220
  87.2 2.2 %copy-start.15 = (bf16[128,512]{1,0:T(8,128)(2,1)}, bf16[128,512]{1,0:T(8,128)(2,1)S(1)}, u32[]{:S(2)}) copy-start(bf16[128,512]{1,0:T(8,128)(2,1)S(1)} %get-tuple-element.44) | copy-start | bytes 393220
  87.9 2.6 %collective-permute-start.3 = (bf16[128,3584]{1,0:T(8,128)(2,1)S(1)}, bf16[128,3584]{1,0:T(8,128)(2,1)S(1)}, u32[]{:S(2)}, u32[]{:S(2)}) collective-permute-start(bf16[128,3584]{1,0:T(8,128)(2,1)S(1)} %convolution_convert_fusion.3), channel_id=1, source_target_pairs={{0,1},{1,0},{2,3},{3,2},{4,5},{5,4},{6,7},{7,6},{8,9},{9,8},{10,11... | collective-permute-start | bytes 2752520 | tf_op jit(solution)/shard_map/ppermute | solution.py:32
  114.0 22.0 %copy-start.17 = (f32[2,3584]{1,0:T(2,128)}, f32[2,3584]{1,0:T(2,128)S(1)}, u32[]{:S(2)}) copy-start(f32[2,3584]{1,0:T(2,128)S(1)} %convert_reduce_fusion.2) | copy-start | bytes 86020
  114.0 22.0 %copy-start.19 = (bf16[2,3584]{1,0:T(2,128)(2,1)}, bf16[2,3584]{1,0:T(2,128)(2,1)S(1)}, u32[]{:S(2)}) copy-start(bf16[2,3584]{1,0:T(2,128)(2,1)S(1)} %add_convert_fusion.2) | copy-start | bytes 43012
  135.7 2.5 %collective-permute-start.4 = (bf16[64,2,3584]{2,1,0:T(2,128)(2,1)S(1)}, bf16[64,2,3584]{2,1,0:T(2,128)(2,1)S(1)}, u32[]{:S(2)}, u32[]{:S(2)}) collective-permute-start(bf16[64,2,3584]{2,1,0:T(2,128)(2,1)S(1)} %all_to_all.40.v), channel_id=1, source_target_pairs={{0,1},{1,0},{2,3},{3,2},{4,5},{5,4},{6,7},{7,6},{8,9},{9,8},{10,11... | collective-permute-start | bytes 2752520 | tf_op jit(solution)/shard_map/ppermute | solution.py:32
  137.3 4.0 %copy-start.11 = (bf16[128,512]{1,0:T(8,128)(2,1)}, bf16[128,512]{1,0:T(8,128)(2,1)S(1)}, u32[]{:S(2)}) copy-start(bf16[128,512]{1,0:T(8,128)(2,1)S(1)} %fusion.5) | copy-start | bytes 393220
  138.4 2.6 %copy-start.1 = (bf16[128,3584]{1,0:T(8,128)(2,1)}, bf16[128,3584]{1,0:T(8,128)(2,1)S(1)}, u32[]{:S(2)}) copy-start(bf16[128,3584]{1,0:T(8,128)(2,1)S(1)} %shard_map.142) | copy-start | bytes 2752516
  139.8 2.9 %copy-start.12 = (bf16[128,512]{1,0:T(8,128)(2,1)}, bf16[128,512]{1,0:T(8,128)(2,1)S(1)}, u32[]{:S(2)}) copy-start(bf16[128,512]{1,0:T(8,128)(2,1)S(1)} %fusion.6) | copy-start | bytes 393220
  141.1 2.6 %collective-permute-start.5 = (bf16[128,3584]{1,0:T(8,128)(2,1)S(1)}, bf16[128,3584]{1,0:T(8,128)(2,1)S(1)}, u32[]{:S(2)}, u32[]{:S(2)}) collective-permute-start(bf16[128,3584]{1,0:T(8,128)(2,1)S(1)} %convolution_convert_fusion.2), channel_id=1, source_target_pairs={{0,1},{1,0},{2,3},{3,2},{4,5},{5,4},{6,7},{7,6},{8,9},{9,8},{10,11... | collective-permute-start | bytes 2752520 | tf_op jit(solution)/shard_map/ppermute | solution.py:32
  144.6 1.0 copy-start.3
  145.5 23.2 %all-to-all-start.6 = ((bf16[64,2,3584]{2,1,0:T(2,128)(2,1)}), bf16[64,2,3584]{2,1,0:T(2,128)(2,1)}, u32[]{:S(2)}, u32[]{:S(2)}) async-start(bf16[64,2,3584]{2,1,0:T(2,128)(2,1)} %copy-done.3), calls=%async_computation.6 | async-start | bytes 1835008 | tf_op jit(solution)/shard_map/all_to_all | solution.py:36
  151.0 4.2 %copy-start.2 = (bf16[128,3584]{1,0:T(8,128)(2,1)S(1)}, bf16[128,3584]{1,0:T(8,128)(2,1)}, u32[]{:S(2)}) copy-start(bf16[128,3584]{1,0:T(8,128)(2,1)} %copy-done.1) | copy-start | bytes 2752516
  151.0 4.2 %copy-start.14 = (bf16[128,512]{1,0:T(8,128)(2,1)S(1)}, bf16[128,512]{1,0:T(8,128)(2,1)}, u32[]{:S(2)}) copy-start(bf16[128,512]{1,0:T(8,128)(2,1)} %copy-done.13) | copy-start | bytes 393220
  151.0 4.2 %copy-start.16 = (bf16[128,512]{1,0:T(8,128)(2,1)S(1)}, bf16[128,512]{1,0:T(8,128)(2,1)}, u32[]{:S(2)}) copy-start(bf16[128,512]{1,0:T(8,128)(2,1)} %copy-done.15) | copy-start | bytes 393220
  155.2 3.0 %copy-start.5 = (bf16[256,512]{1,0:T(8,128)(2,1)S(1)}, bf16[256,512]{1,0:T(8,128)(2,1)}, u32[]{:S(2)}) copy-start(bf16[256,512]{1,0:T(8,128)(2,1)} %copy-done.4) | copy-start | bytes 786436
  155.2 3.0 %copy-start.6 = (bf16[256,256]{1,0:T(8,128)(2,1)S(1)}, bf16[256,256]{1,0:T(8,128)(2,1)}, u32[]{:S(2)}) copy-start(bf16[256,256]{1,0:T(8,128)(2,1)} %constant.52.clone.rows) | copy-start | bytes 393220
  155.2 4.0 %copy-start.18 = (f32[2,3584]{1,0:T(2,128)S(1)}, f32[2,3584]{1,0:T(2,128)}, u32[]{:S(2)}) copy-start(f32[2,3584]{1,0:T(2,128)} %copy-done.17) | copy-start | bytes 86020
  155.3 4.0 %copy-start.22 = (f32[3584]{0:T(1024)S(1)}, f32[3584]{0:T(1024)}, u32[]{:S(2)}) copy-start(f32[3584]{0:T(1024)} %param.18) | copy-start | bytes 43012
  155.3 15.4 %copy-start.20 = (bf16[2,3584]{1,0:T(2,128)(2,1)S(1)}, bf16[2,3584]{1,0:T(2,128)(2,1)}, u32[]{:S(2)}) copy-start(bf16[2,3584]{1,0:T(2,128)(2,1)} %copy-done.19) | copy-start | bytes 43012

commit v7 on v6

--- a/solution.py
+++ b/solution.py
@@ -96,18 +96,15 @@
     return dot(high, ones, 0, 0) + dot(low, ones, 0, 0)
 
 
-def project_other(source, gain, weight, sent, ordered, scaled, squares):
-    size = source.shape[0]
-    same = lax.broadcasted_iota(jnp.int32, (size, size), 0) == lax.broadcasted_iota(jnp.int32, (size, size), 1)
-    column = jnp.sum(jnp.where(same, gain[...], 0.0), axis=1, keepdims=True)
+def project_other(source, weight, sent, ordered, scaled, squares):
     zero, one = dot(source[...], rows_of(0), 1, 0), dot(source[...], rows_of(1), 1, 0)
     ordered[:, :HALF] = zero.astype(bf16)
     ordered[:, HALF:] = one.astype(bf16)
     first = lax.axis_index("c") == 0
     kept, other = jnp.where(first, zero, one), jnp.where(first, one, zero)
-    scaled[...] = (kept * column).astype(bf16)
+    scaled[...] = kept.astype(bf16)
     squares[...] = square_sums(kept)
-    other_scaled = (other * column).astype(bf16)
+    other_scaled = other.astype(bf16)
     columns = weight.shape[1]
     for at in range(0, columns, 512):
         sent[:, at : at + 512] = dot(other_scaled, weight[:, at : at + 512], 0, 0).astype(bf16)
@@ -151,13 +148,16 @@
 
     at = np.arange(ROWS)
     place = (at % HALF) // 2 * 4 + at // HALF * 2 + at % 2
-    joint_weight = jnp.concatenate([gate_weight, up_weight], axis=1)
+    gain = norm_gain[:, None]
+    joint_weight = jnp.concatenate(
+        [(w.astype(f32) * gain).astype(bf16) for w in (gate_weight, up_weight)], axis=1
+    )
     payload = [((HALF, joint_weight.shape[1] + 128), bf16)]
     columns = residual_in.shape[1]
     sent, ordered, scaled, squares = local(
         project_other,
         payload + [((columns, ROWS), bf16), ((columns, HALF), bf16), ((HALF, 128), f32)],
-        [residual_in.T, norm_gain[None, :], joint_weight],
+        [residual_in.T, joint_weight],
         10**9,
     )
     (both,) = local(project_kept, payload, [scaled, squares, joint_weight, swap(sent)], 10**9)

time: 172 us -> 170 us (0.988)
  local copies, waits for them, and re-layouts: 5.92 us -> 1.91 us
  other arithmetic: 4.46 us -> 6.49 us
    unnamed x47 -> x44, local copies, waits for them, and re-layouts: 3.9 us -> 1.08 us
    convert_element_type x0 -> x1, other arithmetic: none -> 1.93 us  [shards(): (w.astype(f32) * gain).astype(bf16)]
where the time goes in v7:
time: 170 us; the launch traced here: 169 us
  blocking collectives  114 us (67%)
  waiting for transfers between devices  18.2 us (11%)
  matrix products  17.2 us (10%)
  other arithmetic  6.49 us (4%)
  starting transfers between devices  6.1 us (4%)
  Pallas kernels  4.52 us (3%)
  local copies, waits for them, and re-layouts  1.91 us (1%)
    all_to_all x6, blocking collectives, exchange(): return lax.all_to_all(v, axes, 0, 0, tiled=True)  114 us
    dot_general x12, matrix products, dot(): lax.dot_general(a, b, (((ca,), (cb,)), ((), ())), preferred_element_type=...  17.2 us
    ppermute x6, waiting for transfers between devices, swap(): return lax.ppermute(v, 'c', [(0, 1), (1, 0)])  9.3 us
    all_to_all x1, waiting for transfers between devices, exchange(): return lax.all_to_all(v, axes, 0, 0, tiled=True)  8.9 us
    all_to_all x1, starting transfers between devices, exchange(): return lax.all_to_all(v, axes, 0, 0, tiled=True)  5.48 us
    pallas_call x8, Pallas kernels, local(): pl.pallas_call(kernel, out_shape=[jax.ShapeDtypeStruct(shape, kind) for s...  4.52 us
  transfers between devices with their start and end apart: 7, of which 7 were waited for; matrix products, arithmetic and copies ran while one was open for 7% of the time, Pallas kernels for 1%

profile of v7, /device:TPU:0, one launch (start us, length us, event | category | flops | bytes accessed | tf_op | source)
XLA Modules:
  0.0 169.3 jit_solution(10784529817703656321)
XLA Ops:
  0.6 0.0 copy-start
  0.7 1.9 %multiply_convert_fusion.1 = (bf16[224,1792]{1,0:T(8,128)(2,1)S(1)}, bf16[224,1792]{1,0:T(8,128)(2,1)S(1)}) fusion(bf16[224,1792]{1,0:T(8,128)(2,1)} %param.12, f32[224]{0:T(256)} %param.11, bf16[224,1792]{1,0:T(8,128)(2,1)} %param.13), kind=kLoop, calls=%fused_computation.13 | loop fusion | flops 2408448 | bytes 3212160 | tf_op jit(solution)/shard_map/convert_element_type | solution.py:153
  2.6 0.1 pad_maximum_fusion.weight
  2.7 0.7 shard_map.137
  3.4 0.1 collective-permute-start
  3.5 2.5 %collective-permute-done.arrived = bf16[128,3712]{1,0:T(8,128)(2,1)S(1)} collective-permute-done((bf16[128,3712]{1,0:T(8,128)(2,1)S(1)}, bf16[128,3712]{1,0:T(8,128)(2,1)S(1)}, u32[]{:S(2)}, u32[]{:S(2)}) %collective-permute-start) | collective-permute-done | bytes 950304 | tf_op jit(solution)/shard_map/ppermute | solution.py:32
  6.0 0.4 shard_map.138
  6.5 23.9 %all_to_all.35 = bf16[8,16,3712]{2,1,0:T(8,128)(2,1)S(1)} all-to-all(bf16[8,16,3712]{2,1,0:T(8,128)(2,1)S(1)} %bitcast.31), channel_id=1, replica_groups=mesh['zl'=2,'x'=4,'y'=4,'zh'=2,'c'=2] {'y','zh'}, dimensions={0} | all-to-all | bytes 1900544 | tf_op jit(solution)/shard_map/all_to_all | solution.py:36
  30.4 0.1 convert_reduce_fusion
  30.5 0.1 slice_reduce_fusion
  30.6 0.1 slice_multiply_fusion
  30.8 12.6 %all_to_all.36 = bf16[8,16,1792]{2,1,0:T(8,128)(2,1)S(1)} all-to-all(bf16[8,16,1792]{2,1,0:T(8,128)(2,1)S(1)} %broadcast_in_dim.6), channel_id=1, replica_groups=mesh['zl'=2,'x'=4,'y'=4,'zh'=2,'c'=2] {'y','zh'}, dimensions={0} | all-to-all | bytes 917504 | tf_op jit(solution)/shard_map/all_to_all | solution.py:36
  43.4 0.0 collective-permute-start.1
  43.4 0.4 fusion.7
  43.8 1.4 collective-permute-done.1
  45.3 0.4 fusion.8
  45.7 11.1 %all_to_all.37 = bf16[8,28,256]{2,1,0:T(8,128)(2,1)S(1)} all-to-all(bf16[8,28,256]{2,1,0:T(8,128)(2,1)S(1)} %maximum_select_fusion.2), channel_id=1, replica_groups=mesh['zl'=2,'x'=4,'y'=4,'zh'=2,'c'=2] {'zl','x'}, dimensions={0} | all-to-all | bytes 229376 | tf_op jit(solution)/shard_map/all_to_all | solution.py:36
  56.9 0.1 broadcast_in_dim.7
  57.0 23.0 %all_to_all.38 = bf16[64,28,256]{2,1,0:T(8,128)(2,1)S(1)} all-to-all(bf16[64,28,256]{2,1,0:T(8,128)(2,1)S(1)} %broadcast_in_dim.7), channel_id=1, replica_groups=mesh['zl'=2,'x'=4,'y'=4,'zh'=2,'c'=2] {'y','zh','zl','x'}, dimensions={0} | all-to-all | bytes 1835008 | tf_op jit(solution)/shard_map/all_to_all | solution.py:36
  80.0 0.2 reshape.43.kept
  80.2 0.0 copy-start.9
  80.2 0.1 collective-permute-start.2
  80.3 2.5 %collective-permute-done.2.other = bf16[8,224,256]{2,1,0:T(8,128)(2,1)S(1)} collective-permute-done((bf16[8,224,256]{2,1,0:T(8,128)(2,1)S(1)}, bf16[8,224,256]{2,1,0:T(8,128)(2,1)S(1)}, u32[]{:S(2)}, u32[]{:S(2)}) %collective-permute-start.2) | collective-permute-done | bytes 917536 | tf_op jit(solution)/shard_map/ppermute | solution.py:32
  82.8 0.1 shard_map.139
  82.9 0.0 copy-start.8
  82.9 2.3 %add_divide_fusion = (f32[256,512]{1,0:T(8,128)S(1)}, bf16[256,512]{1,0:T(8,128)(2,1)S(1)}) fusion(f32[512]{0:T(512)} %param.16, bf16[3584,256]{1,0:T(8,128)(2,1)S(1)} %bitcast.28, bf16[3584,512]{1,0:T(8,128)(2,1)S(1)} %copy-done.9), kind=kOutput, calls=%fused_computation.27 | convolution fusion | flops 940965888 | bytes 6293504 | tf_op jit(solution)/shard_map/dot_general | solution.py:28
  85.2 0.0 copy-start.4
  85.2 0.0 copy-start.20
  85.3 0.7 convolution_convert_fusion.3
  85.9 0.2 collective-permute-start.3
  86.2 0.6 convolution_subtract_fusion
  86.7 0.0 copy-done.14
  86.8 0.6 fusion.25.kept
  87.4 1.1 collective-permute-done.3.arrived
  88.5 0.9 shard_map.140
  89.4 21.9 %all_to_all.39 = bf16[64,2,3584]{2,1,0:T(2,128)(2,1)S(1)} all-to-all(bf16[64,2,3584]{2,1,0:T(2,128)(2,1)S(1)} %shard_map.140), channel_id=1, replica_groups=mesh['zl'=2,'x'=4,'y'=4,'zh'=2,'c'=2] {'zl','x','y','zh'}, dimensions={0} | all-to-all | bytes 1835008 | tf_op jit(solution)/shard_map/all_to_all | solution.py:36
  111.3 0.7 convert_reduce_fusion.2
  112.0 0.5 broadcast_in_dim.8
  112.5 21.2 %all_to_all.40.v = bf16[64,2,3584]{2,1,0:T(2,128)(2,1)S(1)} all-to-all(bf16[64,2,3584]{2,1,0:T(2,128)(2,1)S(1)} %broadcast_in_dim.8), channel_id=1, replica_groups=mesh['zl'=2,'x'=4,'y'=4,'zh'=2,'c'=2] {'zl','x','y','zh'}, dimensions={0} | all-to-all | bytes 1835008 | tf_op jit(solution)/shard_map/all_to_all | solution.py:36
  133.7 0.3 shard_map.141
  134.0 1.3 fusion.5
  135.3 0.9 collective-permute-done.4.v
  136.2 0.3 shard_map.142
  136.5 0.0 copy-start.1
  136.5 1.3 fusion.6
  137.8 1.3 convolution_convert_fusion.2
  139.1 0.2 collective-permute-start.5
  139.4 1.3 fusion.26.kept
  140.7 1.0 collective-permute-done.5.arrived
  141.7 0.9 shard_map.143
  142.6 1.0 copy-done.3
  143.5 5.5 %all-to-all-start.6 = ((bf16[64,2,3584]{2,1,0:T(2,128)(2,1)}), bf16[64,2,3584]{2,1,0:T(2,128)(2,1)}, u32[]{:S(2)}, u32[]{:S(2)}) async-start(bf16[64,2,3584]{2,1,0:T(2,128)(2,1)} %copy-done.3), calls=%async_computation.6 | async-start | bytes 1835008 | tf_op jit(solution)/shard_map/all_to_all | solution.py:36
  149.0 0.0 copy-start.2
  149.0 4.2 %convolution_convert_fusion = bf16[3584,512]{1,0:T(8,128)(2,1)} fusion(bf16[3584,256]{1,0:T(8,128)(2,1)S(1)} %bitcast.30, bf16[128,512]{1,0:T(8,128)(2,1)} %copy-done.11, bf16[128,512]{1,0:T(8,128)(2,1)} %copy-done.10, pred[]{:T(512)S(6)} %eq.6), kind=kOutput, calls=%fused_computation | convolution fusion | flops 942538752 | bytes 5767169 | tf_op jit(solution)/shard_map/dot_general | solution.py:28
  153.2 0.0 copy-start.5
  153.2 0.0 copy-start.6
  153.3 0.0 copy-start.17
  153.3 0.0 copy-start.21
  153.3 3.0 %convolution_convert_fusion.1 = bf16[512,3584]{1,0:T(8,128)(2,1)} fusion(bf16[128,3584]{1,0:T(8,128)(2,1)S(1)} %copy-done.2, bf16[128,3584]{1,0:T(8,128)(2,1)S(1)} %shard_map.141, bf16[128,512]{1,0:T(8,128)(2,1)S(1)} %copy-done.13, bf16[128,512]{1,0:T(8,128)(2,1)S(1)} %copy-done.15), kind=kOutput, calls=%fused_computation.1 | convolution fusion | flops 945553408 | bytes 5767168 | tf_op jit(solution)/shard_map/dot_general | solution.py:28
  156.3 0.9 shard_map.144
  157.2 0.6 add_convert_fusion.1
  157.8 8.9 %all-to-all-done.6 = bf16[64,2,3584]{2,1,0:T(2,128)(2,1)} async-done(((bf16[64,2,3584]{2,1,0:T(2,128)(2,1)}), bf16[64,2,3584]{2,1,0:T(2,128)(2,1)}, u32[]{:S(2)}, u32[]{:S(2)}) %all-to-all-start.6) | async-done | bytes 917536 | tf_op jit(solution)/shard_map/all_to_all | solution.py:36
  166.7 1.9 %convert_reduce_fusion.1 = f32[2,3584]{1,0:T(2,128)S(1)} fusion(bf16[64,2,3584]{2,1,0:T(2,128)(2,1)} %all-to-all-done.6), kind=kLoop, calls=%fused_computation.9 | loop fusion | flops 910336 | bytes 946176 | tf_op jit(solution)/shard_map/reduce_sum | solution.py:242
  168.7 0.6 convert_subtract_fusion
  (43 shorter events, 0.3 us)
Async XLA Ops:
  0.6 42.8 %copy-start = (bf16[1792,224]{0,1:T(8,128)(2,1)S(1)}, bf16[1792,224]{0,1:T(8,128)(2,1)}, u32[]{:S(2)}) copy-start(bf16[1792,224]{0,1:T(8,128)(2,1)} %param.14) | copy-start | bytes 2408452
  0.7 2.1 %copy-start.7 = (bf16[256,224]{0,1:T(8,128)(2,1)S(1)}, bf16[256,224]{0,1:T(8,128)(2,1)}, u32[]{:S(2)}) copy-start(bf16[256,224]{0,1:T(8,128)(2,1)} %param.10) | copy-start | bytes 344068
  3.4 2.6 %collective-permute-start = (bf16[128,3712]{1,0:T(8,128)(2,1)S(1)}, bf16[128,3712]{1,0:T(8,128)(2,1)S(1)}, u32[]{:S(2)}, u32[]{:S(2)}) collective-permute-start(bf16[128,3712]{1,0:T(8,128)(2,1)S(1)} %get-tuple-element.37), channel_id=1, source_target_pairs={{0,1},{1,0},{2,3},{3,2},{4,5},{5,4},{6,7},{7,6},{8,9},{9,8},{10,11... | collective-permute-start | bytes 2850824 | tf_op jit(solution)/shard_map/ppermute | solution.py:32
  43.4 1.8 %collective-permute-start.1 = (bf16[128,1792]{1,0:T(8,128)(2,1)S(1)}, bf16[128,1792]{1,0:T(8,128)(2,1)S(1)}, u32[]{:S(2)}, u32[]{:S(2)}) collective-permute-start(bf16[128,1792]{1,0:T(8,128)(2,1)S(1)} %bitcast.33), channel_id=1, source_target_pairs={{0,1},{1,0},{2,3},{3,2},{4,5},{5,4},{6,7},{7,6},{8,9},{9,8},{10,11... | collective-permute-start | bytes 1376264 | tf_op jit(solution)/shard_map/ppermute | solution.py:32
  80.2 2.7 %copy-start.9 = (bf16[3584,512]{1,0:T(8,128)(2,1)S(1)}, bf16[3584,512]{1,0:T(8,128)(2,1)}, u32[]{:S(2)}) copy-start(bf16[3584,512]{1,0:T(8,128)(2,1)} %param.15) | copy-start | bytes 11010052
  80.2 2.6 %collective-permute-start.2 = (bf16[8,224,256]{2,1,0:T(8,128)(2,1)S(1)}, bf16[8,224,256]{2,1,0:T(8,128)(2,1)S(1)}, u32[]{:S(2)}, u32[]{:S(2)}) collective-permute-start(bf16[8,224,256]{2,1,0:T(8,128)(2,1)S(1)} %reshape.43.kept), channel_id=1, source_target_pairs={{0,1},{1,0},{2,3},{3,2},{4,5},{5,4},{6,7},{7,6},{8,9},{9,8},{10,11... | collective-permute-start | bytes 2752520 | tf_op jit(solution)/shard_map/ppermute | solution.py:32
  82.9 2.4 %copy-start.8 = (bf16[512,3584]{1,0:T(8,128)(2,1)S(1)}, bf16[512,3584]{1,0:T(8,128)(2,1)}, u32[]{:S(2)}) copy-start(bf16[512,3584]{1,0:T(8,128)(2,1)} %param.17) | copy-start | bytes 11010052
  85.2 1.5 copy-start.4
  85.2 1.0 copy-start.20
  85.2 1.5 copy-start.12
  85.3 1.5 copy-start.14
  85.9 2.6 %collective-permute-start.3 = (bf16[128,3584]{1,0:T(8,128)(2,1)S(1)}, bf16[128,3584]{1,0:T(8,128)(2,1)S(1)}, u32[]{:S(2)}, u32[]{:S(2)}) collective-permute-start(bf16[128,3584]{1,0:T(8,128)(2,1)S(1)} %convolution_convert_fusion.3), channel_id=1, source_target_pairs={{0,1},{1,0},{2,3},{3,2},{4,5},{5,4},{6,7},{7,6},{8,9},{9,8},{10,11... | collective-permute-start | bytes 2752520 | tf_op jit(solution)/shard_map/ppermute | solution.py:32
  112.0 22.0 %copy-start.16 = (f32[2,3584]{1,0:T(2,128)}, f32[2,3584]{1,0:T(2,128)S(1)}, u32[]{:S(2)}) copy-start(f32[2,3584]{1,0:T(2,128)S(1)} %convert_reduce_fusion.2) | copy-start | bytes 86020
  112.0 22.0 %copy-start.18 = (bf16[2,3584]{1,0:T(2,128)(2,1)}, bf16[2,3584]{1,0:T(2,128)(2,1)S(1)}, u32[]{:S(2)}) copy-start(bf16[2,3584]{1,0:T(2,128)(2,1)S(1)} %add_convert_fusion.2) | copy-start | bytes 43012
  133.7 2.5 %collective-permute-start.4 = (bf16[64,2,3584]{2,1,0:T(2,128)(2,1)S(1)}, bf16[64,2,3584]{2,1,0:T(2,128)(2,1)S(1)}, u32[]{:S(2)}, u32[]{:S(2)}) collective-permute-start(bf16[64,2,3584]{2,1,0:T(2,128)(2,1)S(1)} %all_to_all.40.v), channel_id=1, source_target_pairs={{0,1},{1,0},{2,3},{3,2},{4,5},{5,4},{6,7},{7,6},{8,9},{9,8},{10,11... | collective-permute-start | bytes 2752520 | tf_op jit(solution)/shard_map/ppermute | solution.py:32
  135.3 4.0 %copy-start.10 = (bf16[128,512]{1,0:T(8,128)(2,1)}, bf16[128,512]{1,0:T(8,128)(2,1)S(1)}, u32[]{:S(2)}) copy-start(bf16[128,512]{1,0:T(8,128)(2,1)S(1)} %fusion.5) | copy-start | bytes 393220
  136.5 2.6 %copy-start.1 = (bf16[128,3584]{1,0:T(8,128)(2,1)}, bf16[128,3584]{1,0:T(8,128)(2,1)S(1)}, u32[]{:S(2)}) copy-start(bf16[128,3584]{1,0:T(8,128)(2,1)S(1)} %shard_map.142) | copy-start | bytes 2752516
  137.8 2.9 %copy-start.11 = (bf16[128,512]{1,0:T(8,128)(2,1)}, bf16[128,512]{1,0:T(8,128)(2,1)S(1)}, u32[]{:S(2)}) copy-start(bf16[128,512]{1,0:T(8,128)(2,1)S(1)} %fusion.6) | copy-start | bytes 393220
  139.1 2.6 %collective-permute-start.5 = (bf16[128,3584]{1,0:T(8,128)(2,1)S(1)}, bf16[128,3584]{1,0:T(8,128)(2,1)S(1)}, u32[]{:S(2)}, u32[]{:S(2)}) collective-permute-start(bf16[128,3584]{1,0:T(8,128)(2,1)S(1)} %convolution_convert_fusion.2), channel_id=1, source_target_pairs={{0,1},{1,0},{2,3},{3,2},{4,5},{5,4},{6,7},{7,6},{8,9},{9,8},{10,11... | collective-permute-start | bytes 2752520 | tf_op jit(solution)/shard_map/ppermute | solution.py:32
  142.6 1.0 copy-start.3
  143.5 23.2 %all-to-all-start.6 = ((bf16[64,2,3584]{2,1,0:T(2,128)(2,1)}), bf16[64,2,3584]{2,1,0:T(2,128)(2,1)}, u32[]{:S(2)}, u32[]{:S(2)}) async-start(bf16[64,2,3584]{2,1,0:T(2,128)(2,1)} %copy-done.3), calls=%async_computation.6 | async-start | bytes 1835008 | tf_op jit(solution)/shard_map/all_to_all | solution.py:36
  149.0 4.2 %copy-start.2 = (bf16[128,3584]{1,0:T(8,128)(2,1)S(1)}, bf16[128,3584]{1,0:T(8,128)(2,1)}, u32[]{:S(2)}) copy-start(bf16[128,3584]{1,0:T(8,128)(2,1)} %copy-done.1) | copy-start | bytes 2752516
  149.0 4.2 %copy-start.13 = (bf16[128,512]{1,0:T(8,128)(2,1)S(1)}, bf16[128,512]{1,0:T(8,128)(2,1)}, u32[]{:S(2)}) copy-start(bf16[128,512]{1,0:T(8,128)(2,1)} %copy-done.12) | copy-start | bytes 393220
  149.0 4.2 %copy-start.15 = (bf16[128,512]{1,0:T(8,128)(2,1)S(1)}, bf16[128,512]{1,0:T(8,128)(2,1)}, u32[]{:S(2)}) copy-start(bf16[128,512]{1,0:T(8,128)(2,1)} %copy-done.14) | copy-start | bytes 393220
  153.2 3.0 %copy-start.5 = (bf16[256,512]{1,0:T(8,128)(2,1)S(1)}, bf16[256,512]{1,0:T(8,128)(2,1)}, u32[]{:S(2)}) copy-start(bf16[256,512]{1,0:T(8,128)(2,1)} %copy-done.4) | copy-start | bytes 786436
  153.2 3.0 %copy-start.6 = (bf16[256,256]{1,0:T(8,128)(2,1)S(1)}, bf16[256,256]{1,0:T(8,128)(2,1)}, u32[]{:S(2)}) copy-start(bf16[256,256]{1,0:T(8,128)(2,1)} %constant.52.clone.rows) | copy-start | bytes 393220
  153.3 4.0 %copy-start.17 = (f32[2,3584]{1,0:T(2,128)S(1)}, f32[2,3584]{1,0:T(2,128)}, u32[]{:S(2)}) copy-start(f32[2,3584]{1,0:T(2,128)} %copy-done.16) | copy-start | bytes 86020
  153.3 3.9 %copy-start.21 = (f32[3584]{0:T(1024)S(1)}, f32[3584]{0:T(1024)}, u32[]{:S(2)}) copy-start(f32[3584]{0:T(1024)} %param.18) | copy-start | bytes 43012
  153.3 15.4 %copy-start.19 = (bf16[2,3584]{1,0:T(2,128)(2,1)S(1)}, bf16[2,3584]{1,0:T(2,128)(2,1)}, u32[]{:S(2)}) copy-start(bf16[2,3584]{1,0:T(2,128)(2,1)} %copy-done.18) | copy-start | bytes 43012
